TPU v7x, 32 devices: a whole 2x2x4 slice. The times are simulated.
32 devices in a mesh: sample: 8 (over y, x, core), space: 4 (over z).
Axes of the slice: x: 2, y: 2, z: 4, core: 2. Of those that a mesh axis runs over, the one named last changes fastest.
Arguments:
- volumes: bfloat16 [32, 32, 2048], P('sample', None, 'space'), may hold values from -6 to 6
- grad_out: bfloat16 [32, 128, 256], P(('sample', 'space')), may hold values from -6 to 6
- kernel_first: bfloat16 [27, 64, 32], replicated, may hold values from -0.21875 to 0.21875
- bias_first: float32 [64], replicated, may hold values from -3 to 3
- kernel_second: bfloat16 [27, 128, 64], replicated, may hold values from -0.15625 to 0.15625
- bias_second: float32 [128], replicated, may hold values from -3 to 3
Outputs:
- features: bfloat16 [32, 128, 256], P(('sample', 'space'))
- kernel_grad_first: float32 [27, 64, 32], replicated
- bias_grad_first: float32 [64], replicated
- kernel_grad_second: float32 [27, 128, 64], replicated
- bias_grad_second: float32 [128], replicated
All inputs are finite; a program needn't handle non-finite values.
Results may differ from a plain program's by a relative error of at most 0.0085.
The roundings to bfloat16 on the way count: a program that leaves them out, or rounds other values in their place, can miss the bound.
Values may be sent and summed in bfloat16 or wider, within the bound.
No kernel may reach another device: no remote copies, remote signals or barrier semaphores. Data moves between devices by JAX's collectives and lax.ppermute only.
A program may use at most 192 MiB of HBM per device.

v0:
```python
import math

import jax
import jax.numpy as jnp
from jax import lax
from jax.sharding import PartitionSpec as P

SIDE = 8


LEAK_SLOPE = 0.3


def padded_2(shard, sides, width):
    for axis, dim in sides:
        size, length = (lax.axis_size(axis), shard.shape[dim])
        up = [(i, (i + 1) % size) for i in range(size - 1)]
        down = [(j, i) for i, j in up]
        last = lax.slice_in_dim(shard, length - width, length, axis=dim)
        first = lax.slice_in_dim(shard, 0, width, axis=dim)
        before = lax.ppermute(last, axis, up)
        after = lax.ppermute(first, axis, down)
        shard = jnp.concatenate([before, shard, after], axis=dim)
    return shard


def leaky_unit(values):
    return jnp.where(values > 0, values, LEAK_SLOPE * values)


def pad_cube(flat, depth_len, side_len):
    cube_view = flat.reshape(flat.shape[0], flat.shape[1], depth_len, side_len, side_len)
    return jnp.pad(cube_view, ((0, 0), (0, 0), (1, 1), (1, 1), (1, 1)))


def pad_sides(flat, depth_ext, side_len):
    cube_view = flat.reshape(flat.shape[0], flat.shape[1], depth_ext, side_len, side_len)
    return jnp.pad(cube_view, ((0, 0), (0, 0), (0, 0), (1, 1), (1, 1)))


def stack_windows(padded, depth_len, side_len, mirror):
    pieces = []
    for tap_index in range(27):
        deep_off = tap_index // 9
        high_off = tap_index // 3 % 3
        wide_off = tap_index % 3
        if mirror:
            deep_off, high_off, wide_off = (2 - deep_off, 2 - high_off, 2 - wide_off)
        window = padded[
            :,
            :,
            deep_off : deep_off + depth_len,
            high_off : high_off + side_len,
            wide_off : wide_off + side_len,
        ]
        pieces.append(
            window.reshape(padded.shape[0], padded.shape[1], depth_len * side_len * side_len)
        )
    return jnp.concatenate(pieces, axis=1)


def convolve(stacked, weight):
    flat_weight = jnp.transpose(weight, (1, 0, 2)).reshape(weight.shape[1], -1)
    return jnp.einsum("ok,vkn->von", flat_weight, stacked, preferred_element_type=jnp.float32)


def weight_grad(gradient, stacked, out_chan, in_chan):
    flat_grad = jnp.einsum("von,vkn->ok", gradient, stacked, preferred_element_type=jnp.float32)
    return jnp.transpose(flat_grad.reshape(out_chan, 27, in_chan), (1, 0, 2))


def spread_back(delta, weight, depth_len, side_len):
    padded = pad_cube(delta, depth_len, side_len)
    stacked = stack_windows(padded, depth_len, side_len, True)
    flat_weight = jnp.transpose(weight, (2, 0, 1)).reshape(weight.shape[2], -1)
    return jnp.einsum("ck,vkn->vcn", flat_weight, stacked, preferred_element_type=jnp.float32)


def pool_mean(values, depth_len, side_len):
    lead_dim, chan_dim = (values.shape[0], values.shape[1])
    cube_view = values.reshape(
        lead_dim, chan_dim, depth_len // 2, 2, side_len // 2, 2, side_len // 2, 2
    )
    return jnp.mean(cube_view, axis=(3, 5, 7)).reshape(lead_dim, chan_dim, -1)


def unpool_even(values, depth_len, side_len):
    lead_dim, chan_dim = (values.shape[0], values.shape[1])
    shape_small = (lead_dim, chan_dim, depth_len // 2, 1, side_len // 2, 1, side_len // 2, 1)
    shape_large = (lead_dim, chan_dim, depth_len // 2, 2, side_len // 2, 2, side_len // 2, 2)
    cube_view = jnp.broadcast_to(values.reshape(shape_small), shape_large)
    return cube_view.reshape(lead_dim, chan_dim, -1)


def on_device(volumes, grad_out, kernel_first, bias_first, kernel_second, bias_second):
    side_len = SIDE
    half_side = side_len // 2
    plane_cells = side_len * side_len
    volume_count = volumes.shape[0]
    slab_len = volumes.shape[2] // plane_cells
    in_chan = kernel_first.shape[2]
    mid_chan = kernel_first.shape[1]
    out_chan = kernel_second.shape[1]
    devices = lax.axis_size("sample") * lax.axis_size("space")
    extended = padded_2(volumes, (("space", 2),), plane_cells)
    padded_in = pad_sides(extended, slab_len + 2, side_len)
    stacked_in = stack_windows(padded_in, slab_len, side_len, False)
    first_pre = convolve(stacked_in, kernel_first) + bias_first[None, :, None]
    positive = first_pre > 0
    pooled = pool_mean(leaky_unit(first_pre), slab_len, side_len).astype(jnp.bfloat16)
    owned_cubes = lax.all_to_all(pooled, "space", split_axis=0, concat_axis=2, tiled=True)
    depth_half = owned_cubes.shape[2] // (half_side * half_side)
    padded_mid = pad_cube(owned_cubes, depth_half, half_side)
    stacked_mid = stack_windows(padded_mid, depth_half, half_side, False)
    second = convolve(stacked_mid, kernel_second) + bias_second[None, :, None]
    features = leaky_unit(second).astype(jnp.bfloat16)
    slope_two = jnp.where(second > 0, 1.0, LEAK_SLOPE)
    delta_two = (grad_out.astype(jnp.float32) * slope_two).astype(jnp.bfloat16)
    scale_two = 1.0 / math.sqrt(owned_cubes.shape[0] * owned_cubes.shape[2] * devices)
    kernel_two = weight_grad(delta_two, stacked_mid, out_chan, mid_chan) * scale_two
    bias_two = jnp.sum(delta_two.astype(jnp.float32), axis=(0, 2)) * scale_two
    spread = spread_back(delta_two, kernel_second, depth_half, half_side).astype(jnp.bfloat16)
    returned = lax.all_to_all(spread, "space", split_axis=2, concat_axis=0, tiled=True)
    slope_one = jnp.where(positive, 1.0, LEAK_SLOPE)
    delta_one = (
        unpool_even(returned.astype(jnp.float32), slab_len, side_len) * 0.125 * slope_one
    ).astype(jnp.bfloat16)
    scale_one = 1.0 / math.sqrt(volume_count * volumes.shape[2] * devices)
    kernel_one = weight_grad(delta_one, stacked_in, mid_chan, in_chan) * scale_one
    bias_one = jnp.sum(delta_one.astype(jnp.float32), axis=(0, 2)) * scale_one
    kernel_one, bias_one, kernel_two, bias_two = lax.psum(
        (kernel_one, bias_one, kernel_two, bias_two), ("sample", "space")
    )
    return (features, kernel_one, bias_one, kernel_two, bias_two)


def solution(mesh):
    in_specs = (P("sample", None, "space"), P(("sample", "space"), None, None), P(), P(), P(), P())
    out_specs = (P(("sample", "space"), None, None), P(), P(), P(), P())
    return jax.shard_map(
        on_device, mesh=mesh, in_specs=in_specs, out_specs=out_specs, check_vma=False
    )
```

profile of v0, /device:TPU:0, one launch (start us, length us, event | category | flops | bytes accessed | tf_op | source)
XLA Modules:
  0.0 255.0 jit_solution(13459455933505439467)
XLA Ops:
  7.2 0.9 fusion.24
  8.1 4.9 %collective-permute-start = (bf16[4,32,64]{2,1,0:T(8,128)(2,1)S(1)}, bf16[4,32,64]{2,1,0:T(8,128)(2,1)S(1)}, u32[]{:S(2)}, u32[]{:S(2)}) collective-permute-start(bf16[4,32,64]{2,1,0:T(8,128)(2,1)S(1)} %get-tuple-element.56), channel_id=1, source_target_pairs={{0,1},{1,2},{2,3},{4,5},{5,6},{6,7},{8,9},{9,10},{10,11},{12,13},{... | collective-permute-start | bytes 49160 | tf_op jit(solution)/shard_map/ppermute | solution.py:21
  13.0 1.3 collective-permute-start.1
  14.6 4.2 %collective-permute-done.1 = bf16[4,32,64]{2,1,0:T(8,128)(2,1)S(1)} collective-permute-done((bf16[4,32,64]{2,1,0:T(8,128)(2,1)S(1)}, bf16[4,32,64]{2,1,0:T(8,128)(2,1)S(1)}, u32[]{:S(2)}, u32[]{:S(2)}) %collective-permute-start.1) | collective-permute-done | bytes 16416 | tf_op jit(solution)/shard_map/ppermute | solution.py:22
  18.8 1.0 pad_maximum_fusion
  20.2 2.1 pad_slice_fusion.1
  22.2 4.6 %pad_slice_fusion = (bf16[4,32,8,8,8]{1,4,3,2,0:T(8,128)(2,1)}, bf16[4,32,8,8,8]{1,4,3,2,0:T(8,128)(2,1)}, bf16[4,32,8,8,8]{1,4,3,2,0:T(8,128)(2,1)}, bf16[4,32,...) fusion(bf16[4,32,10,8,8]{1,4,3,2,0:T(8,128)(2,1)S(1)} %bitcast.166), kind=kLoop, calls=%fused_computation | loop fusion | bytes 2654208 | tf_op jit(solution)/shard_map/slice | solution.py:49
  26.8 1.3 copy.83
  28.1 1.9 copy.79
  30.0 1.2 copy.81
  31.4 0.9 copy.80
  32.3 0.8 copy.71
  33.1 0.8 copy.62
  33.9 0.8 copy.58
  34.8 1.6 constant_dynamic-update-slice_fusion.26
  36.4 1.9 copy.84
  38.3 1.9 copy.59
  40.3 0.8 copy.60
  41.1 0.8 copy.61
  42.0 0.8 copy.63
  42.8 0.9 copy.64
  43.6 0.9 copy.65
  44.5 1.9 copy.66
  46.5 0.9 copy.67
  47.3 0.8 copy.68
  48.2 0.9 copy.69
  49.0 0.8 copy.70
  49.9 0.8 copy.72
  50.7 1.9 copy.73
  52.7 0.8 copy.74
  54.4 1.6 constant_dynamic-update-slice_fusion.25
  56.0 1.6 constant_dynamic-update-slice_fusion.24
  58.9 1.6 constant_dynamic-update-slice_fusion.21
  74.7 2.8 %multiply_select_fusion = (f32[4,64,512]{2,1,0:T(8,128)S(1)}, f32[4,64,512]{2,1,0:T(8,128)S(1)}) fusion(f32[64]{0:T(128)S(1)} %copy-done.36, bf16[4,864,512]{2,1,0:T(8,128)(2,1)} %constant_dynamic-update-slice_fusion, bf16[64,864,1]{0,1,2:T(8,128)(2,1)S(1)} %bitcast.258), kind=kOutput, calls=%fused_computation.90 | convolution fusion | flops 227016704 | bytes 4698368 | tf_op jit(solution)/shard_map/ok,vkn->von/dot_general | solution.py:64
  79.4 3.9 %all-to-all-start = ((bf16[4,2,2048]{2,1,0:T(2,128)(2,1)}), bf16[4,2,2048]{2,1,0:T(2,128)(2,1)S(1)}, u32[]{:S(2)}, u32[]{:S(2)}) async-start(bf16[4,2,2048]{2,1,0:T(2,128)(2,1)} %reshape.411), calls=%async_computation | async-start | bytes 65536 | tf_op jit(solution)/shard_map/all_to_all | solution.py:111
  84.0 4.9 %all-to-all-done = bf16[4,2,2048]{2,1,0:T(2,128)(2,1)S(1)} async-done(((bf16[4,2,2048]{2,1,0:T(2,128)(2,1)}), bf16[4,2,2048]{2,1,0:T(2,128)(2,1)S(1)}, u32[]{:S(2)}, u32[]{:S(2)}) %all-to-all-start) | async-done | bytes 32800 | tf_op jit(solution)/shard_map/all_to_all | solution.py:111
  89.1 0.8 pad_slice_fusion.51
  90.3 4.2 %concatenate.14 = bf16[1,1728,256]{1,2,0:T(8,128)(2,1)S(1)} concatenate(bf16[1,64,256]{1,2,0:T(8,128)(2,1)} %bitcast.257, bf16[1,64,256]{1,2,0:T(8,128)(2,1)S(1)} %bitcast.233, bf16[1,64,256]{1,2,0:T(8,128)(2,1)S(1)} %bitcast.234, bf16[1,64,256]{1,2,0:T(8,128)(2,1)S(1)} %bitcast.235, bf16[1,64,256]{1,2,0:T(8,128)(2,1)S(1)} %bitcast.236, bf16[1,64,256]{1,2,0:T(8,128)(2,1)S(1)} %bitcast.237, ...), dimensions={1} | concatenate | bytes 1769472 | tf_op jit(solution)/shard_map/concatenate | solution.py:59
  98.5 1.0 reduce
  100.2 3.3 %all-to-all-start.1 = ((bf16[4,2,2048]{2,1,0:T(2,128)(2,1)}), bf16[4,2,2048]{2,1,0:T(2,128)(2,1)S(1)}, u32[]{:S(2)}, u32[]{:S(2)}) async-start(bf16[4,2,2048]{2,1,0:T(2,128)(2,1)} %reshape.413), calls=%async_computation.1 | async-start | bytes 65536 | tf_op jit(solution)/shard_map/all_to_all | solution.py:123
  103.5 1.3 fusion.2
  104.9 4.3 %all-to-all-done.1 = bf16[4,2,2048]{2,1,0:T(2,128)(2,1)S(1)} async-done(((bf16[4,2,2048]{2,1,0:T(2,128)(2,1)}), bf16[4,2,2048]{2,1,0:T(2,128)(2,1)S(1)}, u32[]{:S(2)}, u32[]{:S(2)}) %all-to-all-start.1) | async-done | bytes 32800 | tf_op jit(solution)/shard_map/all_to_all | solution.py:123
  110.2 3.2 %fusion.4 = f32[64,864]{1,0:T(8,128)S(1)} fusion(bf16[4,64,512]{2,1,0:T(8,128)(2,1)S(1)} %get-tuple-element.27, bf16[4,864,512]{2,1,0:T(8,128)(2,1)} %constant_dynamic-update-slice_fusion), kind=kOutput, calls=%fused_computation.83 | convolution fusion | flops 226547712 | bytes 4022272 | tf_op jit(solution)/shard_map/von,vkn->ok/dot_general | solution.py:68
  113.4 1.0 copy.91
  115.2 39.5 %all-reduce.3 = (f32[64]{0:T(128)}, f32[128]{0:T(128)}) all-reduce(f32[64]{0:T(128)S(1)} %broadcast_multiply_fusion.1, f32[128]{0:T(128)S(1)} %broadcast_multiply_fusion), channel_id=1, replica_groups=mesh['sample'=8,'space'=4] {'sample','space'}, use_global_device_ids=true, to_apply=%region_3.4 | all-reduce | flops 192 | bytes 1536 | tf_op jit(solution)/shard_map/psum | solution.py:131
  154.7 89.5 %all-reduce.7.cloned.1.call-done = (f32[27,64,32]{1,2,0:T(8,128)}, f32[27,128,64]{1,2,0:T(8,128)}) async-done(((f32[27,64,32]{1,2,0:T(8,128)}, f32[27,128,64]{1,2,0:T(8,128)}), (f32[27,64,32]{1,2,0:T(8,128)}, f32[27,128,64]{1,2,0:T(8,128)})) %all-reduce.7.cloned.1.call-update) | async-done | bytes 1105936 | tf_op jit(solution)/shard_map/psum | solution.py:131
  244.2 1.8 copy.158
  246.0 2.2 copy.159
  (158 shorter events, 26.6 us)
Async XLA Ops:
  7.2 88.1 %copy-start = (bf16[27,128,64]{1,2,0:T(8,128)(2,1)S(1)}, bf16[27,128,64]{1,2,0:T(8,128)(2,1)}, u32[]{:S(2)}) copy-start(bf16[27,128,64]{1,2,0:T(8,128)(2,1)} %param.10) | copy-start | bytes 1327108
  8.1 6.5 %collective-permute-start = (bf16[4,32,64]{2,1,0:T(8,128)(2,1)S(1)}, bf16[4,32,64]{2,1,0:T(8,128)(2,1)S(1)}, u32[]{:S(2)}, u32[]{:S(2)}) collective-permute-start(bf16[4,32,64]{2,1,0:T(8,128)(2,1)S(1)} %get-tuple-element.56), channel_id=1, source_target_pairs={{0,1},{1,2},{2,3},{4,5},{5,6},{6,7},{8,9},{9,10},{10,11},{12,13},{... | collective-permute-start | bytes 49160 | tf_op jit(solution)/shard_map/ppermute | solution.py:21
  13.0 5.8 %collective-permute-start.1 = (bf16[4,32,64]{2,1,0:T(8,128)(2,1)S(1)}, bf16[4,32,64]{2,1,0:T(8,128)(2,1)S(1)}, u32[]{:S(2)}, u32[]{:S(2)}) collective-permute-start(bf16[4,32,64]{2,1,0:T(8,128)(2,1)S(1)} %get-tuple-element.57), channel_id=1, source_target_pairs={{1,0},{2,1},{3,2},{5,4},{6,5},{7,6},{9,8},{10,9},{11,10},{13,12},{... | collective-permute-start | bytes 49160 | tf_op jit(solution)/shard_map/ppermute | solution.py:22
  26.8 4.4 %copy-start.1 = (bf16[4,32,8,8,8]{1,4,3,2,0:T(8,128)(2,1)S(1)}, bf16[4,32,8,8,8]{1,4,3,2,0:T(8,128)(2,1)}, u32[]{:S(2)}) copy-start(bf16[4,32,8,8,8]{1,4,3,2,0:T(8,128)(2,1)} %get-tuple-element.50) | copy-start | bytes 393220
  32.3 8.0 %copy-start.16 = (bf16[4,32,8,8,8]{1,4,3,2,0:T(8,128)(2,1)S(1)}, bf16[4,32,8,8,8]{1,4,3,2,0:T(8,128)(2,1)}, u32[]{:S(2)}) copy-start(bf16[4,32,8,8,8]{1,4,3,2,0:T(8,128)(2,1)} %get-tuple-element.30) | copy-start | bytes 393220
  33.1 8.0 %copy-start.15 = (bf16[4,32,8,8,8]{1,4,3,2,0:T(8,128)(2,1)S(1)}, bf16[4,32,8,8,8]{1,4,3,2,0:T(8,128)(2,1)}, u32[]{:S(2)}) copy-start(bf16[4,32,8,8,8]{1,4,3,2,0:T(8,128)(2,1)} %get-tuple-element.31) | copy-start | bytes 393220
  33.9 8.0 %copy-start.14 = (bf16[4,32,8,8,8]{1,4,3,2,0:T(8,128)(2,1)S(1)}, bf16[4,32,8,8,8]{1,4,3,2,0:T(8,128)(2,1)}, u32[]{:S(2)}) copy-start(bf16[4,32,8,8,8]{1,4,3,2,0:T(8,128)(2,1)} %get-tuple-element.32) | copy-start | bytes 393220
  34.8 8.0 %copy-start.13 = (bf16[4,32,8,8,8]{1,4,3,2,0:T(8,128)(2,1)S(1)}, bf16[4,32,8,8,8]{1,4,3,2,0:T(8,128)(2,1)}, u32[]{:S(2)}) copy-start(bf16[4,32,8,8,8]{1,4,3,2,0:T(8,128)(2,1)} %get-tuple-element.33) | copy-start | bytes 393220
  38.3 5.3 %copy-start.12 = (bf16[4,32,8,8,8]{1,4,3,2,0:T(8,128)(2,1)S(1)}, bf16[4,32,8,8,8]{1,4,3,2,0:T(8,128)(2,1)}, u32[]{:S(2)}) copy-start(bf16[4,32,8,8,8]{1,4,3,2,0:T(8,128)(2,1)} %get-tuple-element.34) | copy-start | bytes 393220
  41.1 5.4 %copy-start.11 = (bf16[4,32,8,8,8]{1,4,3,2,0:T(8,128)(2,1)S(1)}, bf16[4,32,8,8,8]{1,4,3,2,0:T(8,128)(2,1)}, u32[]{:S(2)}) copy-start(bf16[4,32,8,8,8]{1,4,3,2,0:T(8,128)(2,1)} %get-tuple-element.36) | copy-start | bytes 393220
  41.9 5.4 %copy-start.10 = (bf16[4,32,8,8,8]{1,4,3,2,0:T(8,128)(2,1)S(1)}, bf16[4,32,8,8,8]{1,4,3,2,0:T(8,128)(2,1)}, u32[]{:S(2)}) copy-start(bf16[4,32,8,8,8]{1,4,3,2,0:T(8,128)(2,1)} %get-tuple-element.37) | copy-start | bytes 393220
  42.8 5.4 %copy-start.9 = (bf16[4,32,8,8,8]{1,4,3,2,0:T(8,128)(2,1)S(1)}, bf16[4,32,8,8,8]{1,4,3,2,0:T(8,128)(2,1)}, u32[]{:S(2)}) copy-start(bf16[4,32,8,8,8]{1,4,3,2,0:T(8,128)(2,1)} %get-tuple-element.38) | copy-start | bytes 393220
  43.6 5.4 %copy-start.8 = (bf16[4,32,8,8,8]{1,4,3,2,0:T(8,128)(2,1)S(1)}, bf16[4,32,8,8,8]{1,4,3,2,0:T(8,128)(2,1)}, u32[]{:S(2)}) copy-start(bf16[4,32,8,8,8]{1,4,3,2,0:T(8,128)(2,1)} %get-tuple-element.39) | copy-start | bytes 393220
  44.5 5.4 %copy-start.7 = (bf16[4,32,8,8,8]{1,4,3,2,0:T(8,128)(2,1)S(1)}, bf16[4,32,8,8,8]{1,4,3,2,0:T(8,128)(2,1)}, u32[]{:S(2)}) copy-start(bf16[4,32,8,8,8]{1,4,3,2,0:T(8,128)(2,1)} %get-tuple-element.40) | copy-start | bytes 393220
  47.3 5.3 %copy-start.6 = (bf16[4,32,8,8,8]{1,4,3,2,0:T(8,128)(2,1)S(1)}, bf16[4,32,8,8,8]{1,4,3,2,0:T(8,128)(2,1)}, u32[]{:S(2)}) copy-start(bf16[4,32,8,8,8]{1,4,3,2,0:T(8,128)(2,1)} %get-tuple-element.42) | copy-start | bytes 393220
  48.2 5.4 %copy-start.5 = (bf16[4,32,8,8,8]{1,4,3,2,0:T(8,128)(2,1)S(1)}, bf16[4,32,8,8,8]{1,4,3,2,0:T(8,128)(2,1)}, u32[]{:S(2)}) copy-start(bf16[4,32,8,8,8]{1,4,3,2,0:T(8,128)(2,1)} %get-tuple-element.43) | copy-start | bytes 393220
  49.0 4.7 %copy-start.4 = (bf16[4,32,8,8,8]{1,4,3,2,0:T(8,128)(2,1)S(1)}, bf16[4,32,8,8,8]{1,4,3,2,0:T(8,128)(2,1)}, u32[]{:S(2)}) copy-start(bf16[4,32,8,8,8]{1,4,3,2,0:T(8,128)(2,1)} %get-tuple-element.44) | copy-start | bytes 393220
  49.9 4.1 %copy-start.3 = (bf16[4,32,8,8,8]{1,4,3,2,0:T(8,128)(2,1)S(1)}, bf16[4,32,8,8,8]{1,4,3,2,0:T(8,128)(2,1)}, u32[]{:S(2)}) copy-start(bf16[4,32,8,8,8]{1,4,3,2,0:T(8,128)(2,1)} %get-tuple-element.45) | copy-start | bytes 393220
  50.7 3.4 %copy-start.2 = (bf16[4,32,8,8,8]{1,4,3,2,0:T(8,128)(2,1)S(1)}, bf16[4,32,8,8,8]{1,4,3,2,0:T(8,128)(2,1)}, u32[]{:S(2)}) copy-start(bf16[4,32,8,8,8]{1,4,3,2,0:T(8,128)(2,1)} %get-tuple-element.46) | copy-start | bytes 393220
  53.5 4.8 %copy-start.22 = (bf16[4,32,512]{2,1,0:T(8,128)(2,1)S(1)}, bf16[4,32,512]{2,1,0:T(8,128)(2,1)}, u32[]{:S(2)}) copy-start(bf16[4,32,512]{2,1,0:T(8,128)(2,1)} %copy.62) | copy-start | bytes 393220
  53.7 6.8 %copy-start.31 = (bf16[4,32,512]{2,1,0:T(8,128)(2,1)S(1)}, bf16[4,32,512]{2,1,0:T(8,128)(2,1)}, u32[]{:S(2)}) copy-start(bf16[4,32,512]{2,1,0:T(8,128)(2,1)} %copy.64) | copy-start | bytes 393220
  53.7 7.5 %copy-start.30 = (bf16[4,32,512]{2,1,0:T(8,128)(2,1)S(1)}, bf16[4,32,512]{2,1,0:T(8,128)(2,1)}, u32[]{:S(2)}) copy-start(bf16[4,32,512]{2,1,0:T(8,128)(2,1)} %copy.65) | copy-start | bytes 393220
  53.7 8.1 %copy-start.29 = (bf16[4,32,512]{2,1,0:T(8,128)(2,1)S(1)}, bf16[4,32,512]{2,1,0:T(8,128)(2,1)}, u32[]{:S(2)}) copy-start(bf16[4,32,512]{2,1,0:T(8,128)(2,1)} %copy.66) | copy-start | bytes 393220
  53.9 3.7 %copy-start.32 = (bf16[4,32,512]{2,1,0:T(8,128)(2,1)S(1)}, bf16[4,32,512]{2,1,0:T(8,128)(2,1)}, u32[]{:S(2)}) copy-start(bf16[4,32,512]{2,1,0:T(8,128)(2,1)} %copy.61) | copy-start | bytes 393220
  53.9 8.6 %copy-start.28 = (bf16[4,32,512]{2,1,0:T(8,128)(2,1)S(1)}, bf16[4,32,512]{2,1,0:T(8,128)(2,1)}, u32[]{:S(2)}) copy-start(bf16[4,32,512]{2,1,0:T(8,128)(2,1)} %copy.67) | copy-start | bytes 393220
  54.0 9.3 %copy-start.27 = (bf16[4,32,512]{2,1,0:T(8,128)(2,1)S(1)}, bf16[4,32,512]{2,1,0:T(8,128)(2,1)}, u32[]{:S(2)}) copy-start(bf16[4,32,512]{2,1,0:T(8,128)(2,1)} %copy.68) | copy-start | bytes 393220
  54.1 9.7 %copy-start.26 = (bf16[4,32,512]{2,1,0:T(8,128)(2,1)S(1)}, bf16[4,32,512]{2,1,0:T(8,128)(2,1)}, u32[]{:S(2)}) copy-start(bf16[4,32,512]{2,1,0:T(8,128)(2,1)} %copy.69) | copy-start | bytes 393220
  54.2 10.4 %copy-start.25 = (bf16[4,32,512]{2,1,0:T(8,128)(2,1)S(1)}, bf16[4,32,512]{2,1,0:T(8,128)(2,1)}, u32[]{:S(2)}) copy-start(bf16[4,32,512]{2,1,0:T(8,128)(2,1)} %copy.70) | copy-start | bytes 393220
  54.2 11.1 %copy-start.20 = (bf16[4,32,512]{2,1,0:T(8,128)(2,1)S(1)}, bf16[4,32,512]{2,1,0:T(8,128)(2,1)}, u32[]{:S(2)}) copy-start(bf16[4,32,512]{2,1,0:T(8,128)(2,1)} %copy.71) | copy-start | bytes 393220
  54.4 11.5 %copy-start.24 = (bf16[4,32,512]{2,1,0:T(8,128)(2,1)S(1)}, bf16[4,32,512]{2,1,0:T(8,128)(2,1)}, u32[]{:S(2)}) copy-start(bf16[4,32,512]{2,1,0:T(8,128)(2,1)} %copy.72) | copy-start | bytes 393220
  56.0 10.6 %copy-start.23 = (bf16[4,32,512]{2,1,0:T(8,128)(2,1)S(1)}, bf16[4,32,512]{2,1,0:T(8,128)(2,1)}, u32[]{:S(2)}) copy-start(bf16[4,32,512]{2,1,0:T(8,128)(2,1)} %copy.73) | copy-start | bytes 393220
  57.6 9.7 %copy-start.21 = (bf16[4,32,512]{2,1,0:T(8,128)(2,1)S(1)}, bf16[4,32,512]{2,1,0:T(8,128)(2,1)}, u32[]{:S(2)}) copy-start(bf16[4,32,512]{2,1,0:T(8,128)(2,1)} %copy.74) | copy-start | bytes 393220
  61.9 8.8 %copy-start.17 = (bf16[4,32,512]{2,1,0:T(8,128)(2,1)S(1)}, bf16[4,32,512]{2,1,0:T(8,128)(2,1)}, u32[]{:S(2)}) copy-start(bf16[4,32,512]{2,1,0:T(8,128)(2,1)} %copy.79) | copy-start | bytes 393220
  62.5 8.8 %copy-start.19 = (bf16[4,32,512]{2,1,0:T(8,128)(2,1)S(1)}, bf16[4,32,512]{2,1,0:T(8,128)(2,1)}, u32[]{:S(2)}) copy-start(bf16[4,32,512]{2,1,0:T(8,128)(2,1)} %copy.80) | copy-start | bytes 393220
  65.2 8.8 %copy-start.18 = (bf16[4,32,512]{2,1,0:T(8,128)(2,1)S(1)}, bf16[4,32,512]{2,1,0:T(8,128)(2,1)}, u32[]{:S(2)}) copy-start(bf16[4,32,512]{2,1,0:T(8,128)(2,1)} %copy.84) | copy-start | bytes 393220
  65.9 8.7 %copy-start.33 = (bf16[27,64,32]{1,2,0:T(8,128)(2,1)S(1)}, bf16[27,64,32]{1,2,0:T(8,128)(2,1)}, u32[]{:S(2)}) copy-start(bf16[27,64,32]{1,2,0:T(8,128)(2,1)} %param.8) | copy-start | bytes 331780
  65.9 8.7 %copy-start.36 = (f32[64]{0:T(128)S(1)}, f32[64]{0:T(128)}, u32[]{:S(2)}) copy-start(f32[64]{0:T(128)} %param.9) | copy-start | bytes 772
  77.5 5.8 %copy-start.34 = (bf16[1,128,256]{2,1,0:T(8,128)(2,1)S(1)}, bf16[1,128,256]{2,1,0:T(8,128)(2,1)}, u32[]{:S(2)}) copy-start(bf16[1,128,256]{2,1,0:T(8,128)(2,1)} %param.7) | copy-start | bytes 196612
  79.4 9.5 %all-to-all-start = ((bf16[4,2,2048]{2,1,0:T(2,128)(2,1)}), bf16[4,2,2048]{2,1,0:T(2,128)(2,1)S(1)}, u32[]{:S(2)}, u32[]{:S(2)}) async-start(bf16[4,2,2048]{2,1,0:T(2,128)(2,1)} %reshape.411), calls=%async_computation | async-start | bytes 65536 | tf_op jit(solution)/shard_map/all_to_all | solution.py:111
  94.6 0.8 copy-start.35
  94.6 0.8 copy-start.37
  100.2 8.9 %all-to-all-start.1 = ((bf16[4,2,2048]{2,1,0:T(2,128)(2,1)}), bf16[4,2,2048]{2,1,0:T(2,128)(2,1)S(1)}, u32[]{:S(2)}, u32[]{:S(2)}) async-start(bf16[4,2,2048]{2,1,0:T(2,128)(2,1)} %reshape.413), calls=%async_computation.1 | async-start | bytes 65536 | tf_op jit(solution)/shard_map/all_to_all | solution.py:123
  103.5 140.7 %all-reduce.7.cloned.1.call-start = ((), (), s32[]{:S(2)}) async-start(), calls=%async_computation.2 | async-start | bytes 2654208 | tf_op jit(solution)/shard_map/psum | solution.py:131
Sparse Core Ops, SparseCore 0:
  114.5 129.5 all-reduce.6
where the time goes:
time: 256 us; the launch traced here: 255 us
  waiting for transfers between devices  103 us (40%)
  local copies, waits for them, and re-layouts  72.7 us (28%)
  blocking collectives  39.5 us (15%)
  between operations  14.6 us (6%)
  starting transfers between devices  13.4 us (5%)
  matrix products  8.4 us (3%)
  other arithmetic  3.21 us (1%)
    psum x1, waiting for transfers between devices, on_device(): lax.psum((kernel_one, bias_one, kernel_two, bias_two), ('sample', 'space'))  89.5 us
    psum x1, blocking collectives, on_device(): lax.psum((kernel_one, bias_one, kernel_two, bias_two), ('sample', 'space'))  39.5 us
    unnamed x137, local copies, waits for them, and re-layouts  29.7 us
    reshape x27, local copies, waits for them, and re-layouts, stack_windows(): window.reshape(padded.shape[0], padded.shape[1], depth_len * side_len * s...  25.7 us
    slice x6, local copies, waits for them, and re-layouts, stack_windows(): padded[:, :, deep_off:deep_off + depth_len, high_off:high_off + side_len,...  8.49 us
    concatenate x4, local copies, waits for them, and re-layouts, stack_windows(): return jnp.concatenate(pieces, axis=1)  5.53 us
  transfers between devices with their start and end apart: 5, of which 5 were waited for; matrix products, arithmetic and copies ran while one was open for 1% of the time, Pallas kernels for 0%

commit v1 on v0

v1 whole, which is shorter than its diff:
```python
import functools
import math

import jax
import jax.numpy as jnp
from jax import lax
from jax.experimental import pallas as pl
from jax.experimental.pallas import tpu as pltpu
from jax.sharding import PartitionSpec as P

SIDE = 8
LEAK_SLOPE = 0.3
LANES = 128
ROWS = 16
BF16 = jnp.bfloat16
F32 = jnp.float32


def vmem():
    return pl.BlockSpec(memory_space=pltpu.VMEM)


def lane_iota(rows):
    return lax.broadcasted_iota(jnp.int32, (rows, LANES), 1)


def turn(block, shift):
    return pltpu.roll(block, (-shift) % LANES, 1) if shift % LANES else block


def dot(left, right):
    return jnp.dot(left, right, preferred_element_type=F32)


def dot_lanes(left, right):
    return lax.dot_general(left, right, (((1,), (1,)), ((), ())), preferred_element_type=F32)


def in_plane(side, tap):
    high, wide = tap // 3 - 1, tap % 3 - 1
    lane = lane_iota(1)
    row, col = lane // side % side + high, lane % side + wide
    valid = (row >= 0) & (row < side) & (col >= 0) & (col < side)
    return valid, high * side + wide


def weights_kernel(first_ref, second_ref, bias_one_ref, bias_two_ref, conv_one_ref, conv_two_ref, back_ref, col_one_ref, col_two_ref):
    mid, out = first_ref.shape[2], second_ref.shape[2]
    inner, deep = first_ref.shape[1], second_ref.shape[1]

    def eye(size):
        row = lax.broadcasted_iota(jnp.int32, (size, size), 0)
        return row == lax.broadcasted_iota(jnp.int32, (size, size), 1)

    for a in range(3):
        taps = first_ref[9 * a : 9 * a + 9].reshape(9 * inner, mid)
        conv_one_ref[a * mid : (a + 1) * mid, :] = dot_lanes(eye(mid).astype(BF16), taps).astype(BF16)
        taps = second_ref[9 * a : 9 * a + 9].reshape(9 * deep, out)
        conv_two_ref[a * out : (a + 1) * out, :] = dot_lanes(eye(out).astype(BF16), taps).astype(BF16)
        for t in range(9):
            back_ref[a * deep : (a + 1) * deep, t * out : (t + 1) * out] = second_ref[9 * a + t]
    for row_ref, col_ref, size in ((bias_one_ref, col_one_ref, mid), (bias_two_ref, col_two_ref, out)):
        col = jnp.sum(jnp.where(eye(size), row_ref[...], 0.0), axis=1, keepdims=True)
        col_ref[...] = jnp.broadcast_to(col, (size, LANES))


def prepare_weights(kernel_first, bias_first, kernel_second, bias_second):
    first, second = jnp.swapaxes(kernel_first, 1, 2), jnp.swapaxes(kernel_second, 1, 2)
    inner, mid, out = first.shape[1], first.shape[2], second.shape[2]
    shapes = (
        ((3 * mid, 9 * inner), BF16),
        ((3 * out, 9 * mid), BF16),
        ((3 * mid, 9 * out), BF16),
        ((mid, LANES), F32),
        ((out, LANES), F32),
    )
    return pl.pallas_call(
        weights_kernel,
        out_shape=[jax.ShapeDtypeStruct(s, d) for s, d in shapes],
        in_specs=[vmem()] * 4,
        out_specs=[vmem()] * 5,
        name="weights",
    )(first, second, bias_first.reshape(1, -1), bias_second.reshape(1, -1))


def main_kernel(plan, *refs):
    parts, grad_ref, conv_one_ref, conv_two_ref, back_ref, col_one_ref, col_two_ref = (
        refs[: plan.space],
        *refs[plan.space : plan.space + 6],
    )
    feat_ref, keep_ref, send_ref = refs[plan.space + 6 : plan.space + 9]
    x_ref, s_one, t_one, slope_ref, lk_ref, d_one, s_two, t_two, d_two, sd_two, u_two, pay_ref = refs[plan.space + 9 :]
    inner, mid, out = plan.inner, plan.mid, plan.out
    blocks, halves = plan.blocks, plan.halves
    place, core = lax.axis_index("space"), lax.axis_index("sample") % plan.cores
    side, small = SIDE, SIDE // 2
    plane = side * side
    low = small * small
    lane = lane_iota(1)

    s_one[9 * inner :, :] = jnp.ones((ROWS, blocks * LANES), BF16)
    s_two[9 * mid :, :] = jnp.ones((ROWS, halves * LANES), BF16)
    cell = lax.broadcasted_iota(jnp.int32, (LANES, LANES), 0)
    lanes = lax.broadcasted_iota(jnp.int32, (LANES, LANES), 1)
    parent = (cell % plane // side // 2) * small + cell % side // 2
    pool = jnp.where(parent == lanes % low, 0.125, 0.0).astype(BF16)
    pool = jnp.concatenate([pool, pool], axis=0)
    parent = (lanes % plane // side // 2) * small + lanes % side // 2

    for volume in range(plan.owned):
        for k, part in enumerate(parts):
            start = (place ^ k) * plan.part_blocks
            for j in range(plan.part_blocks):
                x_ref[start + j] = part[volume, :, j * LANES : (j + 1) * LANES]

        for tap in range(9):
            valid, shift = in_plane(side, tap)
            for j in range(blocks):
                block = x_ref[j]
                if shift:
                    block = jnp.where(valid, turn(block, shift), jnp.zeros_like(block))
                s_one[tap * inner : (tap + 1) * inner, j * LANES : (j + 1) * LANES] = block

        t_one[...] = dot(conv_one_ref[...], s_one[: 9 * inner, :])

        upper = lane >= plane
        for j in range(blocks):
            here = slice(j * LANES, (j + 1) * LANES)
            before, after = slice(here.start - LANES, here.start), slice(here.stop, here.stop + LANES)
            zero = jnp.zeros((mid, LANES), F32)
            up = jnp.where(upper, t_one[:mid, before] if j else zero, t_one[:mid, here])
            down = jnp.where(upper, t_one[2 * mid :, here], t_one[2 * mid :, after] if j < blocks - 1 else zero)
            pre = t_one[mid : 2 * mid, here] + turn(up + down, plane) + col_one_ref[...]
            slope = jnp.where(pre > 0, 1.0, LEAK_SLOPE)
            slope_ref[:, here] = slope * 0.125
            value = slope * pre
            high = value.astype(BF16)
            lk_ref[j * mid : (j + 1) * mid, :LANES] = high
            lk_ref[j * mid : (j + 1) * mid, LANES:] = (value - high.astype(F32)).astype(BF16)

        means = dot(lk_ref[...], pool)
        for h in range(halves):
            here = slice(h * LANES, (h + 1) * LANES)
            pooled = jnp.zeros((mid, LANES), F32)
            for j in range(LANES // low):
                row = (h * (LANES // low) + j) * mid
                pooled = jnp.where(lane // low == j, means[row : row + mid], pooled)
            for tap in range(9):
                valid, shift = in_plane(small, tap)
                block = jnp.where(valid, turn(pooled, shift), 0.0) if shift else pooled
                s_two[tap * mid : (tap + 1) * mid, here] = block.astype(BF16)

        t_two[...] = dot(conv_two_ref[...], s_two[: 9 * mid, :])
        deltas = []
        for h in range(halves):
            here = slice(h * LANES, (h + 1) * LANES)
            before, after = slice(here.start - LANES, here.start), slice(here.stop, here.stop + LANES)
            zero = jnp.zeros((out, LANES), F32)
            up = jnp.where(lane >= LANES - low, t_two[:out, before] if h else zero, t_two[:out, here])
            down = jnp.where(lane < low, t_two[2 * out :, after] if h < halves - 1 else zero, t_two[2 * out :, here])
            pre = t_two[out : 2 * out, here] + turn(up, -low) + turn(down, low) + col_two_ref[...]
            slope = jnp.where(pre > 0, 1.0, LEAK_SLOPE)
            feat_ref[volume, :, here] = (slope * pre).astype(BF16)
            delta = (grad_ref[volume, :, here].astype(F32) * slope).astype(BF16).astype(F32)
            deltas.append(delta)
            for tap in range(9):
                valid, shift = in_plane(small, 8 - tap)
                block = jnp.where(valid, turn(delta, shift), 0.0) if shift else delta
                sd_two[tap * out : (tap + 1) * out, here] = block.astype(BF16)

        for h in range(halves):
            here = slice(h * LANES, (h + 1) * LANES)
            zero = jnp.zeros((out, LANES), F32)
            after = deltas[h + 1] if h < halves - 1 else zero
            before = deltas[h - 1] if h else zero
            d_two[:out, here] = turn(jnp.where(lane < low, after, deltas[h]), low).astype(BF16)
            d_two[out : 2 * out, here] = deltas[h].astype(BF16)
            d_two[2 * out :, here] = turn(jnp.where(lane >= LANES - low, before, deltas[h]), -low).astype(BF16)

        u_two[...] = dot(back_ref[...], sd_two[...])
        spreads = []
        for h in range(halves):
            here = slice(h * LANES, (h + 1) * LANES)
            before, after = slice(here.start - LANES, here.start), slice(here.stop, here.stop + LANES)
            zero = jnp.zeros((mid, LANES), F32)
            down = jnp.where(lane < low, u_two[:mid, after] if h < halves - 1 else zero, u_two[:mid, here])
            up = jnp.where(lane >= LANES - low, u_two[2 * mid :, before] if h else zero, u_two[2 * mid :, here])
            spreads.append((u_two[mid : 2 * mid, here] + turn(down, low) + turn(up, -low)).astype(BF16))
        spread = jnp.concatenate(spreads, axis=0)

        deltas = []
        for j in range(LANES // low):
            unpool = jnp.where(parent + j * low == cell, 1.0, 0.0).astype(BF16)
            deltas.append(dot(spread, unpool))
        wide = []
        for j in range(blocks):
            here = slice(j * LANES, (j + 1) * LANES)
            h, i = j // (LANES // low), j % (LANES // low)
            wide.append(deltas[i][h * mid : (h + 1) * mid] * slope_ref[:, here])
        for j in range(blocks):
            here = slice(j * LANES, (j + 1) * LANES)
            zero = jnp.zeros((mid, LANES), F32)
            after = wide[j + 1] if j < blocks - 1 else zero
            before = wide[j - 1] if j else zero
            d_one[:mid, here] = turn(jnp.where(upper, wide[j], after), plane).astype(BF16)
            d_one[mid : 2 * mid, here] = wide[j].astype(BF16)
            d_one[2 * mid :, here] = turn(jnp.where(upper, before, wide[j]), plane).astype(BF16)

        two = dot_lanes(s_two[...], d_two[...]) * plan.scale_two
        one = dot_lanes(s_one[...], d_one[...]) * plan.scale_one
        first = 9 * inner
        total = 27 * mid
        half = first // 2
        pieces = [(a * 9 * mid, two[: 9 * mid, a * out : (a + 1) * out]) for a in range(3)]
        pieces.append((total, one[:first, : 2 * mid]))
        pieces.append((total + first, jnp.concatenate([one[:half, 2 * mid :], one[half:first, 2 * mid :]], axis=1)))
        row = lax.broadcasted_iota(jnp.int32, (ROWS // 2, LANES), 0)
        own = one[first : first + ROWS // 2, : 2 * mid]
        own = jnp.where(lane_iota(1) < mid, turn(own, mid), 0.0)
        tail = jnp.where(row == 0, two[9 * mid : 9 * mid + ROWS // 2, out : 2 * out], jnp.where(row == 1, own, 0.0))
        if volume:
            tail = tail + pay_ref[plan.total - ROWS : plan.total - ROWS // 2] + pay_ref[plan.total - ROWS // 2 :]
        for start, piece in pieces:
            span = slice(start, start + piece.shape[0])
            pay_ref[span, :] = piece + pay_ref[span, :] if volume else piece
        used = total + first + half
        if not volume and used < plan.total - ROWS:
            pay_ref[used : plan.total - ROWS, :] = jnp.zeros((plan.total - ROWS - used, LANES), F32)
        high = tail.astype(BF16).astype(F32)
        pay_ref[plan.total - ROWS :, :] = jnp.concatenate([high, tail - high], axis=0)

    share = plan.total // plan.cores
    keep_ref[...] = pay_ref[pl.ds(pl.multiple_of(core * share, ROWS), share), :]
    send_ref[...] = pay_ref[pl.ds(pl.multiple_of((1 - core) * share, ROWS), share), :].astype(BF16)


def split_again(values, plan, last):
    rows = values.shape[0]
    tail = values[rows - ROWS : rows - ROWS // 2] + values[rows - ROWS // 2 :]
    high = tail.astype(BF16).astype(F32)
    parted = jnp.concatenate([high, tail - high], axis=0)
    return jnp.where(last, parted, values[rows - ROWS :])


def core_sum_kernel(plan, keep_ref, got_ref, own_ref, *rest):
    sends, sum_ref = rest[:-1], rest[-1]
    group = lax.axis_index("sample") // plan.cores
    core = lax.axis_index("sample") % plan.cores
    rows = keep_ref.shape[0]
    sum_ref[...] = keep_ref[...] + got_ref[...].astype(F32)
    sum_ref[rows - ROWS :, :] = split_again(sum_ref[rows - ROWS :, :], plan, core == plan.cores - 1)

    def chunk(k):
        return sum_ref[pl.ds(pl.multiple_of((group ^ k) * plan.chunk, ROWS), plan.chunk), :]

    own_ref[...] = chunk(0)
    for k, send in enumerate(sends, start=1):
        send[...] = chunk(k).astype(BF16)


def last_chunk(plan):
    return lax.axis_index("sample") == lax.axis_size("sample") - 1


def group_sum_kernel(plan, own_ref, *rest):
    gots, out_ref = rest[:-1], rest[-1]
    total = own_ref[...]
    for got in gots:
        total = total + got[...].astype(F32)
    rows = total.shape[0]
    out_ref[: rows - ROWS, :] = total[: rows - ROWS].astype(BF16)
    out_ref[rows - ROWS :, :] = split_again(total[rows - ROWS :], plan, last_chunk(plan)).astype(BF16)


def space_sum_kernel(plan, *refs):
    values, out_ref = [ref[...].astype(F32) for ref in refs[:-1]], refs[-1]
    while len(values) > 1:
        values = [values[i] + values[i + 1] for i in range(0, len(values), 2)]
    total = values[0]
    rows = total.shape[0]
    out_ref[: rows - ROWS, :] = total[: rows - ROWS].astype(BF16)
    out_ref[rows - ROWS :, :] = split_again(total[rows - ROWS :], plan, last_chunk(plan)).astype(BF16)


def gather_kernel(plan, *refs):
    chunks, out_ref = refs[:-1], refs[-1]
    group = lax.axis_index("sample") // plan.cores
    for k, ref in enumerate(chunks):
        out_ref[pl.ds(pl.multiple_of((group ^ k) * plan.chunk, ROWS), plan.chunk), :] = ref[...]


def unpack_kernel(plan, mine_ref, other_ref, one_ref, bias_one_ref, two_ref, bias_two_ref, all_ref):
    inner, mid, out = plan.inner, plan.mid, plan.out
    core = lax.axis_index("sample") % plan.cores
    share = plan.total // plan.cores
    all_ref[pl.ds(pl.multiple_of(core * share, ROWS), share), :] = mine_ref[...].astype(F32)
    all_ref[pl.ds(pl.multiple_of((1 - core) * share, ROWS), share), :] = other_ref[...].astype(F32)
    total, first = 27 * mid, 9 * inner
    two_ref[...] = all_ref[:total, :].reshape(27, mid, out)
    pair = all_ref[total : total + first, :]
    one_ref[0:9] = pair[:, :mid].reshape(9, inner, mid)
    one_ref[9:18] = pair[:, mid:].reshape(9, inner, mid)
    pair = all_ref[total + first : total + first + first // 2, :]
    pair = jnp.concatenate([pair[:, :mid], pair[:, mid:]], axis=0)
    one_ref[18:27] = pair.reshape(9, inner, mid)
    tail = all_ref[plan.total - ROWS : plan.total - ROWS // 2, :] + all_ref[plan.total - ROWS // 2 : plan.total, :]
    bias_two_ref[...] = tail[0:1, :out]
    bias_one_ref[...] = tail[1:2, :mid]


class Plan:
    def __init__(self, volumes, kernel_first, kernel_second):
        self.space, self.sample = lax.axis_size("space"), lax.axis_size("sample")
        self.inner, self.mid, self.out = kernel_first.shape[2], kernel_first.shape[1], kernel_second.shape[1]
        self.owned = volumes.shape[0] // self.space
        self.part_blocks = volumes.shape[2] // LANES
        self.blocks = self.part_blocks * self.space
        self.halves = self.blocks // 8
        self.cores = 2
        self.groups = self.sample // self.cores
        cells = self.blocks * LANES * volumes.shape[0] * self.sample
        self.scale_one = 1.0 / math.sqrt(cells)
        self.scale_two = 1.0 / math.sqrt(cells // 8)
        used = 27 * self.mid + 9 * self.inner * 3 // 2 + ROWS
        step = ROWS * self.groups * self.cores
        self.total = -(-used // step) * step
        self.chunk = self.total // self.groups // self.cores


def call(kernel, plan, name, out_shapes, *args, scratch=(), limit=None):
    return pl.pallas_call(
        functools.partial(kernel, plan),
        out_shape=[jax.ShapeDtypeStruct(s, d) for s, d in out_shapes],
        in_specs=[vmem()] * len(args),
        out_specs=[vmem()] * len(out_shapes),
        scratch_shapes=[pltpu.VMEM(s, d) for s, d in scratch],
        compiler_params=pltpu.CompilerParams(vmem_limit_bytes=limit),
        name=name,
    )(*args)


def swap(value, axis, k):
    return lax.ppermute(value, axis, [(i, i ^ k) for i in range(lax.axis_size(axis))])


def on_device(volumes, grad_out, kernel_first, bias_first, kernel_second, bias_second):
    plan = Plan(volumes, kernel_first, kernel_second)
    inner, mid, out = plan.inner, plan.mid, plan.out
    me = lax.axis_index("space")

    def piece(k):
        return lax.dynamic_slice_in_dim(volumes, (me ^ k) * plan.owned, plan.owned, axis=0)

    parts = [piece(0)] + [swap(piece(k), "space", k) for k in range(1, plan.space)]
    weights = prepare_weights(kernel_first, bias_first, kernel_second, bias_second)
    cells, small = plan.blocks * LANES, plan.halves * LANES
    share = plan.total // plan.cores
    scratch = (
        ((plan.blocks, inner, LANES), BF16),
        ((9 * inner + ROWS, cells), BF16),
        ((3 * mid, cells), F32),
        ((mid, cells), F32),
        ((plan.blocks * mid, 2 * LANES), BF16),
        ((3 * mid, cells), BF16),
        ((9 * mid + ROWS, small), BF16),
        ((3 * out, small), F32),
        ((3 * out, small), BF16),
        ((9 * out, small), BF16),
        ((3 * mid, small), F32),
        ((plan.total, LANES), F32),
    )
    features, keep, send = call(
        main_kernel,
        plan,
        "main",
        (((plan.owned, out, small), BF16), ((share, LANES), F32), ((share, LANES), BF16)),
        *parts,
        grad_out,
        *weights,
        scratch=scratch,
        limit=48 * 1024 * 1024,
    )
    chunk = (plan.chunk, LANES)
    got = swap(send, "sample", 1)
    own, *sends = call(core_sum_kernel, plan, "core_sum", ((chunk, F32),) + ((chunk, BF16),) * (plan.groups - 1), keep, got, scratch=(((share, LANES), F32),))
    gots = [swap(s, "sample", plan.cores * k) for k, s in enumerate(sends, start=1)]
    (partial,) = call(group_sum_kernel, plan, "group_sum", ((chunk, BF16),), own, *gots)
    gots = [swap(partial, "space", k) for k in range(1, plan.space)]
    (whole,) = call(space_sum_kernel, plan, "space_sum", ((chunk, BF16),), partial, *gots)
    gots = [swap(whole, "sample", plan.cores * k) for k in range(1, plan.groups)]
    (mine,) = call(gather_kernel, plan, "gather", (((share, LANES), BF16),), whole, *gots)
    other = swap(mine, "sample", 1)
    one, bias_one, two, bias_two = call(
        unpack_kernel,
        plan,
        "unpack",
        (((27, inner, mid), F32), ((1, mid), F32), ((27, mid, out), F32), ((1, out), F32)),
        mine,
        other,
        scratch=(((plan.total, LANES), F32),),
    )
    return (features, jnp.swapaxes(one, 1, 2), bias_one.reshape(mid), jnp.swapaxes(two, 1, 2), bias_two.reshape(out))


def solution(mesh):
    in_specs = (P("sample", None, "space"), P(("sample", "space"), None, None), P(), P(), P(), P())
    out_specs = (P(("sample", "space"), None, None), P(), P(), P(), P())
    return jax.shard_map(
        on_device, mesh=mesh, in_specs=in_specs, out_specs=out_specs, check_vma=False
    )
```

time: 256 us -> 61.1 us (0.24)
  waiting for transfers between devices: 103 us -> 17.6 us
  local copies, waits for them, and re-layouts: 72.7 us -> 10 us
  blocking collectives: 39.5 us -> 0 us
  Pallas kernels: 0 us -> 15 us
  between operations: 14.6 us -> 0.7 us
  matrix products: 8.4 us -> 0 us
  starting transfers between devices: 13.4 us -> 17.1 us
  other arithmetic: 3.21 us -> 0 us
    psum x1 -> x0, waiting for transfers between devices: 89.5 us -> none  [on_device(): lax.psum((kernel_one, bias_one, kernel_two, bias_two), ('sample', 'space'))]
    psum x1 -> x0, blocking collectives: 39.5 us -> none  [on_device(): lax.psum((kernel_one, bias_one, kernel_two, bias_two), ('sample', 'space'))]
    reshape x27 -> x0, local copies, waits for them, and re-layouts: 25.7 us -> none  [stack_windows(): window.reshape(padded.shape[0], padded.shape[1], depth_len * side_len * s...]
    unnamed x137 -> x36, local copies, waits for them, and re-layouts: 29.7 us -> 9.22 us
    pallas_call x0 -> x7, Pallas kernels: none -> 15 us  [the longest x6 12.6 us: call(): pl.pallas_call(functools.partial(kernel, plan), out_shape=[jax.ShapeDtype...]
    ppermute x2 -> x14, waiting for transfers between devices: 4.51 us -> 17.6 us  [swap(): lax.ppermute(value, axis, [(i, i ^ k) for i in range(lax.axis_size(axis))])]
    ppermute x2 -> x14, starting transfers between devices: 6.21 us -> 17.1 us  [swap(): lax.ppermute(value, axis, [(i, i ^ k) for i in range(lax.axis_size(axis))])]
    slice x7 -> x0, local copies, waits for them, and re-layouts: 9.4 us -> none  [the longest x6 8.49 us: stack_windows(): padded[:, :, deep_off:deep_off + depth_len, high_off:high_off + side_len,...]
  transfers between devices with their start and end apart: 5 -> 14, of which waited for: 5 -> 13; matrix products, arithmetic and copies ran while one was open for 1% -> 0% of each run, Pallas kernels for 0% -> 4%
where the time goes in v1:
time: 61.1 us; the launch traced here: 60.5 us
  waiting for transfers between devices  17.6 us (29%)
  starting transfers between devices  17.1 us (28%)
  Pallas kernels  15 us (25%)
  local copies, waits for them, and re-layouts  10 us (16%)
  between operations  0.7 us (1%)
    ppermute x14, waiting for transfers between devices, swap(): lax.ppermute(value, axis, [(i, i ^ k) for i in range(lax.axis_size(axis))])  17.6 us
    ppermute x14, starting transfers between devices, swap(): lax.ppermute(value, axis, [(i, i ^ k) for i in range(lax.axis_size(axis))])  17.1 us
    pallas_call x6, Pallas kernels, call(): pl.pallas_call(functools.partial(kernel, plan), out_shape=[jax.ShapeDtype...  12.6 us
    unnamed x36, local copies, waits for them, and re-layouts  9.22 us
    pallas_call x1, Pallas kernels, prepare_weights(): pl.pallas_call(weights_kernel, out_shape=[jax.ShapeDtypeStruct(s, d) for...  2.48 us
  transfers between devices with their start and end apart: 14, of which 13 were waited for; matrix products, arithmetic and copies ran while one was open for 0% of the time, Pallas kernels for 4%

profile of v1, /device:TPU:0, one launch (start us, length us, event | category | flops | bytes accessed | tf_op | source)
XLA Modules:
  0.0 60.5 jit_solution(4805038801402712696)
XLA Ops:
  0.6 0.8 %constant_dynamic-slice_fusion = (bf16[1,32,512]{2,1,0:T(8,128)(2,1)S(1)}, bf16[1,32,512]{2,1,0:T(8,128)(2,1)S(1)}, bf16[1,32,512]{2,1,0:T(8,128)(2,1)S(1)}, bf16[1,32,512]{2,1,0:T(8,128)(2,1)S(1)}) fusion(bf16[4,32,512]{2,1,0:T(8,128)(2,1)} %param.6, s32[]{:T(128)S(6)} %select_n.15, s32[]{:T(128)S(6)} %select_n.13, s32[]{:T(128)S(6)} %select_n.12, s32[]{:T(128)S(6)} %select_n.14), kind=kLoop, calls=%fused_computation | loop fusion | bytes 262160 | tf_op jit(solution)/shard_map/dynamic_slice | solution.py:352
  1.5 5.1 %collective-permute-start.2 = (bf16[1,32,512]{2,1,0:T(8,128)(2,1)S(1)}, bf16[1,32,512]{2,1,0:T(8,128)(2,1)S(1)}, u32[]{:S(2)}, u32[]{:S(2)}) collective-permute-start(bf16[1,32,512]{2,1,0:T(8,128)(2,1)S(1)} %get-tuple-element.37), channel_id=1, source_target_pairs={{0,3},{1,2},{2,1},{3,0},{4,7},{5,6},{6,5},{7,4},{8,11},{9,10},{10,... | collective-permute-start | bytes 98312 | tf_op jit(solution)/shard_map/ppermute | solution.py:343
  6.6 0.0 collective-permute-start
  6.6 0.6 %collective-permute-start.1 = (bf16[1,32,512]{2,1,0:T(8,128)(2,1)S(1)}, bf16[1,32,512]{2,1,0:T(8,128)(2,1)S(1)}, u32[]{:S(2)}, u32[]{:S(2)}) collective-permute-start(bf16[1,32,512]{2,1,0:T(8,128)(2,1)S(1)} %get-tuple-element.40), channel_id=1, source_target_pairs={{0,2},{1,3},{2,0},{3,1},{4,6},{5,7},{6,4},{7,5},{8,10},{9,11},{10,... | collective-permute-start | bytes 98312 | tf_op jit(solution)/shard_map/ppermute | solution.py:343
  7.2 2.5 %weights.1 = (bf16[192,288]{1,0:T(8,128)(2,1)}, bf16[384,576]{1,0:T(8,128)(2,1)}, bf16[192,1152]{1,0:T(8,128)(2,1)}, f32[64,128]{1,0:T(8,128)}, f32[128,128]{1,0:T(8,128)}) custom-call(bf16[27,32,64]{2,1,0:T(8,128)(2,1)} %bitcast.9, bf16[27,64,128]{2,1,0:T(8,128)(2,1)} %bitcast.8, f32[1,64]{1,0:T(1,128)} %bitcast.10, f32[1,128]{1,0:T(1,128)} %bitcast.11), custom_call_target="tpu_custom_call" | custom-call | tf_op jit(solution)/shard_map/weights/pallas_call | solution.py:77
  9.7 0.8 %collective-permute-done.refs_1_ = bf16[1,32,512]{2,1,0:T(8,128)(2,1)S(1)} collective-permute-done((bf16[1,32,512]{2,1,0:T(8,128)(2,1)S(1)}, bf16[1,32,512]{2,1,0:T(8,128)(2,1)S(1)}, u32[]{:S(2)}, u32[]{:S(2)}) %collective-permute-start) | collective-permute-done | bytes 32800 | tf_op jit(solution)/shard_map/ppermute | solution.py:343
  10.5 1.0 %collective-permute-done.1.refs_2_ = bf16[1,32,512]{2,1,0:T(8,128)(2,1)S(1)} collective-permute-done((bf16[1,32,512]{2,1,0:T(8,128)(2,1)S(1)}, bf16[1,32,512]{2,1,0:T(8,128)(2,1)S(1)}, u32[]{:S(2)}, u32[]{:S(2)}) %collective-permute-start.1) | collective-permute-done | bytes 32800 | tf_op jit(solution)/shard_map/ppermute | solution.py:343
  11.5 1.0 %copy-done.1 = bf16[384,576]{1,0:T(8,128)(2,1)S(1)} copy-done((bf16[384,576]{1,0:T(8,128)(2,1)S(1)}, bf16[384,576]{1,0:T(8,128)(2,1)}, u32[]{:S(2)}) %copy-start.1) | copy-done | bytes 442392
  12.6 1.0 %copy-done.2 = bf16[192,1152]{1,0:T(8,128)(2,1)S(1)} copy-done((bf16[192,1152]{1,0:T(8,128)(2,1)S(1)}, bf16[192,1152]{1,0:T(8,128)(2,1)}, u32[]{:S(2)}) %copy-start.2) | copy-done | bytes 442392
  13.6 0.9 %copy-done.3 = bf16[192,288]{1,0:T(8,128)(2,1)S(1)} copy-done((bf16[192,288]{1,0:T(8,128)(2,1)S(1)}, bf16[192,288]{1,0:T(8,128)(2,1)}, u32[]{:S(2)}) %copy-start.3) | copy-done | bytes 110616
  14.5 0.8 %copy-done.5 = f32[128,128]{1,0:T(8,128)S(1)} copy-done((f32[128,128]{1,0:T(8,128)S(1)}, f32[128,128]{1,0:T(8,128)}, u32[]{:S(2)}) %copy-start.5) | copy-done | bytes 65560
  15.3 0.8 %copy-done.6 = f32[64,128]{1,0:T(8,128)S(1)} copy-done((f32[64,128]{1,0:T(8,128)S(1)}, f32[64,128]{1,0:T(8,128)}, u32[]{:S(2)}) %copy-start.6) | copy-done | bytes 32792
  16.1 3.3 %main.1 = (bf16[1,128,256]{2,1,0:T(8,128)(2,1)}, f32[1088,128]{1,0:T(8,128)S(1)}, bf16[1088,128]{1,0:T(8,128)(2,1)S(1)}) custom-call(bf16[1,32,512]{2,1,0:T(8,128)(2,1)S(1)} %get-tuple-element.39.refs_0_, bf16[1,32,512]{2,1,0:T(8,128)(2,1)S(1)} %collective-permute-done.refs_1_, bf16[1,32,512]{2,1,0:T(8,128)(2,1)S(1)} %collective-permute-done.1.refs_2_, ...), custom_call_target="tpu_custom_call" | custom-call | tf_op jit(solution)/shard_map/main/pallas_call | solution.py:331
  19.4 0.0 copy-start
  19.4 0.8 %copy-done = f32[1088,128]{1,0:T(8,128)} copy-done((f32[1088,128]{1,0:T(8,128)}, f32[1088,128]{1,0:T(8,128)S(1)}, u32[]{:S(2)}) %copy-start) | copy-done | bytes 557080
  20.2 0.0 collective-permute-start.3
  20.2 1.6 %collective-permute-done.3.got_ref = bf16[1088,128]{1,0:T(8,128)(2,1)S(1)} collective-permute-done((bf16[1088,128]{1,0:T(8,128)(2,1)S(1)}, bf16[1088,128]{1,0:T(8,128)(2,1)S(1)}, u32[]{:S(2)}, u32[]{:S(2)}) %collective-permute-start.3) | collective-permute-done | bytes 278560 | tf_op jit(solution)/shard_map/ppermute | solution.py:343
  21.8 0.7 %copy-done.7 = bf16[1088,128]{1,0:T(8,128)(2,1)} copy-done((bf16[1088,128]{1,0:T(8,128)(2,1)}, bf16[1088,128]{1,0:T(8,128)(2,1)S(1)}, u32[]{:S(2)}) %copy-start.7) | copy-done | bytes 278552
  22.5 1.9 %core_sum.1 = (f32[272,128]{1,0:T(8,128)}, bf16[272,128]{1,0:T(8,128)(2,1)}, bf16[272,128]{1,0:T(8,128)(2,1)}, bf16[272,128]{1,0:T(8,128)(2,1)}) custom-call(f32[1088,128]{1,0:T(8,128)} %copy-done, bf16[1088,128]{1,0:T(8,128)(2,1)} %copy-done.7), custom_call_target="tpu_custom_call" | custom-call | tf_op jit(solution)/shard_map/core_sum/pallas_call | solution.py:331
  24.4 1.5 %collective-permute-start.4 = (bf16[272,128]{1,0:T(8,128)(2,1)}, bf16[272,128]{1,0:T(8,128)(2,1)S(1)}, u32[]{:S(2)}, u32[]{:S(2)}) collective-permute-start(bf16[272,128]{1,0:T(8,128)(2,1)} %get-tuple-element.30), channel_id=1, source_target_pairs={{0,8},{4,12},{8,0},{12,4},{16,24},{20,28},{24,16},{28,20},{1,9},{5... | collective-permute-start | bytes 208904 | tf_op jit(solution)/shard_map/ppermute | solution.py:343
  25.9 1.5 %collective-permute-start.5 = (bf16[272,128]{1,0:T(8,128)(2,1)}, bf16[272,128]{1,0:T(8,128)(2,1)S(1)}, u32[]{:S(2)}, u32[]{:S(2)}) collective-permute-start(bf16[272,128]{1,0:T(8,128)(2,1)} %get-tuple-element.31), channel_id=1, source_target_pairs={{0,16},{4,20},{8,24},{12,28},{16,0},{20,4},{24,8},{28,12},{1,17},{... | collective-permute-start | bytes 208904 | tf_op jit(solution)/shard_map/ppermute | solution.py:343
  27.4 0.5 collective-permute-start.6
  27.9 1.0 %collective-permute-done.4.rest_0_ = bf16[272,128]{1,0:T(8,128)(2,1)S(1)} collective-permute-done((bf16[272,128]{1,0:T(8,128)(2,1)}, bf16[272,128]{1,0:T(8,128)(2,1)S(1)}, u32[]{:S(2)}, u32[]{:S(2)}) %collective-permute-start.4) | collective-permute-done | bytes 69664 | tf_op jit(solution)/shard_map/ppermute | solution.py:343
  28.9 1.5 %collective-permute-done.5.rest_1_ = bf16[272,128]{1,0:T(8,128)(2,1)S(1)} collective-permute-done((bf16[272,128]{1,0:T(8,128)(2,1)}, bf16[272,128]{1,0:T(8,128)(2,1)S(1)}, u32[]{:S(2)}, u32[]{:S(2)}) %collective-permute-start.5) | collective-permute-done | bytes 69664 | tf_op jit(solution)/shard_map/ppermute | solution.py:343
  30.4 2.4 %collective-permute-done.6.rest_2_ = bf16[272,128]{1,0:T(8,128)(2,1)S(1)} collective-permute-done((bf16[272,128]{1,0:T(8,128)(2,1)}, bf16[272,128]{1,0:T(8,128)(2,1)S(1)}, u32[]{:S(2)}, u32[]{:S(2)}) %collective-permute-start.6) | collective-permute-done | bytes 69664 | tf_op jit(solution)/shard_map/ppermute | solution.py:343
  32.8 0.6 %copy-done.12 = bf16[272,128]{1,0:T(8,128)(2,1)} copy-done((bf16[272,128]{1,0:T(8,128)(2,1)}, bf16[272,128]{1,0:T(8,128)(2,1)S(1)}, u32[]{:S(2)}) %copy-start.12) | copy-done | bytes 69656
  33.5 1.7 %group_sum.1.refs_0_ = bf16[272,128]{1,0:T(8,128)(2,1)} custom-call(f32[272,128]{1,0:T(8,128)} %get-tuple-element.29.own_ref, bf16[272,128]{1,0:T(8,128)(2,1)} %copy-done.9, bf16[272,128]{1,0:T(8,128)(2,1)} %copy-done.10, bf16[272,128]{1,0:T(8,128)(2,1)} %copy-done.12), custom_call_target="tpu_custom_call" | custom-call | tf_op jit(solution)/shard_map/group_sum/pallas_call | solution.py:331
  35.1 2.0 %collective-permute-start.9 = (bf16[272,128]{1,0:T(8,128)(2,1)}, bf16[272,128]{1,0:T(8,128)(2,1)S(1)}, u32[]{:S(2)}, u32[]{:S(2)}) collective-permute-start(bf16[272,128]{1,0:T(8,128)(2,1)} %group_sum.1.refs_0_), channel_id=1, source_target_pairs={{0,3},{1,2},{2,1},{3,0},{4,7},{5,6},{6,5},{7,4},{8,11},{9,10},{10,... | collective-permute-start | bytes 208904 | tf_op jit(solution)/shard_map/ppermute | solution.py:343
  37.1 1.4 %collective-permute-start.8 = (bf16[272,128]{1,0:T(8,128)(2,1)}, bf16[272,128]{1,0:T(8,128)(2,1)S(1)}, u32[]{:S(2)}, u32[]{:S(2)}) collective-permute-start(bf16[272,128]{1,0:T(8,128)(2,1)} %group_sum.1.refs_0_), channel_id=1, source_target_pairs={{0,2},{1,3},{2,0},{3,1},{4,6},{5,7},{6,4},{7,5},{8,10},{9,11},{10,... | collective-permute-start | bytes 208904 | tf_op jit(solution)/shard_map/ppermute | solution.py:343
  38.5 1.0 %collective-permute-start.7 = (bf16[272,128]{1,0:T(8,128)(2,1)}, bf16[272,128]{1,0:T(8,128)(2,1)S(1)}, u32[]{:S(2)}, u32[]{:S(2)}) collective-permute-start(bf16[272,128]{1,0:T(8,128)(2,1)} %group_sum.1.refs_0_), channel_id=1, source_target_pairs={{0,1},{1,0},{2,3},{3,2},{4,5},{5,4},{6,7},{7,6},{8,9},{9,8},{10,11... | collective-permute-start | bytes 208904 | tf_op jit(solution)/shard_map/ppermute | solution.py:343
  39.5 2.1 %collective-permute-done.9.refs_3_ = bf16[272,128]{1,0:T(8,128)(2,1)S(1)} collective-permute-done((bf16[272,128]{1,0:T(8,128)(2,1)}, bf16[272,128]{1,0:T(8,128)(2,1)S(1)}, u32[]{:S(2)}, u32[]{:S(2)}) %collective-permute-start.9) | collective-permute-done | bytes 69664 | tf_op jit(solution)/shard_map/ppermute | solution.py:343
  41.6 2.2 %collective-permute-done.8.refs_2_ = bf16[272,128]{1,0:T(8,128)(2,1)S(1)} collective-permute-done((bf16[272,128]{1,0:T(8,128)(2,1)}, bf16[272,128]{1,0:T(8,128)(2,1)S(1)}, u32[]{:S(2)}, u32[]{:S(2)}) %collective-permute-start.8) | collective-permute-done | bytes 69664 | tf_op jit(solution)/shard_map/ppermute | solution.py:343
  43.8 0.1 collective-permute-done.7.refs_1_
  43.9 0.5 copy-done.16
  44.4 0.6 %copy-done.17 = bf16[272,128]{1,0:T(8,128)(2,1)} copy-done((bf16[272,128]{1,0:T(8,128)(2,1)}, bf16[272,128]{1,0:T(8,128)(2,1)S(1)}, u32[]{:S(2)}) %copy-start.17) | copy-done | bytes 69656
  45.0 1.6 %space_sum.1.refs_0_ = bf16[272,128]{1,0:T(8,128)(2,1)} custom-call(bf16[272,128]{1,0:T(8,128)(2,1)} %group_sum.1.refs_0_, bf16[272,128]{1,0:T(8,128)(2,1)} %copy-done.17, bf16[272,128]{1,0:T(8,128)(2,1)} %copy-done.16, bf16[272,128]{1,0:T(8,128)(2,1)} %copy-done.15), custom_call_target="tpu_custom_call" | custom-call | tf_op jit(solution)/shard_map/space_sum/pallas_call | solution.py:331
  46.7 0.7 %collective-permute-start.12 = (bf16[272,128]{1,0:T(8,128)(2,1)}, bf16[272,128]{1,0:T(8,128)(2,1)S(1)}, u32[]{:S(2)}, u32[]{:S(2)}) collective-permute-start(bf16[272,128]{1,0:T(8,128)(2,1)} %space_sum.1.refs_0_), channel_id=1, source_target_pairs={{0,24},{4,28},{8,16},{12,20},{16,8},{20,12},{24,0},{28,4},{1,25},{... | collective-permute-start | bytes 208904 | tf_op jit(solution)/shard_map/ppermute | solution.py:343
  47.4 1.5 %collective-permute-start.11 = (bf16[272,128]{1,0:T(8,128)(2,1)}, bf16[272,128]{1,0:T(8,128)(2,1)S(1)}, u32[]{:S(2)}, u32[]{:S(2)}) collective-permute-start(bf16[272,128]{1,0:T(8,128)(2,1)} %space_sum.1.refs_0_), channel_id=1, source_target_pairs={{0,16},{4,20},{8,24},{12,28},{16,0},{20,4},{24,8},{28,12},{1,17},{... | collective-permute-start | bytes 208904 | tf_op jit(solution)/shard_map/ppermute | solution.py:343
  48.8 1.3 %collective-permute-start.10 = (bf16[272,128]{1,0:T(8,128)(2,1)}, bf16[272,128]{1,0:T(8,128)(2,1)S(1)}, u32[]{:S(2)}, u32[]{:S(2)}) collective-permute-start(bf16[272,128]{1,0:T(8,128)(2,1)} %space_sum.1.refs_0_), channel_id=1, source_target_pairs={{0,8},{4,12},{8,0},{12,4},{16,24},{20,28},{24,16},{28,20},{1,9},{5... | collective-permute-start | bytes 208904 | tf_op jit(solution)/shard_map/ppermute | solution.py:343
  50.2 2.0 %collective-permute-done.12.refs_3_ = bf16[272,128]{1,0:T(8,128)(2,1)S(1)} collective-permute-done((bf16[272,128]{1,0:T(8,128)(2,1)}, bf16[272,128]{1,0:T(8,128)(2,1)S(1)}, u32[]{:S(2)}, u32[]{:S(2)}) %collective-permute-start.12) | collective-permute-done | bytes 69664 | tf_op jit(solution)/shard_map/ppermute | solution.py:343
  52.2 0.4 collective-permute-done.11.refs_2_
  52.6 0.7 %collective-permute-done.10.refs_1_ = bf16[272,128]{1,0:T(8,128)(2,1)S(1)} collective-permute-done((bf16[272,128]{1,0:T(8,128)(2,1)}, bf16[272,128]{1,0:T(8,128)(2,1)S(1)}, u32[]{:S(2)}, u32[]{:S(2)}) %collective-permute-start.10) | collective-permute-done | bytes 69664 | tf_op jit(solution)/shard_map/ppermute | solution.py:343
  53.4 0.6 %copy-done.14 = bf16[272,128]{1,0:T(8,128)(2,1)} copy-done((bf16[272,128]{1,0:T(8,128)(2,1)}, bf16[272,128]{1,0:T(8,128)(2,1)S(1)}, u32[]{:S(2)}) %copy-start.14) | copy-done | bytes 69656
  54.0 1.7 %gather.1.mine_ref = bf16[1088,128]{1,0:T(8,128)(2,1)} custom-call(bf16[272,128]{1,0:T(8,128)(2,1)} %space_sum.1.refs_0_, bf16[272,128]{1,0:T(8,128)(2,1)} %copy-done.14, bf16[272,128]{1,0:T(8,128)(2,1)} %copy-done.13, bf16[272,128]{1,0:T(8,128)(2,1)} %copy-done.11), custom_call_target="tpu_custom_call" | custom-call | tf_op jit(solution)/shard_map/gather/pallas_call | solution.py:331
  55.7 0.0 collective-permute-start.13
  55.7 1.8 %collective-permute-done.13.other_ref = bf16[1088,128]{1,0:T(8,128)(2,1)S(1)} collective-permute-done((bf16[1088,128]{1,0:T(8,128)(2,1)}, bf16[1088,128]{1,0:T(8,128)(2,1)S(1)}, u32[]{:S(2)}, u32[]{:S(2)}) %collective-permute-start.13) | collective-permute-done | bytes 278560 | tf_op jit(solution)/shard_map/ppermute | solution.py:343
  57.5 0.7 %copy-done.8 = bf16[1088,128]{1,0:T(8,128)(2,1)} copy-done((bf16[1088,128]{1,0:T(8,128)(2,1)}, bf16[1088,128]{1,0:T(8,128)(2,1)S(1)}, u32[]{:S(2)}) %copy-start.8) | copy-done | bytes 278552
  58.2 2.3 %unpack.1 = (f32[27,32,64]{2,1,0:T(8,128)}, f32[1,64]{1,0:T(1,128)}, f32[27,64,128]{2,1,0:T(8,128)}, f32[1,128]{1,0:T(1,128)}) custom-call(bf16[1088,128]{1,0:T(8,128)(2,1)} %gather.1.mine_ref, bf16[1088,128]{1,0:T(8,128)(2,1)} %copy-done.8), custom_call_target="tpu_custom_call" | custom-call | tf_op jit(solution)/shard_map/unpack/pallas_call | solution.py:331
  (24 shorter events, 0.0 us)
Async XLA Ops:
  1.5 8.2 %collective-permute-start.2 = (bf16[1,32,512]{2,1,0:T(8,128)(2,1)S(1)}, bf16[1,32,512]{2,1,0:T(8,128)(2,1)S(1)}, u32[]{:S(2)}, u32[]{:S(2)}) collective-permute-start(bf16[1,32,512]{2,1,0:T(8,128)(2,1)S(1)} %get-tuple-element.37), channel_id=1, source_target_pairs={{0,3},{1,2},{2,1},{3,0},{4,7},{5,6},{6,5},{7,4},{8,11},{9,10},{10,... | collective-permute-start | bytes 98312 | tf_op jit(solution)/shard_map/ppermute | solution.py:343
  6.6 3.9 %collective-permute-start = (bf16[1,32,512]{2,1,0:T(8,128)(2,1)S(1)}, bf16[1,32,512]{2,1,0:T(8,128)(2,1)S(1)}, u32[]{:S(2)}, u32[]{:S(2)}) collective-permute-start(bf16[1,32,512]{2,1,0:T(8,128)(2,1)S(1)} %get-tuple-element.38), channel_id=1, source_target_pairs={{0,1},{1,0},{2,3},{3,2},{4,5},{5,4},{6,7},{7,6},{8,9},{9,8},{10,11... | collective-permute-start | bytes 98312 | tf_op jit(solution)/shard_map/ppermute | solution.py:343
  6.6 4.9 %collective-permute-start.1 = (bf16[1,32,512]{2,1,0:T(8,128)(2,1)S(1)}, bf16[1,32,512]{2,1,0:T(8,128)(2,1)S(1)}, u32[]{:S(2)}, u32[]{:S(2)}) collective-permute-start(bf16[1,32,512]{2,1,0:T(8,128)(2,1)S(1)} %get-tuple-element.40), channel_id=1, source_target_pairs={{0,2},{1,3},{2,0},{3,1},{4,6},{5,7},{6,4},{7,5},{8,10},{9,11},{10,... | collective-permute-start | bytes 98312 | tf_op jit(solution)/shard_map/ppermute | solution.py:343
  7.2 4.3 %copy-start.4 = (bf16[1,128,256]{2,1,0:T(8,128)(2,1)S(1)}, bf16[1,128,256]{2,1,0:T(8,128)(2,1)}, u32[]{:S(2)}) copy-start(bf16[1,128,256]{2,1,0:T(8,128)(2,1)} %refs_4_.1) | copy-start | bytes 196612
  11.5 1.0 %copy-start.1 = (bf16[384,576]{1,0:T(8,128)(2,1)S(1)}, bf16[384,576]{1,0:T(8,128)(2,1)}, u32[]{:S(2)}) copy-start(bf16[384,576]{1,0:T(8,128)(2,1)} %get-tuple-element.22.refs_6_) | copy-start | bytes 1327108
  12.6 1.0 %copy-start.2 = (bf16[192,1152]{1,0:T(8,128)(2,1)S(1)}, bf16[192,1152]{1,0:T(8,128)(2,1)}, u32[]{:S(2)}) copy-start(bf16[192,1152]{1,0:T(8,128)(2,1)} %get-tuple-element.23.refs_7_) | copy-start | bytes 1327108
  13.6 0.9 %copy-start.3 = (bf16[192,288]{1,0:T(8,128)(2,1)S(1)}, bf16[192,288]{1,0:T(8,128)(2,1)}, u32[]{:S(2)}) copy-start(bf16[192,288]{1,0:T(8,128)(2,1)} %get-tuple-element.21.refs_5_) | copy-start | bytes 331780
  14.5 0.8 %copy-start.5 = (f32[128,128]{1,0:T(8,128)S(1)}, f32[128,128]{1,0:T(8,128)}, u32[]{:S(2)}) copy-start(f32[128,128]{1,0:T(8,128)} %get-tuple-element.25.refs_9_) | copy-start | bytes 196612
  15.3 0.8 %copy-start.6 = (f32[64,128]{1,0:T(8,128)S(1)}, f32[64,128]{1,0:T(8,128)}, u32[]{:S(2)}) copy-start(f32[64,128]{1,0:T(8,128)} %get-tuple-element.24.refs_8_) | copy-start | bytes 98308
  19.4 0.8 %copy-start = (f32[1088,128]{1,0:T(8,128)}, f32[1088,128]{1,0:T(8,128)S(1)}, u32[]{:S(2)}) copy-start(f32[1088,128]{1,0:T(8,128)S(1)} %get-tuple-element.27.keep_ref) | copy-start | bytes 1671172
  20.2 1.6 %collective-permute-start.3 = (bf16[1088,128]{1,0:T(8,128)(2,1)S(1)}, bf16[1088,128]{1,0:T(8,128)(2,1)S(1)}, u32[]{:S(2)}, u32[]{:S(2)}) collective-permute-start(bf16[1088,128]{1,0:T(8,128)(2,1)S(1)} %get-tuple-element.28), channel_id=1, source_target_pairs={{0,4},{4,0},{8,12},{12,8},{16,20},{20,16},{24,28},{28,24},{1,5},{5... | collective-permute-start | bytes 835592 | tf_op jit(solution)/shard_map/ppermute | solution.py:343
  21.8 0.7 %copy-start.7 = (bf16[1088,128]{1,0:T(8,128)(2,1)}, bf16[1088,128]{1,0:T(8,128)(2,1)S(1)}, u32[]{:S(2)}) copy-start(bf16[1088,128]{1,0:T(8,128)(2,1)S(1)} %collective-permute-done.3.got_ref) | copy-start | bytes 835588
  24.4 4.5 %collective-permute-start.4 = (bf16[272,128]{1,0:T(8,128)(2,1)}, bf16[272,128]{1,0:T(8,128)(2,1)S(1)}, u32[]{:S(2)}, u32[]{:S(2)}) collective-permute-start(bf16[272,128]{1,0:T(8,128)(2,1)} %get-tuple-element.30), channel_id=1, source_target_pairs={{0,8},{4,12},{8,0},{12,4},{16,24},{20,28},{24,16},{28,20},{1,9},{5... | collective-permute-start | bytes 208904 | tf_op jit(solution)/shard_map/ppermute | solution.py:343
  25.9 4.5 %collective-permute-start.5 = (bf16[272,128]{1,0:T(8,128)(2,1)}, bf16[272,128]{1,0:T(8,128)(2,1)S(1)}, u32[]{:S(2)}, u32[]{:S(2)}) collective-permute-start(bf16[272,128]{1,0:T(8,128)(2,1)} %get-tuple-element.31), channel_id=1, source_target_pairs={{0,16},{4,20},{8,24},{12,28},{16,0},{20,4},{24,8},{28,12},{1,17},{... | collective-permute-start | bytes 208904 | tf_op jit(solution)/shard_map/ppermute | solution.py:343
  27.4 5.4 %collective-permute-start.6 = (bf16[272,128]{1,0:T(8,128)(2,1)}, bf16[272,128]{1,0:T(8,128)(2,1)S(1)}, u32[]{:S(2)}, u32[]{:S(2)}) collective-permute-start(bf16[272,128]{1,0:T(8,128)(2,1)} %get-tuple-element.32), channel_id=1, source_target_pairs={{0,24},{4,28},{8,16},{12,20},{16,8},{20,12},{24,0},{28,4},{1,25},{... | collective-permute-start | bytes 208904 | tf_op jit(solution)/shard_map/ppermute | solution.py:343
  28.9 3.9 %copy-start.9 = (bf16[272,128]{1,0:T(8,128)(2,1)}, bf16[272,128]{1,0:T(8,128)(2,1)S(1)}, u32[]{:S(2)}) copy-start(bf16[272,128]{1,0:T(8,128)(2,1)S(1)} %collective-permute-done.4.rest_0_) | copy-start | bytes 208900
  30.4 2.4 %copy-start.10 = (bf16[272,128]{1,0:T(8,128)(2,1)}, bf16[272,128]{1,0:T(8,128)(2,1)S(1)}, u32[]{:S(2)}) copy-start(bf16[272,128]{1,0:T(8,128)(2,1)S(1)} %collective-permute-done.5.rest_1_) | copy-start | bytes 208900
  32.8 0.6 %copy-start.12 = (bf16[272,128]{1,0:T(8,128)(2,1)}, bf16[272,128]{1,0:T(8,128)(2,1)S(1)}, u32[]{:S(2)}) copy-start(bf16[272,128]{1,0:T(8,128)(2,1)S(1)} %collective-permute-done.6.rest_2_) | copy-start | bytes 208900
  35.1 6.5 %collective-permute-start.9 = (bf16[272,128]{1,0:T(8,128)(2,1)}, bf16[272,128]{1,0:T(8,128)(2,1)S(1)}, u32[]{:S(2)}, u32[]{:S(2)}) collective-permute-start(bf16[272,128]{1,0:T(8,128)(2,1)} %group_sum.1.refs_0_), channel_id=1, source_target_pairs={{0,3},{1,2},{2,1},{3,0},{4,7},{5,6},{6,5},{7,4},{8,11},{9,10},{10,... | collective-permute-start | bytes 208904 | tf_op jit(solution)/shard_map/ppermute | solution.py:343
  37.1 6.7 %collective-permute-start.8 = (bf16[272,128]{1,0:T(8,128)(2,1)}, bf16[272,128]{1,0:T(8,128)(2,1)S(1)}, u32[]{:S(2)}, u32[]{:S(2)}) collective-permute-start(bf16[272,128]{1,0:T(8,128)(2,1)} %group_sum.1.refs_0_), channel_id=1, source_target_pairs={{0,2},{1,3},{2,0},{3,1},{4,6},{5,7},{6,4},{7,5},{8,10},{9,11},{10,... | collective-permute-start | bytes 208904 | tf_op jit(solution)/shard_map/ppermute | solution.py:343
  38.5 5.4 %collective-permute-start.7 = (bf16[272,128]{1,0:T(8,128)(2,1)}, bf16[272,128]{1,0:T(8,128)(2,1)S(1)}, u32[]{:S(2)}, u32[]{:S(2)}) collective-permute-start(bf16[272,128]{1,0:T(8,128)(2,1)} %group_sum.1.refs_0_), channel_id=1, source_target_pairs={{0,1},{1,0},{2,3},{3,2},{4,5},{5,4},{6,7},{7,6},{8,9},{9,8},{10,11... | collective-permute-start | bytes 208904 | tf_op jit(solution)/shard_map/ppermute | solution.py:343
  41.6 2.2 %copy-start.15 = (bf16[272,128]{1,0:T(8,128)(2,1)}, bf16[272,128]{1,0:T(8,128)(2,1)S(1)}, u32[]{:S(2)}) copy-start(bf16[272,128]{1,0:T(8,128)(2,1)S(1)} %collective-permute-done.9.refs_3_) | copy-start | bytes 208900
  43.8 0.6 %copy-start.16 = (bf16[272,128]{1,0:T(8,128)(2,1)}, bf16[272,128]{1,0:T(8,128)(2,1)S(1)}, u32[]{:S(2)}) copy-start(bf16[272,128]{1,0:T(8,128)(2,1)S(1)} %collective-permute-done.8.refs_2_) | copy-start | bytes 208900
  44.4 0.6 %copy-start.17 = (bf16[272,128]{1,0:T(8,128)(2,1)}, bf16[272,128]{1,0:T(8,128)(2,1)S(1)}, u32[]{:S(2)}) copy-start(bf16[272,128]{1,0:T(8,128)(2,1)S(1)} %collective-permute-done.7.refs_1_) | copy-start | bytes 208900
  46.7 5.5 %collective-permute-start.12 = (bf16[272,128]{1,0:T(8,128)(2,1)}, bf16[272,128]{1,0:T(8,128)(2,1)S(1)}, u32[]{:S(2)}, u32[]{:S(2)}) collective-permute-start(bf16[272,128]{1,0:T(8,128)(2,1)} %space_sum.1.refs_0_), channel_id=1, source_target_pairs={{0,24},{4,28},{8,16},{12,20},{16,8},{20,12},{24,0},{28,4},{1,25},{... | collective-permute-start | bytes 208904 | tf_op jit(solution)/shard_map/ppermute | solution.py:343
  47.4 5.3 %collective-permute-start.11 = (bf16[272,128]{1,0:T(8,128)(2,1)}, bf16[272,128]{1,0:T(8,128)(2,1)S(1)}, u32[]{:S(2)}, u32[]{:S(2)}) collective-permute-start(bf16[272,128]{1,0:T(8,128)(2,1)} %space_sum.1.refs_0_), channel_id=1, source_target_pairs={{0,16},{4,20},{8,24},{12,28},{16,0},{20,4},{24,8},{28,12},{1,17},{... | collective-permute-start | bytes 208904 | tf_op jit(solution)/shard_map/ppermute | solution.py:343
  48.8 4.5 %collective-permute-start.10 = (bf16[272,128]{1,0:T(8,128)(2,1)}, bf16[272,128]{1,0:T(8,128)(2,1)S(1)}, u32[]{:S(2)}, u32[]{:S(2)}) collective-permute-start(bf16[272,128]{1,0:T(8,128)(2,1)} %space_sum.1.refs_0_), channel_id=1, source_target_pairs={{0,8},{4,12},{8,0},{12,4},{16,24},{20,28},{24,16},{28,20},{1,9},{5... | collective-permute-start | bytes 208904 | tf_op jit(solution)/shard_map/ppermute | solution.py:343
  52.2 1.1 %copy-start.11 = (bf16[272,128]{1,0:T(8,128)(2,1)}, bf16[272,128]{1,0:T(8,128)(2,1)S(1)}, u32[]{:S(2)}) copy-start(bf16[272,128]{1,0:T(8,128)(2,1)S(1)} %collective-permute-done.12.refs_3_) | copy-start | bytes 208900
  52.6 0.7 %copy-start.13 = (bf16[272,128]{1,0:T(8,128)(2,1)}, bf16[272,128]{1,0:T(8,128)(2,1)S(1)}, u32[]{:S(2)}) copy-start(bf16[272,128]{1,0:T(8,128)(2,1)S(1)} %collective-permute-done.11.refs_2_) | copy-start | bytes 208900
  53.4 0.6 %copy-start.14 = (bf16[272,128]{1,0:T(8,128)(2,1)}, bf16[272,128]{1,0:T(8,128)(2,1)S(1)}, u32[]{:S(2)}) copy-start(bf16[272,128]{1,0:T(8,128)(2,1)S(1)} %collective-permute-done.10.refs_1_) | copy-start | bytes 208900
  55.7 1.8 %collective-permute-start.13 = (bf16[1088,128]{1,0:T(8,128)(2,1)}, bf16[1088,128]{1,0:T(8,128)(2,1)S(1)}, u32[]{:S(2)}, u32[]{:S(2)}) collective-permute-start(bf16[1088,128]{1,0:T(8,128)(2,1)} %gather.1.mine_ref), channel_id=1, source_target_pairs={{0,4},{4,0},{8,12},{12,8},{16,20},{20,16},{24,28},{28,24},{1,5},{5... | collective-permute-start | bytes 835592 | tf_op jit(solution)/shard_map/ppermute | solution.py:343
  57.5 0.7 %copy-start.8 = (bf16[1088,128]{1,0:T(8,128)(2,1)}, bf16[1088,128]{1,0:T(8,128)(2,1)S(1)}, u32[]{:S(2)}) copy-start(bf16[1088,128]{1,0:T(8,128)(2,1)S(1)} %collective-permute-done.13.other_ref) | copy-start | bytes 835588

commit v2 on v1

--- a/solution.py
+++ b/solution.py
@@ -12,6 +12,7 @@
 LEAK_SLOPE = 0.3
 LANES = 128
 ROWS = 16
+SMALL_LIMIT = 4 * 1024 * 1024
 BF16 = jnp.bfloat16
 F32 = jnp.float32
 
@@ -79,6 +80,7 @@
         out_shape=[jax.ShapeDtypeStruct(s, d) for s, d in shapes],
         in_specs=[vmem()] * 4,
         out_specs=[vmem()] * 5,
+        compiler_params=pltpu.CompilerParams(vmem_limit_bytes=SMALL_LIMIT),
         name="weights",
     )(first, second, bias_first.reshape(1, -1), bias_second.reshape(1, -1))
 
@@ -327,7 +329,7 @@
         self.chunk = self.total // self.groups // self.cores
 
 
-def call(kernel, plan, name, out_shapes, *args, scratch=(), limit=None):
+def call(kernel, plan, name, out_shapes, *args, scratch=(), limit=SMALL_LIMIT):
     return pl.pallas_call(
         functools.partial(kernel, plan),
         out_shape=[jax.ShapeDtypeStruct(s, d) for s, d in out_shapes],

time: 61.1 us -> 43.1 us (0.71)
  Pallas kernels: 15 us -> 5.19 us
  local copies, waits for them, and re-layouts: 10 us -> 2.57 us
    pallas_call x6, Pallas kernels: 12.6 us -> 4.76 us  [call(): pl.pallas_call(functools.partial(kernel, plan), out_shape=[jax.ShapeDtype...]
    unnamed x36 -> x10, local copies, waits for them, and re-layouts: 9.22 us -> 1.69 us
    pallas_call x1, Pallas kernels: 2.48 us -> 0.43 us  [prepare_weights(): pl.pallas_call(weights_kernel, out_shape=[jax.ShapeDtypeStruct(s, d) for...]
  transfers between devices with their start and end apart: 14 -> 14, of which waited for: 13 -> 13; matrix products, arithmetic and copies ran while one was open for 0% -> 0% of each run, Pallas kernels for 4% -> 1%
where the time goes in v2:
time: 43.1 us; the launch traced here: 42.9 us
  starting transfers between devices  17.5 us (41%)
  waiting for transfers between devices  17 us (39%)
  Pallas kernels  5.19 us (12%)
  local copies, waits for them, and re-layouts  2.57 us (6%)
  between operations  0.73 us (2%)
    ppermute x14, starting transfers between devices, swap(): lax.ppermute(value, axis, [(i, i ^ k) for i in range(lax.axis_size(axis))])  17.5 us
    ppermute x14, waiting for transfers between devices, swap(): lax.ppermute(value, axis, [(i, i ^ k) for i in range(lax.axis_size(axis))])  17 us
    pallas_call x6, Pallas kernels, call(): pl.pallas_call(functools.partial(kernel, plan), out_shape=[jax.ShapeDtype...  4.76 us
    unnamed x10, local copies, waits for them, and re-layouts  1.69 us
    dynamic_slice x1, local copies, waits for them, and re-layouts, piece(): lax.dynamic_slice_in_dim(volumes, (me ^ k) * plan.owned, plan.owned, axis=0)  0.88 us
  transfers between devices with their start and end apart: 14, of which 13 were waited for; matrix products, arithmetic and copies ran while one was open for 0% of the time, Pallas kernels for 1%

profile of v2, /device:TPU:0, one launch (start us, length us, event | category | flops | bytes accessed | tf_op | source)
XLA Modules:
  0.0 42.9 jit_solution(17041092071417331564)
XLA Ops:
  0.6 0.0 copy-start.1
  0.7 0.9 %constant_dynamic-slice_fusion = (bf16[1,32,512]{2,1,0:T(8,128)(2,1)S(1)}, bf16[1,32,512]{2,1,0:T(8,128)(2,1)S(1)}, bf16[1,32,512]{2,1,0:T(8,128)(2,1)S(1)}, bf16[1,32,512]{2,1,0:T(8,128)(2,1)S(1)}) fusion(bf16[4,32,512]{2,1,0:T(8,128)(2,1)} %param.6, s32[]{:T(128)S(6)} %select_n.15, s32[]{:T(128)S(6)} %select_n.13, s32[]{:T(128)S(6)} %select_n.12, s32[]{:T(128)S(6)} %select_n.14), kind=kLoop, calls=%fused_computation | loop fusion | bytes 262160 | tf_op jit(solution)/shard_map/dynamic_slice | solution.py:354
  1.5 5.1 %collective-permute-start.2 = (bf16[1,32,512]{2,1,0:T(8,128)(2,1)S(1)}, bf16[1,32,512]{2,1,0:T(8,128)(2,1)S(1)}, u32[]{:S(2)}, u32[]{:S(2)}) collective-permute-start(bf16[1,32,512]{2,1,0:T(8,128)(2,1)S(1)} %get-tuple-element.37), channel_id=1, source_target_pairs={{0,3},{1,2},{2,1},{3,0},{4,7},{5,6},{6,5},{7,4},{8,11},{9,10},{10,... | collective-permute-start | bytes 98312 | tf_op jit(solution)/shard_map/ppermute | solution.py:345
  6.7 0.0 collective-permute-start
  6.7 0.6 %collective-permute-start.1 = (bf16[1,32,512]{2,1,0:T(8,128)(2,1)S(1)}, bf16[1,32,512]{2,1,0:T(8,128)(2,1)S(1)}, u32[]{:S(2)}, u32[]{:S(2)}) collective-permute-start(bf16[1,32,512]{2,1,0:T(8,128)(2,1)S(1)} %get-tuple-element.40), channel_id=1, source_target_pairs={{0,2},{1,3},{2,0},{3,1},{4,6},{5,7},{6,4},{7,5},{8,10},{9,11},{10,... | collective-permute-start | bytes 98312 | tf_op jit(solution)/shard_map/ppermute | solution.py:345
  7.3 0.0 copy-start.3
  7.3 0.0 copy-start.4
  7.3 0.0 copy-done.1
  7.3 0.6 %copy-done.3 = f32[64]{0:T(128)S(1)} copy-done((f32[64]{0:T(128)S(1)}, f32[64]{0:T(128)}, u32[]{:S(2)}) %copy-start.3) | copy-done | bytes 280
  8.0 0.0 copy-done.4
  8.0 0.0 copy-start
  8.0 1.0 %copy-done = bf16[27,128,64]{1,2,0:T(8,128)(2,1)S(1)} copy-done((bf16[27,128,64]{1,2,0:T(8,128)(2,1)S(1)}, bf16[27,128,64]{1,2,0:T(8,128)(2,1)}, u32[]{:S(2)}) %copy-start) | copy-done | bytes 442392
  9.0 0.0 copy-start.2
  9.0 0.4 weights.1
  9.4 0.0 collective-permute-done.2.refs_3_
  9.4 1.1 %collective-permute-done.refs_1_ = bf16[1,32,512]{2,1,0:T(8,128)(2,1)S(1)} collective-permute-done((bf16[1,32,512]{2,1,0:T(8,128)(2,1)S(1)}, bf16[1,32,512]{2,1,0:T(8,128)(2,1)S(1)}, u32[]{:S(2)}, u32[]{:S(2)}) %collective-permute-start) | collective-permute-done | bytes 32800 | tf_op jit(solution)/shard_map/ppermute | solution.py:345
  10.6 1.0 %collective-permute-done.1.refs_2_ = bf16[1,32,512]{2,1,0:T(8,128)(2,1)S(1)} collective-permute-done((bf16[1,32,512]{2,1,0:T(8,128)(2,1)S(1)}, bf16[1,32,512]{2,1,0:T(8,128)(2,1)S(1)}, u32[]{:S(2)}, u32[]{:S(2)}) %collective-permute-start.1) | collective-permute-done | bytes 32800 | tf_op jit(solution)/shard_map/ppermute | solution.py:345
  11.6 0.0 copy-done.2
  11.6 3.3 %main.1 = (bf16[1,128,256]{2,1,0:T(8,128)(2,1)}, f32[1088,128]{1,0:T(8,128)S(1)}, bf16[1088,128]{1,0:T(8,128)(2,1)S(1)}) custom-call(bf16[1,32,512]{2,1,0:T(8,128)(2,1)S(1)} %get-tuple-element.39.refs_0_, bf16[1,32,512]{2,1,0:T(8,128)(2,1)S(1)} %collective-permute-done.refs_1_, bf16[1,32,512]{2,1,0:T(8,128)(2,1)S(1)} %collective-permute-done.1.refs_2_, ...), custom_call_target="tpu_custom_call" | custom-call | tf_op jit(solution)/shard_map/main/pallas_call | solution.py:333
  14.9 0.1 collective-permute-start.3
  15.0 1.5 %collective-permute-done.3.got_ref = bf16[1088,128]{1,0:T(8,128)(2,1)S(1)} collective-permute-done((bf16[1088,128]{1,0:T(8,128)(2,1)S(1)}, bf16[1088,128]{1,0:T(8,128)(2,1)S(1)}, u32[]{:S(2)}, u32[]{:S(2)}) %collective-permute-start.3) | collective-permute-done | bytes 278560 | tf_op jit(solution)/shard_map/ppermute | solution.py:345
  16.5 0.1 core_sum.1
  16.6 1.6 %collective-permute-start.4 = (bf16[272,128]{1,0:T(8,128)(2,1)S(1)}, bf16[272,128]{1,0:T(8,128)(2,1)S(1)}, u32[]{:S(2)}, u32[]{:S(2)}) collective-permute-start(bf16[272,128]{1,0:T(8,128)(2,1)S(1)} %get-tuple-element.30), channel_id=1, source_target_pairs={{0,8},{4,12},{8,0},{12,4},{16,24},{20,28},{24,16},{28,20},{1,9},{5... | collective-permute-start | bytes 208904 | tf_op jit(solution)/shard_map/ppermute | solution.py:345
  18.2 1.5 %collective-permute-start.5 = (bf16[272,128]{1,0:T(8,128)(2,1)S(1)}, bf16[272,128]{1,0:T(8,128)(2,1)S(1)}, u32[]{:S(2)}, u32[]{:S(2)}) collective-permute-start(bf16[272,128]{1,0:T(8,128)(2,1)S(1)} %get-tuple-element.31), channel_id=1, source_target_pairs={{0,16},{4,20},{8,24},{12,28},{16,0},{20,4},{24,8},{28,12},{1,17},{... | collective-permute-start | bytes 208904 | tf_op jit(solution)/shard_map/ppermute | solution.py:345
  19.7 0.5 %collective-permute-start.6 = (bf16[272,128]{1,0:T(8,128)(2,1)S(1)}, bf16[272,128]{1,0:T(8,128)(2,1)S(1)}, u32[]{:S(2)}, u32[]{:S(2)}) collective-permute-start(bf16[272,128]{1,0:T(8,128)(2,1)S(1)} %get-tuple-element.32), channel_id=1, source_target_pairs={{0,24},{4,28},{8,16},{12,20},{16,8},{20,12},{24,0},{28,4},{1,25},{... | collective-permute-start | bytes 208904 | tf_op jit(solution)/shard_map/ppermute | solution.py:345
  20.2 0.8 %collective-permute-done.4.rest_0_ = bf16[272,128]{1,0:T(8,128)(2,1)S(1)} collective-permute-done((bf16[272,128]{1,0:T(8,128)(2,1)S(1)}, bf16[272,128]{1,0:T(8,128)(2,1)S(1)}, u32[]{:S(2)}, u32[]{:S(2)}) %collective-permute-start.4) | collective-permute-done | bytes 69664 | tf_op jit(solution)/shard_map/ppermute | solution.py:345
  21.0 1.5 %collective-permute-done.5.rest_1_ = bf16[272,128]{1,0:T(8,128)(2,1)S(1)} collective-permute-done((bf16[272,128]{1,0:T(8,128)(2,1)S(1)}, bf16[272,128]{1,0:T(8,128)(2,1)S(1)}, u32[]{:S(2)}, u32[]{:S(2)}) %collective-permute-start.5) | collective-permute-done | bytes 69664 | tf_op jit(solution)/shard_map/ppermute | solution.py:345
  22.5 2.4 %collective-permute-done.6.rest_2_ = bf16[272,128]{1,0:T(8,128)(2,1)S(1)} collective-permute-done((bf16[272,128]{1,0:T(8,128)(2,1)S(1)}, bf16[272,128]{1,0:T(8,128)(2,1)S(1)}, u32[]{:S(2)}, u32[]{:S(2)}) %collective-permute-start.6) | collective-permute-done | bytes 69664 | tf_op jit(solution)/shard_map/ppermute | solution.py:345
  25.0 2.0 %collective-permute-start.9 = (bf16[272,128]{1,0:T(8,128)(2,1)S(1)}, bf16[272,128]{1,0:T(8,128)(2,1)S(1)}, u32[]{:S(2)}, u32[]{:S(2)}) collective-permute-start(bf16[272,128]{1,0:T(8,128)(2,1)S(1)} %group_sum.1.refs_0_), channel_id=1, source_target_pairs={{0,3},{1,2},{2,1},{3,0},{4,7},{5,6},{6,5},{7,4},{8,11},{9,10},{10,... | collective-permute-start | bytes 208904 | tf_op jit(solution)/shard_map/ppermute | solution.py:345
  27.0 1.4 %collective-permute-start.8 = (bf16[272,128]{1,0:T(8,128)(2,1)S(1)}, bf16[272,128]{1,0:T(8,128)(2,1)S(1)}, u32[]{:S(2)}, u32[]{:S(2)}) collective-permute-start(bf16[272,128]{1,0:T(8,128)(2,1)S(1)} %group_sum.1.refs_0_), channel_id=1, source_target_pairs={{0,2},{1,3},{2,0},{3,1},{4,6},{5,7},{6,4},{7,5},{8,10},{9,11},{10,... | collective-permute-start | bytes 208904 | tf_op jit(solution)/shard_map/ppermute | solution.py:345
  28.4 1.0 %collective-permute-start.7 = (bf16[272,128]{1,0:T(8,128)(2,1)S(1)}, bf16[272,128]{1,0:T(8,128)(2,1)S(1)}, u32[]{:S(2)}, u32[]{:S(2)}) collective-permute-start(bf16[272,128]{1,0:T(8,128)(2,1)S(1)} %group_sum.1.refs_0_), channel_id=1, source_target_pairs={{0,1},{1,0},{2,3},{3,2},{4,5},{5,4},{6,7},{7,6},{8,9},{9,8},{10,11... | collective-permute-start | bytes 208904 | tf_op jit(solution)/shard_map/ppermute | solution.py:345
  29.4 1.9 %collective-permute-done.9.refs_3_ = bf16[272,128]{1,0:T(8,128)(2,1)S(1)} collective-permute-done((bf16[272,128]{1,0:T(8,128)(2,1)S(1)}, bf16[272,128]{1,0:T(8,128)(2,1)S(1)}, u32[]{:S(2)}, u32[]{:S(2)}) %collective-permute-start.9) | collective-permute-done | bytes 69664 | tf_op jit(solution)/shard_map/ppermute | solution.py:345
  31.3 2.2 %collective-permute-done.8.refs_2_ = bf16[272,128]{1,0:T(8,128)(2,1)S(1)} collective-permute-done((bf16[272,128]{1,0:T(8,128)(2,1)S(1)}, bf16[272,128]{1,0:T(8,128)(2,1)S(1)}, u32[]{:S(2)}, u32[]{:S(2)}) %collective-permute-start.8) | collective-permute-done | bytes 69664 | tf_op jit(solution)/shard_map/ppermute | solution.py:345
  33.5 0.1 collective-permute-done.7.refs_1_
  33.6 0.7 %collective-permute-start.12 = (bf16[272,128]{1,0:T(8,128)(2,1)S(1)}, bf16[272,128]{1,0:T(8,128)(2,1)S(1)}, u32[]{:S(2)}, u32[]{:S(2)}) collective-permute-start(bf16[272,128]{1,0:T(8,128)(2,1)S(1)} %space_sum.1.refs_0_), channel_id=1, source_target_pairs={{0,24},{4,28},{8,16},{12,20},{16,8},{20,12},{24,0},{28,4},{1,25},{... | collective-permute-start | bytes 208904 | tf_op jit(solution)/shard_map/ppermute | solution.py:345
  34.3 1.4 %collective-permute-start.11 = (bf16[272,128]{1,0:T(8,128)(2,1)S(1)}, bf16[272,128]{1,0:T(8,128)(2,1)S(1)}, u32[]{:S(2)}, u32[]{:S(2)}) collective-permute-start(bf16[272,128]{1,0:T(8,128)(2,1)S(1)} %space_sum.1.refs_0_), channel_id=1, source_target_pairs={{0,16},{4,20},{8,24},{12,28},{16,0},{20,4},{24,8},{28,12},{1,17},{... | collective-permute-start | bytes 208904 | tf_op jit(solution)/shard_map/ppermute | solution.py:345
  35.7 1.4 %collective-permute-start.10 = (bf16[272,128]{1,0:T(8,128)(2,1)S(1)}, bf16[272,128]{1,0:T(8,128)(2,1)S(1)}, u32[]{:S(2)}, u32[]{:S(2)}) collective-permute-start(bf16[272,128]{1,0:T(8,128)(2,1)S(1)} %space_sum.1.refs_0_), channel_id=1, source_target_pairs={{0,8},{4,12},{8,0},{12,4},{16,24},{20,28},{24,16},{28,20},{1,9},{5... | collective-permute-start | bytes 208904 | tf_op jit(solution)/shard_map/ppermute | solution.py:345
  37.1 1.8 %collective-permute-done.12.refs_3_ = bf16[272,128]{1,0:T(8,128)(2,1)S(1)} collective-permute-done((bf16[272,128]{1,0:T(8,128)(2,1)S(1)}, bf16[272,128]{1,0:T(8,128)(2,1)S(1)}, u32[]{:S(2)}, u32[]{:S(2)}) %collective-permute-start.12) | collective-permute-done | bytes 69664 | tf_op jit(solution)/shard_map/ppermute | solution.py:345
  39.0 0.4 collective-permute-done.11.refs_2_
  39.3 0.7 %collective-permute-done.10.refs_1_ = bf16[272,128]{1,0:T(8,128)(2,1)S(1)} collective-permute-done((bf16[272,128]{1,0:T(8,128)(2,1)S(1)}, bf16[272,128]{1,0:T(8,128)(2,1)S(1)}, u32[]{:S(2)}, u32[]{:S(2)}) %collective-permute-start.10) | collective-permute-done | bytes 69664 | tf_op jit(solution)/shard_map/ppermute | solution.py:345
  40.1 0.1 collective-permute-start.13
  40.1 1.5 %collective-permute-done.13.other_ref = bf16[1088,128]{1,0:T(8,128)(2,1)S(1)} collective-permute-done((bf16[1088,128]{1,0:T(8,128)(2,1)S(1)}, bf16[1088,128]{1,0:T(8,128)(2,1)S(1)}, u32[]{:S(2)}, u32[]{:S(2)}) %collective-permute-start.13) | collective-permute-done | bytes 278560 | tf_op jit(solution)/shard_map/ppermute | solution.py:345
  41.7 1.2 %unpack.1 = (f32[27,32,64]{2,1,0:T(8,128)}, f32[1,64]{1,0:T(1,128)}, f32[27,64,128]{2,1,0:T(8,128)}, f32[1,128]{1,0:T(1,128)}) custom-call(bf16[1088,128]{1,0:T(8,128)(2,1)S(1)} %gather.1.mine_ref, bf16[1088,128]{1,0:T(8,128)(2,1)S(1)} %collective-permute-done.13.other_ref), custom_call_target="tpu_custom_call" | custom-call | tf_op jit(solution)/shard_map/unpack/pallas_call | solution.py:333
  (3 shorter events, 0.1 us)
Async XLA Ops:
  0.6 6.7 %copy-start.1 = (bf16[27,64,32]{1,2,0:T(8,128)(2,1)S(1)}, bf16[27,64,32]{1,2,0:T(8,128)(2,1)}, u32[]{:S(2)}) copy-start(bf16[27,64,32]{1,2,0:T(8,128)(2,1)} %param.8) | copy-start | bytes 331780
  1.5 7.9 %collective-permute-start.2 = (bf16[1,32,512]{2,1,0:T(8,128)(2,1)S(1)}, bf16[1,32,512]{2,1,0:T(8,128)(2,1)S(1)}, u32[]{:S(2)}, u32[]{:S(2)}) collective-permute-start(bf16[1,32,512]{2,1,0:T(8,128)(2,1)S(1)} %get-tuple-element.37), channel_id=1, source_target_pairs={{0,3},{1,2},{2,1},{3,0},{4,7},{5,6},{6,5},{7,4},{8,11},{9,10},{10,... | collective-permute-start | bytes 98312 | tf_op jit(solution)/shard_map/ppermute | solution.py:345
  6.7 3.9 %collective-permute-start = (bf16[1,32,512]{2,1,0:T(8,128)(2,1)S(1)}, bf16[1,32,512]{2,1,0:T(8,128)(2,1)S(1)}, u32[]{:S(2)}, u32[]{:S(2)}) collective-permute-start(bf16[1,32,512]{2,1,0:T(8,128)(2,1)S(1)} %get-tuple-element.38), channel_id=1, source_target_pairs={{0,1},{1,0},{2,3},{3,2},{4,5},{5,4},{6,7},{7,6},{8,9},{9,8},{10,11... | collective-permute-start | bytes 98312 | tf_op jit(solution)/shard_map/ppermute | solution.py:345
  6.7 4.9 %collective-permute-start.1 = (bf16[1,32,512]{2,1,0:T(8,128)(2,1)S(1)}, bf16[1,32,512]{2,1,0:T(8,128)(2,1)S(1)}, u32[]{:S(2)}, u32[]{:S(2)}) collective-permute-start(bf16[1,32,512]{2,1,0:T(8,128)(2,1)S(1)} %get-tuple-element.40), channel_id=1, source_target_pairs={{0,2},{1,3},{2,0},{3,1},{4,6},{5,7},{6,4},{7,5},{8,10},{9,11},{10,... | collective-permute-start | bytes 98312 | tf_op jit(solution)/shard_map/ppermute | solution.py:345
  7.3 0.7 %copy-start.3 = (f32[64]{0:T(128)S(1)}, f32[64]{0:T(128)}, u32[]{:S(2)}) copy-start(f32[64]{0:T(128)} %param.9) | copy-start | bytes 772
  7.3 0.7 %copy-start.4 = (f32[128]{0:T(128)S(1)}, f32[128]{0:T(128)}, u32[]{:S(2)}) copy-start(f32[128]{0:T(128)} %param.11) | copy-start | bytes 1540
  8.0 1.0 %copy-start = (bf16[27,128,64]{1,2,0:T(8,128)(2,1)S(1)}, bf16[27,128,64]{1,2,0:T(8,128)(2,1)}, u32[]{:S(2)}) copy-start(bf16[27,128,64]{1,2,0:T(8,128)(2,1)} %param.10) | copy-start | bytes 1327108
  9.0 2.6 %copy-start.2 = (bf16[1,128,256]{2,1,0:T(8,128)(2,1)S(1)}, bf16[1,128,256]{2,1,0:T(8,128)(2,1)}, u32[]{:S(2)}) copy-start(bf16[1,128,256]{2,1,0:T(8,128)(2,1)} %refs_4_.1) | copy-start | bytes 196612
  14.9 1.6 %collective-permute-start.3 = (bf16[1088,128]{1,0:T(8,128)(2,1)S(1)}, bf16[1088,128]{1,0:T(8,128)(2,1)S(1)}, u32[]{:S(2)}, u32[]{:S(2)}) collective-permute-start(bf16[1088,128]{1,0:T(8,128)(2,1)S(1)} %get-tuple-element.28), channel_id=1, source_target_pairs={{0,4},{4,0},{8,12},{12,8},{16,20},{20,16},{24,28},{28,24},{1,5},{5... | collective-permute-start | bytes 835592 | tf_op jit(solution)/shard_map/ppermute | solution.py:345
  16.6 4.4 %collective-permute-start.4 = (bf16[272,128]{1,0:T(8,128)(2,1)S(1)}, bf16[272,128]{1,0:T(8,128)(2,1)S(1)}, u32[]{:S(2)}, u32[]{:S(2)}) collective-permute-start(bf16[272,128]{1,0:T(8,128)(2,1)S(1)} %get-tuple-element.30), channel_id=1, source_target_pairs={{0,8},{4,12},{8,0},{12,4},{16,24},{20,28},{24,16},{28,20},{1,9},{5... | collective-permute-start | bytes 208904 | tf_op jit(solution)/shard_map/ppermute | solution.py:345
  18.2 4.3 %collective-permute-start.5 = (bf16[272,128]{1,0:T(8,128)(2,1)S(1)}, bf16[272,128]{1,0:T(8,128)(2,1)S(1)}, u32[]{:S(2)}, u32[]{:S(2)}) collective-permute-start(bf16[272,128]{1,0:T(8,128)(2,1)S(1)} %get-tuple-element.31), channel_id=1, source_target_pairs={{0,16},{4,20},{8,24},{12,28},{16,0},{20,4},{24,8},{28,12},{1,17},{... | collective-permute-start | bytes 208904 | tf_op jit(solution)/shard_map/ppermute | solution.py:345
  19.7 5.2 %collective-permute-start.6 = (bf16[272,128]{1,0:T(8,128)(2,1)S(1)}, bf16[272,128]{1,0:T(8,128)(2,1)S(1)}, u32[]{:S(2)}, u32[]{:S(2)}) collective-permute-start(bf16[272,128]{1,0:T(8,128)(2,1)S(1)} %get-tuple-element.32), channel_id=1, source_target_pairs={{0,24},{4,28},{8,16},{12,20},{16,8},{20,12},{24,0},{28,4},{1,25},{... | collective-permute-start | bytes 208904 | tf_op jit(solution)/shard_map/ppermute | solution.py:345
  25.0 6.3 %collective-permute-start.9 = (bf16[272,128]{1,0:T(8,128)(2,1)S(1)}, bf16[272,128]{1,0:T(8,128)(2,1)S(1)}, u32[]{:S(2)}, u32[]{:S(2)}) collective-permute-start(bf16[272,128]{1,0:T(8,128)(2,1)S(1)} %group_sum.1.refs_0_), channel_id=1, source_target_pairs={{0,3},{1,2},{2,1},{3,0},{4,7},{5,6},{6,5},{7,4},{8,11},{9,10},{10,... | collective-permute-start | bytes 208904 | tf_op jit(solution)/shard_map/ppermute | solution.py:345
  27.0 6.5 %collective-permute-start.8 = (bf16[272,128]{1,0:T(8,128)(2,1)S(1)}, bf16[272,128]{1,0:T(8,128)(2,1)S(1)}, u32[]{:S(2)}, u32[]{:S(2)}) collective-permute-start(bf16[272,128]{1,0:T(8,128)(2,1)S(1)} %group_sum.1.refs_0_), channel_id=1, source_target_pairs={{0,2},{1,3},{2,0},{3,1},{4,6},{5,7},{6,4},{7,5},{8,10},{9,11},{10,... | collective-permute-start | bytes 208904 | tf_op jit(solution)/shard_map/ppermute | solution.py:345
  28.4 5.1 %collective-permute-start.7 = (bf16[272,128]{1,0:T(8,128)(2,1)S(1)}, bf16[272,128]{1,0:T(8,128)(2,1)S(1)}, u32[]{:S(2)}, u32[]{:S(2)}) collective-permute-start(bf16[272,128]{1,0:T(8,128)(2,1)S(1)} %group_sum.1.refs_0_), channel_id=1, source_target_pairs={{0,1},{1,0},{2,3},{3,2},{4,5},{5,4},{6,7},{7,6},{8,9},{9,8},{10,11... | collective-permute-start | bytes 208904 | tf_op jit(solution)/shard_map/ppermute | solution.py:345
  33.6 5.4 %collective-permute-start.12 = (bf16[272,128]{1,0:T(8,128)(2,1)S(1)}, bf16[272,128]{1,0:T(8,128)(2,1)S(1)}, u32[]{:S(2)}, u32[]{:S(2)}) collective-permute-start(bf16[272,128]{1,0:T(8,128)(2,1)S(1)} %space_sum.1.refs_0_), channel_id=1, source_target_pairs={{0,24},{4,28},{8,16},{12,20},{16,8},{20,12},{24,0},{28,4},{1,25},{... | collective-permute-start | bytes 208904 | tf_op jit(solution)/shard_map/ppermute | solution.py:345
  34.3 5.1 %collective-permute-start.11 = (bf16[272,128]{1,0:T(8,128)(2,1)S(1)}, bf16[272,128]{1,0:T(8,128)(2,1)S(1)}, u32[]{:S(2)}, u32[]{:S(2)}) collective-permute-start(bf16[272,128]{1,0:T(8,128)(2,1)S(1)} %space_sum.1.refs_0_), channel_id=1, source_target_pairs={{0,16},{4,20},{8,24},{12,28},{16,0},{20,4},{24,8},{28,12},{1,17},{... | collective-permute-start | bytes 208904 | tf_op jit(solution)/shard_map/ppermute | solution.py:345
  35.7 4.3 %collective-permute-start.10 = (bf16[272,128]{1,0:T(8,128)(2,1)S(1)}, bf16[272,128]{1,0:T(8,128)(2,1)S(1)}, u32[]{:S(2)}, u32[]{:S(2)}) collective-permute-start(bf16[272,128]{1,0:T(8,128)(2,1)S(1)} %space_sum.1.refs_0_), channel_id=1, source_target_pairs={{0,8},{4,12},{8,0},{12,4},{16,24},{20,28},{24,16},{28,20},{1,9},{5... | collective-permute-start | bytes 208904 | tf_op jit(solution)/shard_map/ppermute | solution.py:345
  40.1 1.6 %collective-permute-start.13 = (bf16[1088,128]{1,0:T(8,128)(2,1)S(1)}, bf16[1088,128]{1,0:T(8,128)(2,1)S(1)}, u32[]{:S(2)}, u32[]{:S(2)}) collective-permute-start(bf16[1088,128]{1,0:T(8,128)(2,1)S(1)} %gather.1.mine_ref), channel_id=1, source_target_pairs={{0,4},{4,0},{8,12},{12,8},{16,20},{20,16},{24,28},{28,24},{1,5},{5... | collective-permute-start | bytes 835592 | tf_op jit(solution)/shard_map/ppermute | solution.py:345

commit v3 on v2

--- a/solution.py
+++ b/solution.py
@@ -110,20 +110,21 @@
     parent = (lanes % plane // side // 2) * small + lanes % side // 2
 
     for volume in range(plan.owned):
-        for k, part in enumerate(parts):
+        for k, part in zip(reversed(range(plan.space)), parts):
             start = (place ^ k) * plan.part_blocks
             for j in range(plan.part_blocks):
                 x_ref[start + j] = part[volume, :, j * LANES : (j + 1) * LANES]
 
-        for tap in range(9):
-            valid, shift = in_plane(side, tap)
-            for j in range(blocks):
-                block = x_ref[j]
-                if shift:
-                    block = jnp.where(valid, turn(block, shift), jnp.zeros_like(block))
-                s_one[tap * inner : (tap + 1) * inner, j * LANES : (j + 1) * LANES] = block
-
-        t_one[...] = dot(conv_one_ref[...], s_one[: 9 * inner, :])
+        for first_block in range(0, blocks, plan.part_blocks):
+            for tap in range(9):
+                valid, shift = in_plane(side, tap)
+                for j in range(first_block, first_block + plan.part_blocks):
+                    block = x_ref[j]
+                    if shift:
+                        block = jnp.where(valid, turn(block, shift), jnp.zeros_like(block))
+                    s_one[tap * inner : (tap + 1) * inner, j * LANES : (j + 1) * LANES] = block
+            here = slice(first_block * LANES, (first_block + plan.part_blocks) * LANES)
+            t_one[:, here] = dot(conv_one_ref[...], s_one[: 9 * inner, here])
 
         upper = lane >= plane
         for j in range(blocks):
@@ -284,19 +285,14 @@
     out_ref[rows - ROWS :, :] = split_again(total[rows - ROWS :], plan, last_chunk(plan)).astype(BF16)
 
 
-def gather_kernel(plan, *refs):
-    chunks, out_ref = refs[:-1], refs[-1]
-    group = lax.axis_index("sample") // plan.cores
-    for k, ref in enumerate(chunks):
-        out_ref[pl.ds(pl.multiple_of((group ^ k) * plan.chunk, ROWS), plan.chunk), :] = ref[...]
-
-
-def unpack_kernel(plan, mine_ref, other_ref, one_ref, bias_one_ref, two_ref, bias_two_ref, all_ref):
+def unpack_kernel(plan, *refs):
+    one_ref, bias_one_ref, two_ref, bias_two_ref, all_ref = refs[-5:]
     inner, mid, out = plan.inner, plan.mid, plan.out
-    core = lax.axis_index("sample") % plan.cores
-    share = plan.total // plan.cores
-    all_ref[pl.ds(pl.multiple_of(core * share, ROWS), share), :] = mine_ref[...].astype(F32)
-    all_ref[pl.ds(pl.multiple_of((1 - core) * share, ROWS), share), :] = other_ref[...].astype(F32)
+    group, core = lax.axis_index("sample") // plan.cores, lax.axis_index("sample") % plan.cores
+    for k, ref in enumerate(refs[:-5]):
+        side, k = k // plan.groups, k % plan.groups
+        start = ((core ^ side) * plan.groups + (group ^ k)) * plan.chunk
+        all_ref[pl.ds(pl.multiple_of(start, ROWS), plan.chunk), :] = ref[...].astype(F32)
     total, first = 27 * mid, 9 * inner
     two_ref[...] = all_ref[:total, :].reshape(27, mid, out)
     pair = all_ref[total : total + first, :]
@@ -376,7 +372,7 @@
         plan,
         "main",
         (((plan.owned, out, small), BF16), ((share, LANES), F32), ((share, LANES), BF16)),
-        *parts,
+        *reversed(parts),
         grad_out,
         *weights,
         scratch=scratch,
@@ -386,19 +382,19 @@
     got = swap(send, "sample", 1)
     own, *sends = call(core_sum_kernel, plan, "core_sum", ((chunk, F32),) + ((chunk, BF16),) * (plan.groups - 1), keep, got, scratch=(((share, LANES), F32),))
     gots = [swap(s, "sample", plan.cores * k) for k, s in enumerate(sends, start=1)]
-    (partial,) = call(group_sum_kernel, plan, "group_sum", ((chunk, BF16),), own, *gots)
-    gots = [swap(partial, "space", k) for k in range(1, plan.space)]
+    (partial,) = call(group_sum_kernel, plan, "group_sum", ((chunk, BF16),), own, *gots[1:], gots[0])
+    gots = [swap(partial, "space", k ^ (k >> 1)) for k in range(1, plan.space)]
     (whole,) = call(space_sum_kernel, plan, "space_sum", ((chunk, BF16),), partial, *gots)
     gots = [swap(whole, "sample", plan.cores * k) for k in range(1, plan.groups)]
-    (mine,) = call(gather_kernel, plan, "gather", (((share, LANES), BF16),), whole, *gots)
-    other = swap(mine, "sample", 1)
+    mine = [whole, *gots]
+    other = [swap(value, "sample", 1) for value in mine]
     one, bias_one, two, bias_two = call(
         unpack_kernel,
         plan,
         "unpack",
         (((27, inner, mid), F32), ((1, mid), F32), ((27, mid, out), F32), ((1, out), F32)),
-        mine,
-        other,
+        *mine,
+        *other,
         scratch=(((plan.total, LANES), F32),),
     )
     return (features, jnp.swapaxes(one, 1, 2), bias_one.reshape(mid), jnp.swapaxes(two, 1, 2), bias_two.reshape(out))

time: 43.1 us -> 41.3 us (0.958)
  waiting for transfers between devices: 17 us -> 16 us
  starting transfers between devices: 17.5 us -> 16.7 us
    ppermute x14 -> x17, waiting for transfers between devices: 17 us -> 16 us  [swap(): lax.ppermute(value, axis, [(i, i ^ k) for i in range(lax.axis_size(axis))])]
    ppermute x14 -> x17, starting transfers between devices: 17.5 us -> 16.7 us  [swap(): lax.ppermute(value, axis, [(i, i ^ k) for i in range(lax.axis_size(axis))])]
    pallas_call x6 -> x5, Pallas kernels: 4.76 us -> 4.71 us  [call(): pl.pallas_call(functools.partial(kernel, plan), out_shape=[jax.ShapeDtype...]
  transfers between devices with their start and end apart: 14 -> 17, of which waited for: 13 -> 11; matrix products, arithmetic and copies ran while one was open for 0% -> 0% of each run, Pallas kernels for 1% -> 1%
where the time goes in v3:
time: 41.3 us; the launch traced here: 41.1 us
  starting transfers between devices  16.7 us (40%)
  waiting for transfers between devices  16 us (39%)
  Pallas kernels  5.14 us (12%)
  local copies, waits for them, and re-layouts  2.57 us (6%)
  between operations  0.71 us (2%)
    ppermute x17, starting transfers between devices, swap(): lax.ppermute(value, axis, [(i, i ^ k) for i in range(lax.axis_size(axis))])  16.7 us
    ppermute x17, waiting for transfers between devices, swap(): lax.ppermute(value, axis, [(i, i ^ k) for i in range(lax.axis_size(axis))])  16 us
    pallas_call x5, Pallas kernels, call(): pl.pallas_call(functools.partial(kernel, plan), out_shape=[jax.ShapeDtype...  4.71 us
    unnamed x10, local copies, waits for them, and re-layouts  1.69 us
    dynamic_slice x1, local copies, waits for them, and re-layouts, piece(): lax.dynamic_slice_in_dim(volumes, (me ^ k) * plan.owned, plan.owned, axis=0)  0.88 us
  transfers between devices with their start and end apart: 17, of which 11 were waited for; matrix products, arithmetic and copies ran while one was open for 0% of the time, Pallas kernels for 1%

profile of v3, /device:TPU:0, one launch (start us, length us, event | category | flops | bytes accessed | tf_op | source)
XLA Modules:
  0.0 41.1 jit_solution(9649391136505295674)
XLA Ops:
  0.6 0.0 copy-start.1
  0.7 0.9 %constant_dynamic-slice_fusion = (bf16[1,32,512]{2,1,0:T(8,128)(2,1)S(1)}, bf16[1,32,512]{2,1,0:T(8,128)(2,1)S(1)}, bf16[1,32,512]{2,1,0:T(8,128)(2,1)S(1)}, bf16[1,32,512]{2,1,0:T(8,128)(2,1)S(1)}) fusion(bf16[4,32,512]{2,1,0:T(8,128)(2,1)} %param.6, s32[]{:T(128)S(6)} %select_n.15, s32[]{:T(128)S(6)} %select_n.13, s32[]{:T(128)S(6)} %select_n.12, s32[]{:T(128)S(6)} %select_n.14), kind=kLoop, calls=%fused_computation | loop fusion | bytes 262160 | tf_op jit(solution)/shard_map/dynamic_slice | solution.py:350
  1.5 4.1 %collective-permute-start.1 = (bf16[1,32,512]{2,1,0:T(8,128)(2,1)S(1)}, bf16[1,32,512]{2,1,0:T(8,128)(2,1)S(1)}, u32[]{:S(2)}, u32[]{:S(2)}) collective-permute-start(bf16[1,32,512]{2,1,0:T(8,128)(2,1)S(1)} %get-tuple-element.38), channel_id=1, source_target_pairs={{0,2},{1,3},{2,0},{3,1},{4,6},{5,7},{6,4},{7,5},{8,10},{9,11},{10,... | collective-permute-start | bytes 98312 | tf_op jit(solution)/shard_map/ppermute | solution.py:341
  5.6 1.3 %collective-permute-start = (bf16[1,32,512]{2,1,0:T(8,128)(2,1)S(1)}, bf16[1,32,512]{2,1,0:T(8,128)(2,1)S(1)}, u32[]{:S(2)}, u32[]{:S(2)}) collective-permute-start(bf16[1,32,512]{2,1,0:T(8,128)(2,1)S(1)} %get-tuple-element.39), channel_id=1, source_target_pairs={{0,3},{1,2},{2,1},{3,0},{4,7},{5,6},{6,5},{7,4},{8,11},{9,10},{10,... | collective-permute-start | bytes 98312 | tf_op jit(solution)/shard_map/ppermute | solution.py:341
  7.0 0.2 collective-permute-start.2
  7.2 0.0 copy-start.3
  7.2 0.0 copy-start.4
  7.2 0.0 copy-done.1
  7.2 0.6 %copy-done.3 = f32[64]{0:T(128)S(1)} copy-done((f32[64]{0:T(128)S(1)}, f32[64]{0:T(128)}, u32[]{:S(2)}) %copy-start.3) | copy-done | bytes 280
  7.9 0.0 copy-done.4
  7.9 0.0 copy-start
  7.9 1.0 %copy-done = bf16[27,128,64]{1,2,0:T(8,128)(2,1)S(1)} copy-done((bf16[27,128,64]{1,2,0:T(8,128)(2,1)S(1)}, bf16[27,128,64]{1,2,0:T(8,128)(2,1)}, u32[]{:S(2)}) %copy-start) | copy-done | bytes 442392
  8.9 0.4 %weights.1 = (bf16[192,288]{1,0:T(8,128)(2,1)S(1)}, bf16[384,576]{1,0:T(8,128)(2,1)S(1)}, bf16[192,1152]{1,0:T(8,128)(2,1)S(1)}, f32[64,128]{1,0:T(8,128)S(1)}, f32[128,128]{1,0:T(8,128)S(1)}) custom-call(bf16[27,32,64]{2,1,0:T(8,128)(2,1)S(1)} %bitcast.9, bf16[27,64,128]{2,1,0:T(8,128)(2,1)S(1)} %bitcast.8, f32[1,64]{1,0:T(1,128)S(1)} %bitcast.10, ...), custom_call_target="tpu_custom_call" | custom-call | tf_op jit(solution)/shard_map/weights/pallas_call | solution.py:78
  9.3 0.0 collective-permute-done.1.refs_1_
  9.4 2.0 %collective-permute-done.refs_0_ = bf16[1,32,512]{2,1,0:T(8,128)(2,1)S(1)} collective-permute-done((bf16[1,32,512]{2,1,0:T(8,128)(2,1)S(1)}, bf16[1,32,512]{2,1,0:T(8,128)(2,1)S(1)}, u32[]{:S(2)}, u32[]{:S(2)}) %collective-permute-start) | collective-permute-done | bytes 32800 | tf_op jit(solution)/shard_map/ppermute | solution.py:341
  11.4 0.0 collective-permute-done.2.refs_2_
  11.4 0.0 copy-done.2
  11.4 3.3 %main.1 = (bf16[1,128,256]{2,1,0:T(8,128)(2,1)}, f32[1088,128]{1,0:T(8,128)S(1)}, bf16[1088,128]{1,0:T(8,128)(2,1)S(1)}) custom-call(bf16[1,32,512]{2,1,0:T(8,128)(2,1)S(1)} %collective-permute-done.refs_0_, bf16[1,32,512]{2,1,0:T(8,128)(2,1)S(1)} %collective-permute-done.1.refs_1_, bf16[1,32,512]{2,1,0:T(8,128)(2,1)S(1)} %collective-permute-done.2.refs_2_, ...), custom_call_target="tpu_custom_call" | custom-call | tf_op jit(solution)/shard_map/main/pallas_call | solution.py:329
  14.7 0.1 collective-permute-start.3
  14.8 1.5 %collective-permute-done.3.got_ref = bf16[1088,128]{1,0:T(8,128)(2,1)S(1)} collective-permute-done((bf16[1088,128]{1,0:T(8,128)(2,1)S(1)}, bf16[1088,128]{1,0:T(8,128)(2,1)S(1)}, u32[]{:S(2)}, u32[]{:S(2)}) %collective-permute-start.3) | collective-permute-done | bytes 278560 | tf_op jit(solution)/shard_map/ppermute | solution.py:341
  16.3 0.1 core_sum.1
  16.4 1.6 %collective-permute-start.4 = (bf16[272,128]{1,0:T(8,128)(2,1)S(1)}, bf16[272,128]{1,0:T(8,128)(2,1)S(1)}, u32[]{:S(2)}, u32[]{:S(2)}) collective-permute-start(bf16[272,128]{1,0:T(8,128)(2,1)S(1)} %get-tuple-element.30), channel_id=1, source_target_pairs={{0,16},{4,20},{8,24},{12,28},{16,0},{20,4},{24,8},{28,12},{1,17},{... | collective-permute-start | bytes 208904 | tf_op jit(solution)/shard_map/ppermute | solution.py:341
  18.0 1.4 %collective-permute-start.5 = (bf16[272,128]{1,0:T(8,128)(2,1)S(1)}, bf16[272,128]{1,0:T(8,128)(2,1)S(1)}, u32[]{:S(2)}, u32[]{:S(2)}) collective-permute-start(bf16[272,128]{1,0:T(8,128)(2,1)S(1)} %get-tuple-element.31), channel_id=1, source_target_pairs={{0,24},{4,28},{8,16},{12,20},{16,8},{20,12},{24,0},{28,4},{1,25},{... | collective-permute-start | bytes 208904 | tf_op jit(solution)/shard_map/ppermute | solution.py:341
  19.4 0.5 %collective-permute-start.6 = (bf16[272,128]{1,0:T(8,128)(2,1)S(1)}, bf16[272,128]{1,0:T(8,128)(2,1)S(1)}, u32[]{:S(2)}, u32[]{:S(2)}) collective-permute-start(bf16[272,128]{1,0:T(8,128)(2,1)S(1)} %get-tuple-element.32), channel_id=1, source_target_pairs={{0,8},{4,12},{8,0},{12,4},{16,24},{20,28},{24,16},{28,20},{1,9},{5... | collective-permute-start | bytes 208904 | tf_op jit(solution)/shard_map/ppermute | solution.py:341
  20.0 0.8 %collective-permute-done.4.rest_0_ = bf16[272,128]{1,0:T(8,128)(2,1)S(1)} collective-permute-done((bf16[272,128]{1,0:T(8,128)(2,1)S(1)}, bf16[272,128]{1,0:T(8,128)(2,1)S(1)}, u32[]{:S(2)}, u32[]{:S(2)}) %collective-permute-start.4) | collective-permute-done | bytes 69664 | tf_op jit(solution)/shard_map/ppermute | solution.py:341
  20.8 3.1 %collective-permute-done.5.rest_1_ = bf16[272,128]{1,0:T(8,128)(2,1)S(1)} collective-permute-done((bf16[272,128]{1,0:T(8,128)(2,1)S(1)}, bf16[272,128]{1,0:T(8,128)(2,1)S(1)}, u32[]{:S(2)}, u32[]{:S(2)}) %collective-permute-start.5) | collective-permute-done | bytes 69664 | tf_op jit(solution)/shard_map/ppermute | solution.py:341
  23.8 0.0 collective-permute-done.6.rest_2_
  23.9 1.3 %collective-permute-start.9 = (bf16[272,128]{1,0:T(8,128)(2,1)S(1)}, bf16[272,128]{1,0:T(8,128)(2,1)S(1)}, u32[]{:S(2)}, u32[]{:S(2)}) collective-permute-start(bf16[272,128]{1,0:T(8,128)(2,1)S(1)} %group_sum.1.refs_0_), channel_id=1, source_target_pairs={{0,2},{1,3},{2,0},{3,1},{4,6},{5,7},{6,4},{7,5},{8,10},{9,11},{10,... | collective-permute-start | bytes 208904 | tf_op jit(solution)/shard_map/ppermute | solution.py:341
  25.2 1.3 %collective-permute-start.8 = (bf16[272,128]{1,0:T(8,128)(2,1)S(1)}, bf16[272,128]{1,0:T(8,128)(2,1)S(1)}, u32[]{:S(2)}, u32[]{:S(2)}) collective-permute-start(bf16[272,128]{1,0:T(8,128)(2,1)S(1)} %group_sum.1.refs_0_), channel_id=1, source_target_pairs={{0,3},{1,2},{2,1},{3,0},{4,7},{5,6},{6,5},{7,4},{8,11},{9,10},{10,... | collective-permute-start | bytes 208904 | tf_op jit(solution)/shard_map/ppermute | solution.py:341
  26.5 0.9 %collective-permute-start.7 = (bf16[272,128]{1,0:T(8,128)(2,1)S(1)}, bf16[272,128]{1,0:T(8,128)(2,1)S(1)}, u32[]{:S(2)}, u32[]{:S(2)}) collective-permute-start(bf16[272,128]{1,0:T(8,128)(2,1)S(1)} %group_sum.1.refs_0_), channel_id=1, source_target_pairs={{0,1},{1,0},{2,3},{3,2},{4,5},{5,4},{6,7},{7,6},{8,9},{9,8},{10,11... | collective-permute-start | bytes 208904 | tf_op jit(solution)/shard_map/ppermute | solution.py:341
  27.4 4.2 %collective-permute-done.9.refs_3_ = bf16[272,128]{1,0:T(8,128)(2,1)S(1)} collective-permute-done((bf16[272,128]{1,0:T(8,128)(2,1)S(1)}, bf16[272,128]{1,0:T(8,128)(2,1)S(1)}, u32[]{:S(2)}, u32[]{:S(2)}) %collective-permute-start.9) | collective-permute-done | bytes 69664 | tf_op jit(solution)/shard_map/ppermute | solution.py:341
  31.6 0.0 collective-permute-done.8.refs_2_
  31.6 0.5 %collective-permute-done.7.refs_1_ = bf16[272,128]{1,0:T(8,128)(2,1)S(1)} collective-permute-done((bf16[272,128]{1,0:T(8,128)(2,1)S(1)}, bf16[272,128]{1,0:T(8,128)(2,1)S(1)}, u32[]{:S(2)}, u32[]{:S(2)}) %collective-permute-start.7) | collective-permute-done | bytes 69664 | tf_op jit(solution)/shard_map/ppermute | solution.py:341
  32.1 1.9 %collective-permute-start.12 = (bf16[272,128]{1,0:T(8,128)(2,1)S(1)}, bf16[272,128]{1,0:T(8,128)(2,1)S(1)}, u32[]{:S(2)}, u32[]{:S(2)}) collective-permute-start(bf16[272,128]{1,0:T(8,128)(2,1)S(1)} %space_sum.1.refs_0_), channel_id=1, source_target_pairs={{0,24},{4,28},{8,16},{12,20},{16,8},{20,12},{24,0},{28,4},{1,25},{... | collective-permute-start | bytes 208904 | tf_op jit(solution)/shard_map/ppermute | solution.py:341
  34.1 0.3 collective-permute-start.11
  34.3 1.4 %collective-permute-start.10 = (bf16[272,128]{1,0:T(8,128)(2,1)S(1)}, bf16[272,128]{1,0:T(8,128)(2,1)S(1)}, u32[]{:S(2)}, u32[]{:S(2)}) collective-permute-start(bf16[272,128]{1,0:T(8,128)(2,1)S(1)} %space_sum.1.refs_0_), channel_id=1, source_target_pairs={{0,8},{4,12},{8,0},{12,4},{16,24},{20,28},{24,16},{28,20},{1,9},{5... | collective-permute-start | bytes 208904 | tf_op jit(solution)/shard_map/ppermute | solution.py:341
  35.7 0.0 collective-permute-start.13
  35.7 1.7 %collective-permute-done.12.refs_3_ = bf16[272,128]{1,0:T(8,128)(2,1)S(1)} collective-permute-done((bf16[272,128]{1,0:T(8,128)(2,1)S(1)}, bf16[272,128]{1,0:T(8,128)(2,1)S(1)}, u32[]{:S(2)}, u32[]{:S(2)}) %collective-permute-start.12) | collective-permute-done | bytes 69664 | tf_op jit(solution)/shard_map/ppermute | solution.py:341
  37.4 0.0 collective-permute-start.16
  37.4 1.0 %collective-permute-done.11.refs_2_ = bf16[272,128]{1,0:T(8,128)(2,1)S(1)} collective-permute-done((bf16[272,128]{1,0:T(8,128)(2,1)S(1)}, bf16[272,128]{1,0:T(8,128)(2,1)S(1)}, u32[]{:S(2)}, u32[]{:S(2)}) %collective-permute-start.11) | collective-permute-done | bytes 69664 | tf_op jit(solution)/shard_map/ppermute | solution.py:341
  38.4 0.0 collective-permute-start.15
  38.4 0.3 collective-permute-done.10.refs_1_
  38.7 0.3 collective-permute-start.14
  38.9 0.0 collective-permute-done.13.refs_4_
  38.9 0.0 collective-permute-done.16.refs_7_
  38.9 0.7 %collective-permute-done.15.refs_6_ = bf16[272,128]{1,0:T(8,128)(2,1)S(1)} collective-permute-done((bf16[272,128]{1,0:T(8,128)(2,1)S(1)}, bf16[272,128]{1,0:T(8,128)(2,1)S(1)}, u32[]{:S(2)}, u32[]{:S(2)}) %collective-permute-start.15) | collective-permute-done | bytes 69664 | tf_op jit(solution)/shard_map/ppermute | solution.py:341
  39.7 0.3 collective-permute-done.14.refs_5_
  39.9 1.2 %unpack.1 = (f32[27,32,64]{2,1,0:T(8,128)}, f32[1,64]{1,0:T(1,128)}, f32[27,64,128]{2,1,0:T(8,128)}, f32[1,128]{1,0:T(1,128)}) custom-call(bf16[272,128]{1,0:T(8,128)(2,1)S(1)} %space_sum.1.refs_0_, bf16[272,128]{1,0:T(8,128)(2,1)S(1)} %collective-permute-done.10.refs_1_, bf16[272,128]{1,0:T(8,128)(2,1)S(1)} %collective-permute-done.11.refs_2_, ...), custom_call_target="tpu_custom_call" | custom-call | tf_op jit(solution)/shard_map/unpack/pallas_call | solution.py:329
  (3 shorter events, 0.1 us)
Async XLA Ops:
  0.6 6.6 %copy-start.1 = (bf16[27,64,32]{1,2,0:T(8,128)(2,1)S(1)}, bf16[27,64,32]{1,2,0:T(8,128)(2,1)}, u32[]{:S(2)}) copy-start(bf16[27,64,32]{1,2,0:T(8,128)(2,1)} %param.8) | copy-start | bytes 331780
  1.5 7.8 %collective-permute-start.1 = (bf16[1,32,512]{2,1,0:T(8,128)(2,1)S(1)}, bf16[1,32,512]{2,1,0:T(8,128)(2,1)S(1)}, u32[]{:S(2)}, u32[]{:S(2)}) collective-permute-start(bf16[1,32,512]{2,1,0:T(8,128)(2,1)S(1)} %get-tuple-element.38), channel_id=1, source_target_pairs={{0,2},{1,3},{2,0},{3,1},{4,6},{5,7},{6,4},{7,5},{8,10},{9,11},{10,... | collective-permute-start | bytes 98312 | tf_op jit(solution)/shard_map/ppermute | solution.py:341
  5.6 5.7 %collective-permute-start = (bf16[1,32,512]{2,1,0:T(8,128)(2,1)S(1)}, bf16[1,32,512]{2,1,0:T(8,128)(2,1)S(1)}, u32[]{:S(2)}, u32[]{:S(2)}) collective-permute-start(bf16[1,32,512]{2,1,0:T(8,128)(2,1)S(1)} %get-tuple-element.39), channel_id=1, source_target_pairs={{0,3},{1,2},{2,1},{3,0},{4,7},{5,6},{6,5},{7,4},{8,11},{9,10},{10,... | collective-permute-start | bytes 98312 | tf_op jit(solution)/shard_map/ppermute | solution.py:341
  7.0 4.4 %collective-permute-start.2 = (bf16[1,32,512]{2,1,0:T(8,128)(2,1)S(1)}, bf16[1,32,512]{2,1,0:T(8,128)(2,1)S(1)}, u32[]{:S(2)}, u32[]{:S(2)}) collective-permute-start(bf16[1,32,512]{2,1,0:T(8,128)(2,1)S(1)} %get-tuple-element.40), channel_id=1, source_target_pairs={{0,1},{1,0},{2,3},{3,2},{4,5},{5,4},{6,7},{7,6},{8,9},{9,8},{10,11... | collective-permute-start | bytes 98312 | tf_op jit(solution)/shard_map/ppermute | solution.py:341
  7.2 0.7 %copy-start.3 = (f32[64]{0:T(128)S(1)}, f32[64]{0:T(128)}, u32[]{:S(2)}) copy-start(f32[64]{0:T(128)} %param.9) | copy-start | bytes 772
  7.2 0.7 %copy-start.4 = (f32[128]{0:T(128)S(1)}, f32[128]{0:T(128)}, u32[]{:S(2)}) copy-start(f32[128]{0:T(128)} %param.11) | copy-start | bytes 1540
  7.9 1.0 %copy-start = (bf16[27,128,64]{1,2,0:T(8,128)(2,1)S(1)}, bf16[27,128,64]{1,2,0:T(8,128)(2,1)}, u32[]{:S(2)}) copy-start(bf16[27,128,64]{1,2,0:T(8,128)(2,1)} %param.10) | copy-start | bytes 1327108
  8.9 2.5 %copy-start.2 = (bf16[1,128,256]{2,1,0:T(8,128)(2,1)S(1)}, bf16[1,128,256]{2,1,0:T(8,128)(2,1)}, u32[]{:S(2)}) copy-start(bf16[1,128,256]{2,1,0:T(8,128)(2,1)} %refs_4_.1) | copy-start | bytes 196612
  14.7 1.6 %collective-permute-start.3 = (bf16[1088,128]{1,0:T(8,128)(2,1)S(1)}, bf16[1088,128]{1,0:T(8,128)(2,1)S(1)}, u32[]{:S(2)}, u32[]{:S(2)}) collective-permute-start(bf16[1088,128]{1,0:T(8,128)(2,1)S(1)} %get-tuple-element.28), channel_id=1, source_target_pairs={{0,4},{4,0},{8,12},{12,8},{16,20},{20,16},{24,28},{28,24},{1,5},{5... | collective-permute-start | bytes 835592 | tf_op jit(solution)/shard_map/ppermute | solution.py:341
  16.4 4.4 %collective-permute-start.4 = (bf16[272,128]{1,0:T(8,128)(2,1)S(1)}, bf16[272,128]{1,0:T(8,128)(2,1)S(1)}, u32[]{:S(2)}, u32[]{:S(2)}) collective-permute-start(bf16[272,128]{1,0:T(8,128)(2,1)S(1)} %get-tuple-element.30), channel_id=1, source_target_pairs={{0,16},{4,20},{8,24},{12,28},{16,0},{20,4},{24,8},{28,12},{1,17},{... | collective-permute-start | bytes 208904 | tf_op jit(solution)/shard_map/ppermute | solution.py:341
  18.0 5.9 %collective-permute-start.5 = (bf16[272,128]{1,0:T(8,128)(2,1)S(1)}, bf16[272,128]{1,0:T(8,128)(2,1)S(1)}, u32[]{:S(2)}, u32[]{:S(2)}) collective-permute-start(bf16[272,128]{1,0:T(8,128)(2,1)S(1)} %get-tuple-element.31), channel_id=1, source_target_pairs={{0,24},{4,28},{8,16},{12,20},{16,8},{20,12},{24,0},{28,4},{1,25},{... | collective-permute-start | bytes 208904 | tf_op jit(solution)/shard_map/ppermute | solution.py:341
  19.4 4.4 %collective-permute-start.6 = (bf16[272,128]{1,0:T(8,128)(2,1)S(1)}, bf16[272,128]{1,0:T(8,128)(2,1)S(1)}, u32[]{:S(2)}, u32[]{:S(2)}) collective-permute-start(bf16[272,128]{1,0:T(8,128)(2,1)S(1)} %get-tuple-element.32), channel_id=1, source_target_pairs={{0,8},{4,12},{8,0},{12,4},{16,24},{20,28},{24,16},{28,20},{1,9},{5... | collective-permute-start | bytes 208904 | tf_op jit(solution)/shard_map/ppermute | solution.py:341
  23.9 7.8 %collective-permute-start.9 = (bf16[272,128]{1,0:T(8,128)(2,1)S(1)}, bf16[272,128]{1,0:T(8,128)(2,1)S(1)}, u32[]{:S(2)}, u32[]{:S(2)}) collective-permute-start(bf16[272,128]{1,0:T(8,128)(2,1)S(1)} %group_sum.1.refs_0_), channel_id=1, source_target_pairs={{0,2},{1,3},{2,0},{3,1},{4,6},{5,7},{6,4},{7,5},{8,10},{9,11},{10,... | collective-permute-start | bytes 208904 | tf_op jit(solution)/shard_map/ppermute | solution.py:341
  25.2 6.4 %collective-permute-start.8 = (bf16[272,128]{1,0:T(8,128)(2,1)S(1)}, bf16[272,128]{1,0:T(8,128)(2,1)S(1)}, u32[]{:S(2)}, u32[]{:S(2)}) collective-permute-start(bf16[272,128]{1,0:T(8,128)(2,1)S(1)} %group_sum.1.refs_0_), channel_id=1, source_target_pairs={{0,3},{1,2},{2,1},{3,0},{4,7},{5,6},{6,5},{7,4},{8,11},{9,10},{10,... | collective-permute-start | bytes 208904 | tf_op jit(solution)/shard_map/ppermute | solution.py:341
  26.5 5.6 %collective-permute-start.7 = (bf16[272,128]{1,0:T(8,128)(2,1)S(1)}, bf16[272,128]{1,0:T(8,128)(2,1)S(1)}, u32[]{:S(2)}, u32[]{:S(2)}) collective-permute-start(bf16[272,128]{1,0:T(8,128)(2,1)S(1)} %group_sum.1.refs_0_), channel_id=1, source_target_pairs={{0,1},{1,0},{2,3},{3,2},{4,5},{5,4},{6,7},{7,6},{8,9},{9,8},{10,11... | collective-permute-start | bytes 208904 | tf_op jit(solution)/shard_map/ppermute | solution.py:341
  32.1 5.3 %collective-permute-start.12 = (bf16[272,128]{1,0:T(8,128)(2,1)S(1)}, bf16[272,128]{1,0:T(8,128)(2,1)S(1)}, u32[]{:S(2)}, u32[]{:S(2)}) collective-permute-start(bf16[272,128]{1,0:T(8,128)(2,1)S(1)} %space_sum.1.refs_0_), channel_id=1, source_target_pairs={{0,24},{4,28},{8,16},{12,20},{16,8},{20,12},{24,0},{28,4},{1,25},{... | collective-permute-start | bytes 208904 | tf_op jit(solution)/shard_map/ppermute | solution.py:341
  34.1 4.3 %collective-permute-start.11 = (bf16[272,128]{1,0:T(8,128)(2,1)S(1)}, bf16[272,128]{1,0:T(8,128)(2,1)S(1)}, u32[]{:S(2)}, u32[]{:S(2)}) collective-permute-start(bf16[272,128]{1,0:T(8,128)(2,1)S(1)} %space_sum.1.refs_0_), channel_id=1, source_target_pairs={{0,16},{4,20},{8,24},{12,28},{16,0},{20,4},{24,8},{28,12},{1,17},{... | collective-permute-start | bytes 208904 | tf_op jit(solution)/shard_map/ppermute | solution.py:341
  34.3 4.3 %collective-permute-start.10 = (bf16[272,128]{1,0:T(8,128)(2,1)S(1)}, bf16[272,128]{1,0:T(8,128)(2,1)S(1)}, u32[]{:S(2)}, u32[]{:S(2)}) collective-permute-start(bf16[272,128]{1,0:T(8,128)(2,1)S(1)} %space_sum.1.refs_0_), channel_id=1, source_target_pairs={{0,8},{4,12},{8,0},{12,4},{16,24},{20,28},{24,16},{28,20},{1,9},{5... | collective-permute-start | bytes 208904 | tf_op jit(solution)/shard_map/ppermute | solution.py:341
  35.7 3.2 %collective-permute-start.13 = (bf16[272,128]{1,0:T(8,128)(2,1)S(1)}, bf16[272,128]{1,0:T(8,128)(2,1)S(1)}, u32[]{:S(2)}, u32[]{:S(2)}) collective-permute-start(bf16[272,128]{1,0:T(8,128)(2,1)S(1)} %space_sum.1.refs_0_), channel_id=1, source_target_pairs={{0,4},{4,0},{8,12},{12,8},{16,20},{20,16},{24,28},{28,24},{1,5},{5... | collective-permute-start | bytes 208904 | tf_op jit(solution)/shard_map/ppermute | solution.py:341
  37.4 1.5 %collective-permute-start.16 = (bf16[272,128]{1,0:T(8,128)(2,1)S(1)}, bf16[272,128]{1,0:T(8,128)(2,1)S(1)}, u32[]{:S(2)}, u32[]{:S(2)}) collective-permute-start(bf16[272,128]{1,0:T(8,128)(2,1)S(1)} %collective-permute-done.12.refs_3_), channel_id=1, source_target_pairs={{0,4},{4,0},{8,12},{12,8},{16,20},{20,16},{24,28},{28,24},{1,5},{5... | collective-permute-start | bytes 208904 | tf_op jit(solution)/shard_map/ppermute | solution.py:341
  38.4 1.3 %collective-permute-start.15 = (bf16[272,128]{1,0:T(8,128)(2,1)S(1)}, bf16[272,128]{1,0:T(8,128)(2,1)S(1)}, u32[]{:S(2)}, u32[]{:S(2)}) collective-permute-start(bf16[272,128]{1,0:T(8,128)(2,1)S(1)} %collective-permute-done.11.refs_2_), channel_id=1, source_target_pairs={{0,4},{4,0},{8,12},{12,8},{16,20},{20,16},{24,28},{28,24},{1,5},{5... | collective-permute-start | bytes 208904 | tf_op jit(solution)/shard_map/ppermute | solution.py:341
  38.7 1.3 %collective-permute-start.14 = (bf16[272,128]{1,0:T(8,128)(2,1)S(1)}, bf16[272,128]{1,0:T(8,128)(2,1)S(1)}, u32[]{:S(2)}, u32[]{:S(2)}) collective-permute-start(bf16[272,128]{1,0:T(8,128)(2,1)S(1)} %collective-permute-done.10.refs_1_), channel_id=1, source_target_pairs={{0,4},{4,0},{8,12},{12,8},{16,20},{20,16},{24,28},{28,24},{1,5},{5... | collective-permute-start | bytes 208904 | tf_op jit(solution)/shard_map/ppermute | solution.py:341

commit v4 on v3

--- a/solution.py
+++ b/solution.py
@@ -15,6 +15,29 @@
 SMALL_LIMIT = 4 * 1024 * 1024
 BF16 = jnp.bfloat16
 F32 = jnp.float32
+
+
+def gray(number):
+    return number ^ (number >> 1)
+
+
+def odd(number):
+    for shift in (8, 4, 2, 1):
+        number = number ^ (number >> shift)
+    return number & 1
+
+
+def half_of(plan, sample):
+    return (sample % plan.cores) ^ odd(sample // plan.cores)
+
+
+def own_half(plan):
+    return half_of(plan, lax.axis_index("sample"))
+
+
+def place_in(plan, half):
+    group, space = lax.axis_index("sample") // plan.cores, lax.axis_index("space")
+    return jnp.where(half == 0, group, space) if plan.crossed else group
 
 
 def vmem():
@@ -94,7 +117,7 @@
     x_ref, s_one, t_one, slope_ref, lk_ref, d_one, s_two, t_two, d_two, sd_two, u_two, pay_ref = refs[plan.space + 9 :]
     inner, mid, out = plan.inner, plan.mid, plan.out
     blocks, halves = plan.blocks, plan.halves
-    place, core = lax.axis_index("space"), lax.axis_index("sample") % plan.cores
+    place, own_core = lax.axis_index("space"), own_half(plan)
     side, small = SIDE, SIDE // 2
     plane = side * side
     low = small * small
@@ -233,8 +256,8 @@
         pay_ref[plan.total - ROWS :, :] = jnp.concatenate([high, tail - high], axis=0)
 
     share = plan.total // plan.cores
-    keep_ref[...] = pay_ref[pl.ds(pl.multiple_of(core * share, ROWS), share), :]
-    send_ref[...] = pay_ref[pl.ds(pl.multiple_of((1 - core) * share, ROWS), share), :].astype(BF16)
+    keep_ref[...] = pay_ref[pl.ds(pl.multiple_of(own_core * share, ROWS), share), :]
+    send_ref[...] = pay_ref[pl.ds(pl.multiple_of((1 - own_core) * share, ROWS), share), :].astype(BF16)
 
 
 def split_again(values, plan, last):
@@ -247,14 +270,14 @@
 
 def core_sum_kernel(plan, keep_ref, got_ref, own_ref, *rest):
     sends, sum_ref = rest[:-1], rest[-1]
-    group = lax.axis_index("sample") // plan.cores
-    core = lax.axis_index("sample") % plan.cores
+    half = own_half(plan)
+    place = place_in(plan, half)
     rows = keep_ref.shape[0]
     sum_ref[...] = keep_ref[...] + got_ref[...].astype(F32)
-    sum_ref[rows - ROWS :, :] = split_again(sum_ref[rows - ROWS :, :], plan, core == plan.cores - 1)
+    sum_ref[rows - ROWS :, :] = split_again(sum_ref[rows - ROWS :, :], plan, half == plan.cores - 1)
 
     def chunk(k):
-        return sum_ref[pl.ds(pl.multiple_of((group ^ k) * plan.chunk, ROWS), plan.chunk), :]
+        return sum_ref[pl.ds(pl.multiple_of((place ^ k) * plan.chunk, ROWS), plan.chunk), :]
 
     own_ref[...] = chunk(0)
     for k, send in enumerate(sends, start=1):
@@ -262,7 +285,8 @@
 
 
 def last_chunk(plan):
-    return lax.axis_index("sample") == lax.axis_size("sample") - 1
+    half = own_half(plan)
+    return (half == plan.cores - 1) & (place_in(plan, half) == plan.groups - 1)
 
 
 def group_sum_kernel(plan, own_ref, *rest):
@@ -288,10 +312,10 @@
 def unpack_kernel(plan, *refs):
     one_ref, bias_one_ref, two_ref, bias_two_ref, all_ref = refs[-5:]
     inner, mid, out = plan.inner, plan.mid, plan.out
-    group, core = lax.axis_index("sample") // plan.cores, lax.axis_index("sample") % plan.cores
+    own = own_half(plan)
     for k, ref in enumerate(refs[:-5]):
         side, k = k // plan.groups, k % plan.groups
-        start = ((core ^ side) * plan.groups + (group ^ k)) * plan.chunk
+        start = ((own ^ side) * plan.groups + (place_in(plan, own ^ side) ^ gray(k))) * plan.chunk
         all_ref[pl.ds(pl.multiple_of(start, ROWS), plan.chunk), :] = ref[...].astype(F32)
     total, first = 27 * mid, 9 * inner
     two_ref[...] = all_ref[:total, :].reshape(27, mid, out)
@@ -316,6 +340,7 @@
         self.halves = self.blocks // 8
         self.cores = 2
         self.groups = self.sample // self.cores
+        self.crossed = self.groups == self.space
         cells = self.blocks * LANES * volumes.shape[0] * self.sample
         self.scale_one = 1.0 / math.sqrt(cells)
         self.scale_two = 1.0 / math.sqrt(cells // 8)
@@ -339,6 +364,21 @@
 
 def swap(value, axis, k):
     return lax.ppermute(value, axis, [(i, i ^ k) for i in range(lax.axis_size(axis))])
+
+
+def trade(plan, value, k, within):
+    pairs = []
+    for sample in range(plan.sample):
+        for space in range(plan.space):
+            half = half_of(plan, sample)
+            group, other = sample // plan.cores, space
+            if (plan.crossed and half == 1) == within:
+                other = other ^ k
+            else:
+                group = group ^ k
+            core = half ^ half_of(plan, group * plan.cores)
+            pairs.append((sample * plan.space + space, (group * plan.cores + core) * plan.space + other))
+    return lax.ppermute(value, ("sample", "space"), pairs)
 
 
 def on_device(volumes, grad_out, kernel_first, bias_first, kernel_second, bias_second):
@@ -381,12 +421,11 @@
     chunk = (plan.chunk, LANES)
     got = swap(send, "sample", 1)
     own, *sends = call(core_sum_kernel, plan, "core_sum", ((chunk, F32),) + ((chunk, BF16),) * (plan.groups - 1), keep, got, scratch=(((share, LANES), F32),))
-    gots = [swap(s, "sample", plan.cores * k) for k, s in enumerate(sends, start=1)]
+    gots = [trade(plan, s, k, True) for k, s in enumerate(sends, start=1)]
     (partial,) = call(group_sum_kernel, plan, "group_sum", ((chunk, BF16),), own, *gots[1:], gots[0])
-    gots = [swap(partial, "space", k ^ (k >> 1)) for k in range(1, plan.space)]
+    gots = [trade(plan, partial, gray(k), False) for k in range(1, plan.space)]
     (whole,) = call(space_sum_kernel, plan, "space_sum", ((chunk, BF16),), partial, *gots)
-    gots = [swap(whole, "sample", plan.cores * k) for k in range(1, plan.groups)]
-    mine = [whole, *gots]
+    mine = [whole] + [trade(plan, whole, gray(k), True) for k in range(1, plan.groups)]
     other = [swap(value, "sample", 1) for value in mine]
     one, bias_one, two, bias_two = call(
         unpack_kernel,

time: 41.3 us -> 39.4 us (0.954)
  waiting for transfers between devices: 16 us -> 13.7 us
  starting transfers between devices: 16.7 us -> 17.2 us
    ppermute x17 -> x8, waiting for transfers between devices: 16 us -> 4.78 us  [swap(): lax.ppermute(value, axis, [(i, i ^ k) for i in range(lax.axis_size(axis))])]
    ppermute x0 -> x9, starting transfers between devices: none -> 9.53 us  [trade(): return lax.ppermute(value, ('sample', 'space'), pairs)]
    ppermute x17 -> x8, starting transfers between devices: 16.7 us -> 7.63 us  [swap(): lax.ppermute(value, axis, [(i, i ^ k) for i in range(lax.axis_size(axis))])]
    ppermute x0 -> x9, waiting for transfers between devices: none -> 8.88 us  [trade(): return lax.ppermute(value, ('sample', 'space'), pairs)]
where the time goes in v4:
time: 39.4 us; the launch traced here: 39.2 us
  starting transfers between devices  17.2 us (44%)
  waiting for transfers between devices  13.7 us (35%)
  Pallas kernels  5.08 us (13%)
  local copies, waits for them, and re-layouts  2.57 us (7%)
  between operations  0.72 us (2%)
    ppermute x9, starting transfers between devices, trade(): return lax.ppermute(value, ('sample', 'space'), pairs)  9.53 us
    ppermute x9, waiting for transfers between devices, trade(): return lax.ppermute(value, ('sample', 'space'), pairs)  8.88 us
    ppermute x8, starting transfers between devices, swap(): lax.ppermute(value, axis, [(i, i ^ k) for i in range(lax.axis_size(axis))])  7.63 us
    ppermute x8, waiting for transfers between devices, swap(): lax.ppermute(value, axis, [(i, i ^ k) for i in range(lax.axis_size(axis))])  4.78 us
    pallas_call x5, Pallas kernels, call(): pl.pallas_call(functools.partial(kernel, plan), out_shape=[jax.ShapeDtype...  4.65 us
    unnamed x10, local copies, waits for them, and re-layouts  1.69 us
    dynamic_slice x1, local copies, waits for them, and re-layouts, piece(): lax.dynamic_slice_in_dim(volumes, (me ^ k) * plan.owned, plan.owned, axis=0)  0.88 us
  transfers between devices with their start and end apart: 17, of which 11 were waited for; matrix products, arithmetic and copies ran while one was open for 0% of the time, Pallas kernels for 1%

profile of v4, /device:TPU:0, one launch (start us, length us, event | category | flops | bytes accessed | tf_op | source)
XLA Modules:
  0.0 39.2 jit_solution(13976670668545421765)
XLA Ops:
  0.6 0.0 copy-start.1
  0.7 0.9 %constant_dynamic-slice_fusion = (bf16[1,32,512]{2,1,0:T(8,128)(2,1)S(1)}, bf16[1,32,512]{2,1,0:T(8,128)(2,1)S(1)}, bf16[1,32,512]{2,1,0:T(8,128)(2,1)S(1)}, bf16[1,32,512]{2,1,0:T(8,128)(2,1)S(1)}) fusion(bf16[4,32,512]{2,1,0:T(8,128)(2,1)} %param.6, s32[]{:T(128)S(6)} %select_n.15, s32[]{:T(128)S(6)} %select_n.13, s32[]{:T(128)S(6)} %select_n.12, s32[]{:T(128)S(6)} %select_n.14), kind=kLoop, calls=%fused_computation | loop fusion | bytes 262160 | tf_op jit(solution)/shard_map/dynamic_slice | solution.py:390
  1.5 4.1 %collective-permute-start.1 = (bf16[1,32,512]{2,1,0:T(8,128)(2,1)S(1)}, bf16[1,32,512]{2,1,0:T(8,128)(2,1)S(1)}, u32[]{:S(2)}, u32[]{:S(2)}) collective-permute-start(bf16[1,32,512]{2,1,0:T(8,128)(2,1)S(1)} %get-tuple-element.38), channel_id=1, source_target_pairs={{0,2},{1,3},{2,0},{3,1},{4,6},{5,7},{6,4},{7,5},{8,10},{9,11},{10,... | collective-permute-start | bytes 98312 | tf_op jit(solution)/shard_map/ppermute | solution.py:366
  5.6 1.3 %collective-permute-start = (bf16[1,32,512]{2,1,0:T(8,128)(2,1)S(1)}, bf16[1,32,512]{2,1,0:T(8,128)(2,1)S(1)}, u32[]{:S(2)}, u32[]{:S(2)}) collective-permute-start(bf16[1,32,512]{2,1,0:T(8,128)(2,1)S(1)} %get-tuple-element.39), channel_id=1, source_target_pairs={{0,3},{1,2},{2,1},{3,0},{4,7},{5,6},{6,5},{7,4},{8,11},{9,10},{10,... | collective-permute-start | bytes 98312 | tf_op jit(solution)/shard_map/ppermute | solution.py:366
  7.0 0.2 collective-permute-start.2
  7.2 0.0 copy-start.3
  7.2 0.0 copy-start.4
  7.2 0.0 copy-done.1
  7.2 0.6 %copy-done.3 = f32[64]{0:T(128)S(1)} copy-done((f32[64]{0:T(128)S(1)}, f32[64]{0:T(128)}, u32[]{:S(2)}) %copy-start.3) | copy-done | bytes 280
  7.9 0.0 copy-done.4
  7.9 0.0 copy-start
  7.9 1.0 %copy-done = bf16[27,128,64]{1,2,0:T(8,128)(2,1)S(1)} copy-done((bf16[27,128,64]{1,2,0:T(8,128)(2,1)S(1)}, bf16[27,128,64]{1,2,0:T(8,128)(2,1)}, u32[]{:S(2)}) %copy-start) | copy-done | bytes 442392
  8.9 0.4 %weights.1 = (bf16[192,288]{1,0:T(8,128)(2,1)S(1)}, bf16[384,576]{1,0:T(8,128)(2,1)S(1)}, bf16[192,1152]{1,0:T(8,128)(2,1)S(1)}, f32[64,128]{1,0:T(8,128)S(1)}, f32[128,128]{1,0:T(8,128)S(1)}) custom-call(bf16[27,32,64]{2,1,0:T(8,128)(2,1)S(1)} %bitcast.9, bf16[27,64,128]{2,1,0:T(8,128)(2,1)S(1)} %bitcast.8, f32[1,64]{1,0:T(1,128)S(1)} %bitcast.10, ...), custom_call_target="tpu_custom_call" | custom-call | tf_op jit(solution)/shard_map/weights/pallas_call | solution.py:101
  9.3 0.0 collective-permute-done.1.refs_1_
  9.4 2.0 %collective-permute-done.refs_0_ = bf16[1,32,512]{2,1,0:T(8,128)(2,1)S(1)} collective-permute-done((bf16[1,32,512]{2,1,0:T(8,128)(2,1)S(1)}, bf16[1,32,512]{2,1,0:T(8,128)(2,1)S(1)}, u32[]{:S(2)}, u32[]{:S(2)}) %collective-permute-start) | collective-permute-done | bytes 32800 | tf_op jit(solution)/shard_map/ppermute | solution.py:366
  11.4 0.0 collective-permute-done.2.refs_2_
  11.4 0.0 copy-done.2
  11.4 3.2 %main.1 = (bf16[1,128,256]{2,1,0:T(8,128)(2,1)}, f32[1088,128]{1,0:T(8,128)S(1)}, bf16[1088,128]{1,0:T(8,128)(2,1)S(1)}) custom-call(bf16[1,32,512]{2,1,0:T(8,128)(2,1)S(1)} %collective-permute-done.refs_0_, bf16[1,32,512]{2,1,0:T(8,128)(2,1)S(1)} %collective-permute-done.1.refs_1_, bf16[1,32,512]{2,1,0:T(8,128)(2,1)S(1)} %collective-permute-done.2.refs_2_, ...), custom_call_target="tpu_custom_call" | custom-call | tf_op jit(solution)/shard_map/main/pallas_call | solution.py:354
  14.6 0.1 collective-permute-start.3
  14.7 1.5 %collective-permute-done.3.got_ref = bf16[1088,128]{1,0:T(8,128)(2,1)S(1)} collective-permute-done((bf16[1088,128]{1,0:T(8,128)(2,1)S(1)}, bf16[1088,128]{1,0:T(8,128)(2,1)S(1)}, u32[]{:S(2)}, u32[]{:S(2)}) %collective-permute-start.3) | collective-permute-done | bytes 278560 | tf_op jit(solution)/shard_map/ppermute | solution.py:366
  16.2 0.1 core_sum.1
  16.3 1.3 %collective-permute-start.4 = (bf16[272,128]{1,0:T(8,128)(2,1)S(1)}, bf16[272,128]{1,0:T(8,128)(2,1)S(1)}, u32[]{:S(2)}, u32[]{:S(2)}) collective-permute-start(bf16[272,128]{1,0:T(8,128)(2,1)S(1)} %get-tuple-element.30), channel_id=1, source_target_pairs={{0,20},{1,21},{2,22},{3,23},{4,6},{5,7},{6,4},{7,5},{8,10},{9,11},... | collective-permute-start | bytes 208904 | tf_op jit(solution)/shard_map/ppermute | solution.py:381
  17.7 1.4 %collective-permute-start.5 = (bf16[272,128]{1,0:T(8,128)(2,1)S(1)}, bf16[272,128]{1,0:T(8,128)(2,1)S(1)}, u32[]{:S(2)}, u32[]{:S(2)}) collective-permute-start(bf16[272,128]{1,0:T(8,128)(2,1)S(1)} %get-tuple-element.31), channel_id=1, source_target_pairs={{0,24},{1,25},{2,26},{3,27},{4,7},{5,6},{6,5},{7,4},{8,11},{9,10},... | collective-permute-start | bytes 208904 | tf_op jit(solution)/shard_map/ppermute | solution.py:381
  19.1 0.2 collective-permute-start.6
  19.3 0.8 %collective-permute-done.4.rest_0_ = bf16[272,128]{1,0:T(8,128)(2,1)S(1)} collective-permute-done((bf16[272,128]{1,0:T(8,128)(2,1)S(1)}, bf16[272,128]{1,0:T(8,128)(2,1)S(1)}, u32[]{:S(2)}, u32[]{:S(2)}) %collective-permute-start.4) | collective-permute-done | bytes 69664 | tf_op jit(solution)/shard_map/ppermute | solution.py:381
  20.1 2.7 %collective-permute-done.5.rest_1_ = bf16[272,128]{1,0:T(8,128)(2,1)S(1)} collective-permute-done((bf16[272,128]{1,0:T(8,128)(2,1)S(1)}, bf16[272,128]{1,0:T(8,128)(2,1)S(1)}, u32[]{:S(2)}, u32[]{:S(2)}) %collective-permute-start.5) | collective-permute-done | bytes 69664 | tf_op jit(solution)/shard_map/ppermute | solution.py:381
  22.9 0.0 collective-permute-done.6.rest_2_
  22.9 1.3 %collective-permute-start.9 = (bf16[272,128]{1,0:T(8,128)(2,1)S(1)}, bf16[272,128]{1,0:T(8,128)(2,1)S(1)}, u32[]{:S(2)}, u32[]{:S(2)}) collective-permute-start(bf16[272,128]{1,0:T(8,128)(2,1)S(1)} %group_sum.1.refs_0_), channel_id=1, source_target_pairs={{0,2},{1,3},{2,0},{3,1},{4,16},{5,17},{6,18},{7,19},{8,28},{9,29},... | collective-permute-start | bytes 208904 | tf_op jit(solution)/shard_map/ppermute | solution.py:381
  24.2 1.3 %collective-permute-start.8 = (bf16[272,128]{1,0:T(8,128)(2,1)S(1)}, bf16[272,128]{1,0:T(8,128)(2,1)S(1)}, u32[]{:S(2)}, u32[]{:S(2)}) collective-permute-start(bf16[272,128]{1,0:T(8,128)(2,1)S(1)} %group_sum.1.refs_0_), channel_id=1, source_target_pairs={{0,3},{1,2},{2,1},{3,0},{4,28},{5,29},{6,30},{7,31},{8,16},{9,17},... | collective-permute-start | bytes 208904 | tf_op jit(solution)/shard_map/ppermute | solution.py:381
  25.5 0.9 %collective-permute-start.7 = (bf16[272,128]{1,0:T(8,128)(2,1)S(1)}, bf16[272,128]{1,0:T(8,128)(2,1)S(1)}, u32[]{:S(2)}, u32[]{:S(2)}) collective-permute-start(bf16[272,128]{1,0:T(8,128)(2,1)S(1)} %group_sum.1.refs_0_), channel_id=1, source_target_pairs={{0,1},{1,0},{2,3},{3,2},{4,8},{5,9},{6,10},{7,11},{8,4},{9,5},{10,... | collective-permute-start | bytes 208904 | tf_op jit(solution)/shard_map/ppermute | solution.py:381
  26.5 2.1 %collective-permute-done.9.refs_3_ = bf16[272,128]{1,0:T(8,128)(2,1)S(1)} collective-permute-done((bf16[272,128]{1,0:T(8,128)(2,1)S(1)}, bf16[272,128]{1,0:T(8,128)(2,1)S(1)}, u32[]{:S(2)}, u32[]{:S(2)}) %collective-permute-start.9) | collective-permute-done | bytes 69664 | tf_op jit(solution)/shard_map/ppermute | solution.py:381
  28.5 1.9 %collective-permute-done.8.refs_2_ = bf16[272,128]{1,0:T(8,128)(2,1)S(1)} collective-permute-done((bf16[272,128]{1,0:T(8,128)(2,1)S(1)}, bf16[272,128]{1,0:T(8,128)(2,1)S(1)}, u32[]{:S(2)}, u32[]{:S(2)}) %collective-permute-start.8) | collective-permute-done | bytes 69664 | tf_op jit(solution)/shard_map/ppermute | solution.py:381
  30.4 0.1 collective-permute-done.7.refs_1_
  30.6 0.1 collective-permute-start.12
  30.7 1.7 %collective-permute-start.11 = (bf16[272,128]{1,0:T(8,128)(2,1)S(1)}, bf16[272,128]{1,0:T(8,128)(2,1)S(1)}, u32[]{:S(2)}, u32[]{:S(2)}) collective-permute-start(bf16[272,128]{1,0:T(8,128)(2,1)S(1)} %space_sum.1.refs_0_), channel_id=1, source_target_pairs={{0,24},{1,25},{2,26},{3,27},{4,7},{5,6},{6,5},{7,4},{8,11},{9,10},... | collective-permute-start | bytes 208904 | tf_op jit(solution)/shard_map/ppermute | solution.py:381
  32.4 1.2 %collective-permute-start.10 = (bf16[272,128]{1,0:T(8,128)(2,1)S(1)}, bf16[272,128]{1,0:T(8,128)(2,1)S(1)}, u32[]{:S(2)}, u32[]{:S(2)}) collective-permute-start(bf16[272,128]{1,0:T(8,128)(2,1)S(1)} %space_sum.1.refs_0_), channel_id=1, source_target_pairs={{0,12},{1,13},{2,14},{3,15},{4,5},{5,4},{6,7},{7,6},{8,9},{9,8},{1... | collective-permute-start | bytes 208904 | tf_op jit(solution)/shard_map/ppermute | solution.py:381
  33.6 0.0 collective-permute-start.13
  33.6 0.8 %collective-permute-done.12.refs_3_ = bf16[272,128]{1,0:T(8,128)(2,1)S(1)} collective-permute-done((bf16[272,128]{1,0:T(8,128)(2,1)S(1)}, bf16[272,128]{1,0:T(8,128)(2,1)S(1)}, u32[]{:S(2)}, u32[]{:S(2)}) %collective-permute-start.12) | collective-permute-done | bytes 69664 | tf_op jit(solution)/shard_map/ppermute | solution.py:381
  34.4 1.1 %collective-permute-start.16 = (bf16[272,128]{1,0:T(8,128)(2,1)S(1)}, bf16[272,128]{1,0:T(8,128)(2,1)S(1)}, u32[]{:S(2)}, u32[]{:S(2)}) collective-permute-start(bf16[272,128]{1,0:T(8,128)(2,1)S(1)} %collective-permute-done.12.refs_3_), channel_id=1, source_target_pairs={{0,4},{4,0},{8,12},{12,8},{16,20},{20,16},{24,28},{28,24},{1,5},{5... | collective-permute-start | bytes 208904 | tf_op jit(solution)/shard_map/ppermute | solution.py:366
  35.5 0.4 %collective-permute-done.11.refs_2_ = bf16[272,128]{1,0:T(8,128)(2,1)S(1)} collective-permute-done((bf16[272,128]{1,0:T(8,128)(2,1)S(1)}, bf16[272,128]{1,0:T(8,128)(2,1)S(1)}, u32[]{:S(2)}, u32[]{:S(2)}) %collective-permute-start.11) | collective-permute-done | bytes 69664 | tf_op jit(solution)/shard_map/ppermute | solution.py:381
  36.0 0.7 %collective-permute-start.15 = (bf16[272,128]{1,0:T(8,128)(2,1)S(1)}, bf16[272,128]{1,0:T(8,128)(2,1)S(1)}, u32[]{:S(2)}, u32[]{:S(2)}) collective-permute-start(bf16[272,128]{1,0:T(8,128)(2,1)S(1)} %collective-permute-done.11.refs_2_), channel_id=1, source_target_pairs={{0,4},{4,0},{8,12},{12,8},{16,20},{20,16},{24,28},{28,24},{1,5},{5... | collective-permute-start | bytes 208904 | tf_op jit(solution)/shard_map/ppermute | solution.py:366
  36.7 0.0 collective-permute-done.10.refs_1_
  36.7 0.0 collective-permute-start.14
  36.7 0.0 collective-permute-done.13.refs_4_
  36.7 0.0 collective-permute-done.16.refs_7_
  36.7 0.9 %collective-permute-done.15.refs_6_ = bf16[272,128]{1,0:T(8,128)(2,1)S(1)} collective-permute-done((bf16[272,128]{1,0:T(8,128)(2,1)S(1)}, bf16[272,128]{1,0:T(8,128)(2,1)S(1)}, u32[]{:S(2)}, u32[]{:S(2)}) %collective-permute-start.15) | collective-permute-done | bytes 69664 | tf_op jit(solution)/shard_map/ppermute | solution.py:366
  37.6 0.4 collective-permute-done.14.refs_5_
  38.0 1.2 %unpack.1 = (f32[27,32,64]{2,1,0:T(8,128)}, f32[1,64]{1,0:T(1,128)}, f32[27,64,128]{2,1,0:T(8,128)}, f32[1,128]{1,0:T(1,128)}) custom-call(bf16[272,128]{1,0:T(8,128)(2,1)S(1)} %space_sum.1.refs_0_, bf16[272,128]{1,0:T(8,128)(2,1)S(1)} %collective-permute-done.10.refs_1_, bf16[272,128]{1,0:T(8,128)(2,1)S(1)} %collective-permute-done.11.refs_2_, ...), custom_call_target="tpu_custom_call" | custom-call | tf_op jit(solution)/shard_map/unpack/pallas_call | solution.py:354
  (3 shorter events, 0.1 us)
Async XLA Ops:
  0.6 6.6 %copy-start.1 = (bf16[27,64,32]{1,2,0:T(8,128)(2,1)S(1)}, bf16[27,64,32]{1,2,0:T(8,128)(2,1)}, u32[]{:S(2)}) copy-start(bf16[27,64,32]{1,2,0:T(8,128)(2,1)} %param.8) | copy-start | bytes 331780
  1.5 7.8 %collective-permute-start.1 = (bf16[1,32,512]{2,1,0:T(8,128)(2,1)S(1)}, bf16[1,32,512]{2,1,0:T(8,128)(2,1)S(1)}, u32[]{:S(2)}, u32[]{:S(2)}) collective-permute-start(bf16[1,32,512]{2,1,0:T(8,128)(2,1)S(1)} %get-tuple-element.38), channel_id=1, source_target_pairs={{0,2},{1,3},{2,0},{3,1},{4,6},{5,7},{6,4},{7,5},{8,10},{9,11},{10,... | collective-permute-start | bytes 98312 | tf_op jit(solution)/shard_map/ppermute | solution.py:366
  5.6 5.7 %collective-permute-start = (bf16[1,32,512]{2,1,0:T(8,128)(2,1)S(1)}, bf16[1,32,512]{2,1,0:T(8,128)(2,1)S(1)}, u32[]{:S(2)}, u32[]{:S(2)}) collective-permute-start(bf16[1,32,512]{2,1,0:T(8,128)(2,1)S(1)} %get-tuple-element.39), channel_id=1, source_target_pairs={{0,3},{1,2},{2,1},{3,0},{4,7},{5,6},{6,5},{7,4},{8,11},{9,10},{10,... | collective-permute-start | bytes 98312 | tf_op jit(solution)/shard_map/ppermute | solution.py:366
  7.0 4.4 %collective-permute-start.2 = (bf16[1,32,512]{2,1,0:T(8,128)(2,1)S(1)}, bf16[1,32,512]{2,1,0:T(8,128)(2,1)S(1)}, u32[]{:S(2)}, u32[]{:S(2)}) collective-permute-start(bf16[1,32,512]{2,1,0:T(8,128)(2,1)S(1)} %get-tuple-element.40), channel_id=1, source_target_pairs={{0,1},{1,0},{2,3},{3,2},{4,5},{5,4},{6,7},{7,6},{8,9},{9,8},{10,11... | collective-permute-start | bytes 98312 | tf_op jit(solution)/shard_map/ppermute | solution.py:366
  7.2 0.7 %copy-start.3 = (f32[64]{0:T(128)S(1)}, f32[64]{0:T(128)}, u32[]{:S(2)}) copy-start(f32[64]{0:T(128)} %param.9) | copy-start | bytes 772
  7.2 0.7 %copy-start.4 = (f32[128]{0:T(128)S(1)}, f32[128]{0:T(128)}, u32[]{:S(2)}) copy-start(f32[128]{0:T(128)} %param.11) | copy-start | bytes 1540
  7.9 1.0 %copy-start = (bf16[27,128,64]{1,2,0:T(8,128)(2,1)S(1)}, bf16[27,128,64]{1,2,0:T(8,128)(2,1)}, u32[]{:S(2)}) copy-start(bf16[27,128,64]{1,2,0:T(8,128)(2,1)} %param.10) | copy-start | bytes 1327108
  8.9 2.5 %copy-start.2 = (bf16[1,128,256]{2,1,0:T(8,128)(2,1)S(1)}, bf16[1,128,256]{2,1,0:T(8,128)(2,1)}, u32[]{:S(2)}) copy-start(bf16[1,128,256]{2,1,0:T(8,128)(2,1)} %refs_4_.1) | copy-start | bytes 196612
  14.6 1.6 %collective-permute-start.3 = (bf16[1088,128]{1,0:T(8,128)(2,1)S(1)}, bf16[1088,128]{1,0:T(8,128)(2,1)S(1)}, u32[]{:S(2)}, u32[]{:S(2)}) collective-permute-start(bf16[1088,128]{1,0:T(8,128)(2,1)S(1)} %get-tuple-element.28), channel_id=1, source_target_pairs={{0,4},{4,0},{8,12},{12,8},{16,20},{20,16},{24,28},{28,24},{1,5},{5... | collective-permute-start | bytes 835592 | tf_op jit(solution)/shard_map/ppermute | solution.py:366
  16.3 3.8 %collective-permute-start.4 = (bf16[272,128]{1,0:T(8,128)(2,1)S(1)}, bf16[272,128]{1,0:T(8,128)(2,1)S(1)}, u32[]{:S(2)}, u32[]{:S(2)}) collective-permute-start(bf16[272,128]{1,0:T(8,128)(2,1)S(1)} %get-tuple-element.30), channel_id=1, source_target_pairs={{0,20},{1,21},{2,22},{3,23},{4,6},{5,7},{6,4},{7,5},{8,10},{9,11},... | collective-permute-start | bytes 208904 | tf_op jit(solution)/shard_map/ppermute | solution.py:381
  17.7 5.2 %collective-permute-start.5 = (bf16[272,128]{1,0:T(8,128)(2,1)S(1)}, bf16[272,128]{1,0:T(8,128)(2,1)S(1)}, u32[]{:S(2)}, u32[]{:S(2)}) collective-permute-start(bf16[272,128]{1,0:T(8,128)(2,1)S(1)} %get-tuple-element.31), channel_id=1, source_target_pairs={{0,24},{1,25},{2,26},{3,27},{4,7},{5,6},{6,5},{7,4},{8,11},{9,10},... | collective-permute-start | bytes 208904 | tf_op jit(solution)/shard_map/ppermute | solution.py:381
  19.1 3.8 %collective-permute-start.6 = (bf16[272,128]{1,0:T(8,128)(2,1)S(1)}, bf16[272,128]{1,0:T(8,128)(2,1)S(1)}, u32[]{:S(2)}, u32[]{:S(2)}) collective-permute-start(bf16[272,128]{1,0:T(8,128)(2,1)S(1)} %get-tuple-element.32), channel_id=1, source_target_pairs={{0,12},{1,13},{2,14},{3,15},{4,5},{5,4},{6,7},{7,6},{8,9},{9,8},{1... | collective-permute-start | bytes 208904 | tf_op jit(solution)/shard_map/ppermute | solution.py:381
  22.9 5.6 %collective-permute-start.9 = (bf16[272,128]{1,0:T(8,128)(2,1)S(1)}, bf16[272,128]{1,0:T(8,128)(2,1)S(1)}, u32[]{:S(2)}, u32[]{:S(2)}) collective-permute-start(bf16[272,128]{1,0:T(8,128)(2,1)S(1)} %group_sum.1.refs_0_), channel_id=1, source_target_pairs={{0,2},{1,3},{2,0},{3,1},{4,16},{5,17},{6,18},{7,19},{8,28},{9,29},... | collective-permute-start | bytes 208904 | tf_op jit(solution)/shard_map/ppermute | solution.py:381
  24.2 6.2 %collective-permute-start.8 = (bf16[272,128]{1,0:T(8,128)(2,1)S(1)}, bf16[272,128]{1,0:T(8,128)(2,1)S(1)}, u32[]{:S(2)}, u32[]{:S(2)}) collective-permute-start(bf16[272,128]{1,0:T(8,128)(2,1)S(1)} %group_sum.1.refs_0_), channel_id=1, source_target_pairs={{0,3},{1,2},{2,1},{3,0},{4,28},{5,29},{6,30},{7,31},{8,16},{9,17},... | collective-permute-start | bytes 208904 | tf_op jit(solution)/shard_map/ppermute | solution.py:381
  25.5 5.1 %collective-permute-start.7 = (bf16[272,128]{1,0:T(8,128)(2,1)S(1)}, bf16[272,128]{1,0:T(8,128)(2,1)S(1)}, u32[]{:S(2)}, u32[]{:S(2)}) collective-permute-start(bf16[272,128]{1,0:T(8,128)(2,1)S(1)} %group_sum.1.refs_0_), channel_id=1, source_target_pairs={{0,1},{1,0},{2,3},{3,2},{4,8},{5,9},{6,10},{7,11},{8,4},{9,5},{10,... | collective-permute-start | bytes 208904 | tf_op jit(solution)/shard_map/ppermute | solution.py:381
  30.6 3.8 %collective-permute-start.12 = (bf16[272,128]{1,0:T(8,128)(2,1)S(1)}, bf16[272,128]{1,0:T(8,128)(2,1)S(1)}, u32[]{:S(2)}, u32[]{:S(2)}) collective-permute-start(bf16[272,128]{1,0:T(8,128)(2,1)S(1)} %space_sum.1.refs_0_), channel_id=1, source_target_pairs={{0,20},{1,21},{2,22},{3,23},{4,6},{5,7},{6,4},{7,5},{8,10},{9,11},... | collective-permute-start | bytes 208904 | tf_op jit(solution)/shard_map/ppermute | solution.py:381
  30.7 5.3 %collective-permute-start.11 = (bf16[272,128]{1,0:T(8,128)(2,1)S(1)}, bf16[272,128]{1,0:T(8,128)(2,1)S(1)}, u32[]{:S(2)}, u32[]{:S(2)}) collective-permute-start(bf16[272,128]{1,0:T(8,128)(2,1)S(1)} %space_sum.1.refs_0_), channel_id=1, source_target_pairs={{0,24},{1,25},{2,26},{3,27},{4,7},{5,6},{6,5},{7,4},{8,11},{9,10},... | collective-permute-start | bytes 208904 | tf_op jit(solution)/shard_map/ppermute | solution.py:381
  32.4 4.3 %collective-permute-start.10 = (bf16[272,128]{1,0:T(8,128)(2,1)S(1)}, bf16[272,128]{1,0:T(8,128)(2,1)S(1)}, u32[]{:S(2)}, u32[]{:S(2)}) collective-permute-start(bf16[272,128]{1,0:T(8,128)(2,1)S(1)} %space_sum.1.refs_0_), channel_id=1, source_target_pairs={{0,12},{1,13},{2,14},{3,15},{4,5},{5,4},{6,7},{7,6},{8,9},{9,8},{1... | collective-permute-start | bytes 208904 | tf_op jit(solution)/shard_map/ppermute | solution.py:381
  33.6 3.1 %collective-permute-start.13 = (bf16[272,128]{1,0:T(8,128)(2,1)S(1)}, bf16[272,128]{1,0:T(8,128)(2,1)S(1)}, u32[]{:S(2)}, u32[]{:S(2)}) collective-permute-start(bf16[272,128]{1,0:T(8,128)(2,1)S(1)} %space_sum.1.refs_0_), channel_id=1, source_target_pairs={{0,4},{4,0},{8,12},{12,8},{16,20},{20,16},{24,28},{28,24},{1,5},{5... | collective-permute-start | bytes 208904 | tf_op jit(solution)/shard_map/ppermute | solution.py:366
  34.4 2.3 %collective-permute-start.16 = (bf16[272,128]{1,0:T(8,128)(2,1)S(1)}, bf16[272,128]{1,0:T(8,128)(2,1)S(1)}, u32[]{:S(2)}, u32[]{:S(2)}) collective-permute-start(bf16[272,128]{1,0:T(8,128)(2,1)S(1)} %collective-permute-done.12.refs_3_), channel_id=1, source_target_pairs={{0,4},{4,0},{8,12},{12,8},{16,20},{20,16},{24,28},{28,24},{1,5},{5... | collective-permute-start | bytes 208904 | tf_op jit(solution)/shard_map/ppermute | solution.py:366
  36.0 1.6 %collective-permute-start.15 = (bf16[272,128]{1,0:T(8,128)(2,1)S(1)}, bf16[272,128]{1,0:T(8,128)(2,1)S(1)}, u32[]{:S(2)}, u32[]{:S(2)}) collective-permute-start(bf16[272,128]{1,0:T(8,128)(2,1)S(1)} %collective-permute-done.11.refs_2_), channel_id=1, source_target_pairs={{0,4},{4,0},{8,12},{12,8},{16,20},{20,16},{24,28},{28,24},{1,5},{5... | collective-permute-start | bytes 208904 | tf_op jit(solution)/shard_map/ppermute | solution.py:366
  36.7 1.3 %collective-permute-start.14 = (bf16[272,128]{1,0:T(8,128)(2,1)S(1)}, bf16[272,128]{1,0:T(8,128)(2,1)S(1)}, u32[]{:S(2)}, u32[]{:S(2)}) collective-permute-start(bf16[272,128]{1,0:T(8,128)(2,1)S(1)} %collective-permute-done.10.refs_1_), channel_id=1, source_target_pairs={{0,4},{4,0},{8,12},{12,8},{16,20},{20,16},{24,28},{28,24},{1,5},{5... | collective-permute-start | bytes 208904 | tf_op jit(solution)/shard_map/ppermute | solution.py:366

commit v5 on v4

--- a/solution.py
+++ b/solution.py
@@ -138,15 +138,15 @@
             for j in range(plan.part_blocks):
                 x_ref[start + j] = part[volume, :, j * LANES : (j + 1) * LANES]
 
-        for first_block in range(0, blocks, plan.part_blocks):
+        for first_block in range(0, blocks, 8):
             for tap in range(9):
                 valid, shift = in_plane(side, tap)
-                for j in range(first_block, first_block + plan.part_blocks):
+                for j in range(first_block, first_block + 8):
                     block = x_ref[j]
                     if shift:
                         block = jnp.where(valid, turn(block, shift), jnp.zeros_like(block))
                     s_one[tap * inner : (tap + 1) * inner, j * LANES : (j + 1) * LANES] = block
-            here = slice(first_block * LANES, (first_block + plan.part_blocks) * LANES)
+            here = slice(first_block * LANES, (first_block + 8) * LANES)
             t_one[:, here] = dot(conv_one_ref[...], s_one[: 9 * inner, here])
 
         upper = lane >= plane
@@ -171,10 +171,11 @@
             for j in range(LANES // low):
                 row = (h * (LANES // low) + j) * mid
                 pooled = jnp.where(lane // low == j, means[row : row + mid], pooled)
+            pooled = pooled.astype(BF16)
             for tap in range(9):
                 valid, shift = in_plane(small, tap)
-                block = jnp.where(valid, turn(pooled, shift), 0.0) if shift else pooled
-                s_two[tap * mid : (tap + 1) * mid, here] = block.astype(BF16)
+                block = jnp.where(valid, turn(pooled, shift), jnp.zeros_like(pooled)) if shift else pooled
+                s_two[tap * mid : (tap + 1) * mid, here] = block
 
         t_two[...] = dot(conv_two_ref[...], s_two[: 9 * mid, :])
         deltas = []
@@ -187,21 +188,21 @@
             pre = t_two[out : 2 * out, here] + turn(up, -low) + turn(down, low) + col_two_ref[...]
             slope = jnp.where(pre > 0, 1.0, LEAK_SLOPE)
             feat_ref[volume, :, here] = (slope * pre).astype(BF16)
-            delta = (grad_ref[volume, :, here].astype(F32) * slope).astype(BF16).astype(F32)
+            delta = (grad_ref[volume, :, here].astype(F32) * slope).astype(BF16)
             deltas.append(delta)
             for tap in range(9):
                 valid, shift = in_plane(small, 8 - tap)
-                block = jnp.where(valid, turn(delta, shift), 0.0) if shift else delta
-                sd_two[tap * out : (tap + 1) * out, here] = block.astype(BF16)
+                block = jnp.where(valid, turn(delta, shift), jnp.zeros_like(delta)) if shift else delta
+                sd_two[tap * out : (tap + 1) * out, here] = block
 
         for h in range(halves):
             here = slice(h * LANES, (h + 1) * LANES)
-            zero = jnp.zeros((out, LANES), F32)
+            zero = jnp.zeros((out, LANES), BF16)
             after = deltas[h + 1] if h < halves - 1 else zero
             before = deltas[h - 1] if h else zero
-            d_two[:out, here] = turn(jnp.where(lane < low, after, deltas[h]), low).astype(BF16)
-            d_two[out : 2 * out, here] = deltas[h].astype(BF16)
-            d_two[2 * out :, here] = turn(jnp.where(lane >= LANES - low, before, deltas[h]), -low).astype(BF16)
+            d_two[:out, here] = turn(jnp.where(lane < low, after, deltas[h]), low)
+            d_two[out : 2 * out, here] = deltas[h]
+            d_two[2 * out :, here] = turn(jnp.where(lane >= LANES - low, before, deltas[h]), -low)
 
         u_two[...] = dot(back_ref[...], sd_two[...])
         spreads = []
@@ -309,25 +310,79 @@
     out_ref[rows - ROWS :, :] = split_again(total[rows - ROWS :], plan, last_chunk(plan)).astype(BF16)
 
 
-def unpack_kernel(plan, *refs):
-    one_ref, bias_one_ref, two_ref, bias_two_ref, all_ref = refs[-5:]
+def chunk_in(plan, side, k):
+    half = own_half(plan) ^ side
+    return half * plan.groups + (place_in(plan, half) ^ k)
+
+
+def leave_taps(plan, places, refs, held, two_ref, sems):
+    rows = plan.chunk
+    full, rest = 27 * plan.mid // rows, 27 * plan.mid % rows
+
+    def each(act):
+        for i, place in enumerate(places):
+
+            @pl.when(place < full)
+            def _(i=i, place=place):
+                target = two_ref.at[pl.ds(pl.multiple_of(place * rows, ROWS), rows)]
+                act(pltpu.make_async_copy(held.at[i], target, sems.at[i]))
+
+            if rest:
+
+                @pl.when(place == full)
+                def _(i=i):
+                    target = two_ref.at[full * rows : full * rows + rest]
+                    act(pltpu.make_async_copy(held.at[i, :rest], target, sems.at[i]))
+
+    for i, ref in enumerate(refs):
+        held[i] = ref[...].astype(F32)
+    each(lambda copy: copy.start())
+    return lambda: each(lambda copy: copy.wait())
+
+
+def early_kernel(plan, names, *refs):
+    two_ref, held, sems = refs[-3:]
+    places = [chunk_in(plan, side, k) for side, k in names]
+    leave_taps(plan, places, refs[:-3], held, two_ref, sems)()
+
+
+def unpack_kernel(plan, names, late, *refs):
+    count = len(names)
+    chunks, refs = refs[:count], refs[count + 1 :]
+    two_ref, one_ref, bias_one_ref, bias_two_ref, held, sums, one_buf, bias_one, bias_two, sems = refs
     inner, mid, out = plan.inner, plan.mid, plan.out
-    own = own_half(plan)
-    for k, ref in enumerate(refs[:-5]):
-        side, k = k // plan.groups, k % plan.groups
-        start = ((own ^ side) * plan.groups + (place_in(plan, own ^ side) ^ gray(k))) * plan.chunk
-        all_ref[pl.ds(pl.multiple_of(start, ROWS), plan.chunk), :] = ref[...].astype(F32)
-    total, first = 27 * mid, 9 * inner
-    two_ref[...] = all_ref[:total, :].reshape(27, mid, out)
-    pair = all_ref[total : total + first, :]
-    one_ref[0:9] = pair[:, :mid].reshape(9, inner, mid)
-    one_ref[9:18] = pair[:, mid:].reshape(9, inner, mid)
-    pair = all_ref[total + first : total + first + first // 2, :]
+    places = [chunk_in(plan, side, k) for side, k in names]
+    finish = leave_taps(plan, places[count - late :], chunks[count - late :], held, two_ref, sems)
+    full = 27 * mid // plan.chunk
+    for ref, place in zip(chunks, places):
+
+        @pl.when(place >= full)
+        def _(ref=ref, place=place):
+            start = pl.multiple_of((place - full) * plan.chunk, ROWS)
+            sums[pl.ds(start, plan.chunk), :] = ref[...].astype(F32)
+
+    total, first, end = 27 * mid - full * plan.chunk, 9 * inner, plan.total - full * plan.chunk
+    copies = []
+
+    def leave(source, target):
+        copies.append(pltpu.make_async_copy(source, target, sems.at[late + len(copies)]))
+        copies[-1].start()
+
+    pair = sums[total : total + first, :]
+    one_buf[0:9] = pair[:, :mid].reshape(9, inner, mid)
+    one_buf[9:18] = pair[:, mid:].reshape(9, inner, mid)
+    pair = sums[total + first : total + first + first // 2, :]
     pair = jnp.concatenate([pair[:, :mid], pair[:, mid:]], axis=0)
-    one_ref[18:27] = pair.reshape(9, inner, mid)
-    tail = all_ref[plan.total - ROWS : plan.total - ROWS // 2, :] + all_ref[plan.total - ROWS // 2 : plan.total, :]
-    bias_two_ref[...] = tail[0:1, :out]
-    bias_one_ref[...] = tail[1:2, :mid]
+    one_buf[18:27] = pair.reshape(9, inner, mid)
+    leave(one_buf, one_ref)
+    tail = sums[end - ROWS : end - ROWS // 2, :] + sums[end - ROWS // 2 : end, :]
+    bias_two[...] = tail[0:1, :out]
+    bias_one[...] = tail[1:2, :mid]
+    leave(bias_two, bias_two_ref)
+    leave(bias_one, bias_one_ref)
+    finish()
+    for copy in copies:
+        copy.wait()
 
 
 class Plan:
@@ -427,15 +482,40 @@
     (whole,) = call(space_sum_kernel, plan, "space_sum", ((chunk, BF16),), partial, *gots)
     mine = [whole] + [trade(plan, whole, gray(k), True) for k in range(1, plan.groups)]
     other = [swap(value, "sample", 1) for value in mine]
-    one, bias_one, two, bias_two = call(
-        unpack_kernel,
-        plan,
-        "unpack",
-        (((27, inner, mid), F32), ((1, mid), F32), ((27, mid, out), F32), ((1, out), F32)),
-        *mine,
-        *other,
-        scratch=(((plan.total, LANES), F32),),
-    )
+    order = [gray(k) for k in range(plan.groups)]
+    late = plan.groups // 2
+    names = [(0, k) for k in order] + [(1, order[0])] + [(1, k) for k in reversed(order[1:])]
+    chunks = [*mine, other[0], *reversed(other[1:])]
+    soon = len(chunks) - late
+    far = pl.BlockSpec(memory_space=pl.ANY)
+    early = pl.pallas_call(
+        functools.partial(early_kernel, plan, names[:soon]),
+        out_shape=jax.ShapeDtypeStruct((27 * mid, out), F32),
+        in_specs=[vmem()] * soon,
+        out_specs=far,
+        scratch_shapes=[pltpu.VMEM((soon, *chunk), F32), pltpu.SemaphoreType.DMA((soon,))],
+        compiler_params=pltpu.CompilerParams(vmem_limit_bytes=SMALL_LIMIT),
+        name="early",
+    )(*chunks[:soon])
+    last = plan.total - 27 * mid // plan.chunk * plan.chunk
+    two, one, bias_one, bias_two = pl.pallas_call(
+        functools.partial(unpack_kernel, plan, names, late),
+        out_shape=[jax.ShapeDtypeStruct(s, F32) for s in ((27 * mid, out), (27, inner, mid), (1, mid), (1, out))],
+        in_specs=[vmem()] * len(chunks) + [far],
+        out_specs=[far] * 4,
+        scratch_shapes=[
+            pltpu.VMEM((late, *chunk), F32),
+            pltpu.VMEM((last, LANES), F32),
+            pltpu.VMEM((27, inner, mid), F32),
+            pltpu.VMEM((1, mid), F32),
+            pltpu.VMEM((1, out), F32),
+            pltpu.SemaphoreType.DMA((late + 3,)),
+        ],
+        input_output_aliases={len(chunks): 0},
+        compiler_params=pltpu.CompilerParams(vmem_limit_bytes=SMALL_LIMIT),
+        name="unpack",
+    )(*chunks, early)
+    two = two.reshape(27, mid, out)
     return (features, jnp.swapaxes(one, 1, 2), bias_one.reshape(mid), jnp.swapaxes(two, 1, 2), bias_two.reshape(out))
 
 

time: 39.4 us -> 39.2 us (level)
  waiting for transfers between devices: 13.7 us -> 12.7 us
  Pallas kernels: 5.08 us -> 5.81 us
    pallas_call x0 -> x2, Pallas kernels: none -> 1.97 us  [the longest x1 1.01 us: on_device(): pl.pallas_call(functools.partial(unpack_kernel, plan, names, late), out_s...]
    pallas_call x5 -> x4, Pallas kernels: 4.65 us -> 3.41 us  [call(): pl.pallas_call(functools.partial(kernel, plan), out_shape=[jax.ShapeDtype...]
    ppermute x8, waiting for transfers between devices: 4.78 us -> 3.81 us  [swap(): lax.ppermute(value, axis, [(i, i ^ k) for i in range(lax.axis_size(axis))])]
  transfers between devices with their start and end apart: 17 -> 17, of which waited for: 11 -> 10; matrix products, arithmetic and copies ran while one was open for 0% -> 0% of each run, Pallas kernels for 1% -> 4%
where the time goes in v5:
time: 39.2 us; the launch traced here: 39 us
  starting transfers between devices  17.2 us (44%)
  waiting for transfers between devices  12.7 us (32%)
  Pallas kernels  5.81 us (15%)
  local copies, waits for them, and re-layouts  2.57 us (7%)
  between operations  0.73 us (2%)
    ppermute x9, starting transfers between devices, trade(): return lax.ppermute(value, ('sample', 'space'), pairs)  9.53 us
    ppermute x9, waiting for transfers between devices, trade(): return lax.ppermute(value, ('sample', 'space'), pairs)  8.89 us
    ppermute x8, starting transfers between devices, swap(): lax.ppermute(value, axis, [(i, i ^ k) for i in range(lax.axis_size(axis))])  7.63 us
    ppermute x8, waiting for transfers between devices, swap(): lax.ppermute(value, axis, [(i, i ^ k) for i in range(lax.axis_size(axis))])  3.81 us
    pallas_call x4, Pallas kernels, call(): pl.pallas_call(functools.partial(kernel, plan), out_shape=[jax.ShapeDtype...  3.41 us
    unnamed x10, local copies, waits for them, and re-layouts  1.69 us
    pallas_call x1, Pallas kernels, on_device(): pl.pallas_call(functools.partial(unpack_kernel, plan, names, late), out_s...  1.01 us
    pallas_call x1, Pallas kernels, on_device(): pl.pallas_call(functools.partial(early_kernel, plan, names[:soon]), out_s...  0.96 us
  transfers between devices with their start and end apart: 17, of which 10 were waited for; matrix products, arithmetic and copies ran while one was open for 0% of the time, Pallas kernels for 4%

profile of v5, /device:TPU:0, one launch (start us, length us, event | category | flops | bytes accessed | tf_op | source)
XLA Modules:
  0.0 39.0 jit_solution(12468282622798017349)
XLA Ops:
  0.6 0.0 copy-start.1
  0.7 0.9 %constant_dynamic-slice_fusion = (bf16[1,32,512]{2,1,0:T(8,128)(2,1)S(1)}, bf16[1,32,512]{2,1,0:T(8,128)(2,1)S(1)}, bf16[1,32,512]{2,1,0:T(8,128)(2,1)S(1)}, bf16[1,32,512]{2,1,0:T(8,128)(2,1)S(1)}) fusion(bf16[4,32,512]{2,1,0:T(8,128)(2,1)} %param.6, s32[]{:T(128)S(6)} %select_n.15, s32[]{:T(128)S(6)} %select_n.13, s32[]{:T(128)S(6)} %select_n.12, s32[]{:T(128)S(6)} %select_n.14), kind=kLoop, calls=%fused_computation | loop fusion | bytes 262160 | tf_op jit(solution)/shard_map/dynamic_slice | solution.py:445
  1.5 4.1 %collective-permute-start.1 = (bf16[1,32,512]{2,1,0:T(8,128)(2,1)S(1)}, bf16[1,32,512]{2,1,0:T(8,128)(2,1)S(1)}, u32[]{:S(2)}, u32[]{:S(2)}) collective-permute-start(bf16[1,32,512]{2,1,0:T(8,128)(2,1)S(1)} %get-tuple-element.38), channel_id=1, source_target_pairs={{0,2},{1,3},{2,0},{3,1},{4,6},{5,7},{6,4},{7,5},{8,10},{9,11},{10,... | collective-permute-start | bytes 98312 | tf_op jit(solution)/shard_map/ppermute | solution.py:421
  5.6 1.3 %collective-permute-start = (bf16[1,32,512]{2,1,0:T(8,128)(2,1)S(1)}, bf16[1,32,512]{2,1,0:T(8,128)(2,1)S(1)}, u32[]{:S(2)}, u32[]{:S(2)}) collective-permute-start(bf16[1,32,512]{2,1,0:T(8,128)(2,1)S(1)} %get-tuple-element.39), channel_id=1, source_target_pairs={{0,3},{1,2},{2,1},{3,0},{4,7},{5,6},{6,5},{7,4},{8,11},{9,10},{10,... | collective-permute-start | bytes 98312 | tf_op jit(solution)/shard_map/ppermute | solution.py:421
  7.0 0.2 collective-permute-start.2
  7.2 0.0 copy-start.3
  7.2 0.0 copy-start.4
  7.2 0.0 copy-done.1
  7.2 0.6 %copy-done.3 = f32[64]{0:T(128)S(1)} copy-done((f32[64]{0:T(128)S(1)}, f32[64]{0:T(128)}, u32[]{:S(2)}) %copy-start.3) | copy-done | bytes 280
  7.9 0.0 copy-done.4
  7.9 1.0 %copy-done = bf16[27,128,64]{1,2,0:T(8,128)(2,1)S(1)} copy-done((bf16[27,128,64]{1,2,0:T(8,128)(2,1)S(1)}, bf16[27,128,64]{1,2,0:T(8,128)(2,1)}, u32[]{:S(2)}) %copy-start) | copy-done | bytes 442392
  8.9 0.4 %weights.1 = (bf16[192,288]{1,0:T(8,128)(2,1)S(1)}, bf16[384,576]{1,0:T(8,128)(2,1)S(1)}, bf16[192,1152]{1,0:T(8,128)(2,1)S(1)}, f32[64,128]{1,0:T(8,128)S(1)}, f32[128,128]{1,0:T(8,128)S(1)}) custom-call(bf16[27,32,64]{2,1,0:T(8,128)(2,1)S(1)} %bitcast.11, bf16[27,64,128]{2,1,0:T(8,128)(2,1)S(1)} %bitcast.10, f32[1,64]{1,0:T(1,128)S(1)} %bitcast.12, ...), custom_call_target="tpu_custom_call" | custom-call | tf_op jit(solution)/shard_map/weights/pallas_call | solution.py:101
  9.3 0.0 collective-permute-done.1.refs_1_
  9.4 2.0 %collective-permute-done.refs_0_ = bf16[1,32,512]{2,1,0:T(8,128)(2,1)S(1)} collective-permute-done((bf16[1,32,512]{2,1,0:T(8,128)(2,1)S(1)}, bf16[1,32,512]{2,1,0:T(8,128)(2,1)S(1)}, u32[]{:S(2)}, u32[]{:S(2)}) %collective-permute-start) | collective-permute-done | bytes 32800 | tf_op jit(solution)/shard_map/ppermute | solution.py:421
  11.4 0.0 collective-permute-done.2.refs_2_
  11.4 0.0 copy-done.2
  11.4 3.2 %main.1 = (bf16[1,128,256]{2,1,0:T(8,128)(2,1)}, f32[1088,128]{1,0:T(8,128)S(1)}, bf16[1088,128]{1,0:T(8,128)(2,1)S(1)}) custom-call(bf16[1,32,512]{2,1,0:T(8,128)(2,1)S(1)} %collective-permute-done.refs_0_, bf16[1,32,512]{2,1,0:T(8,128)(2,1)S(1)} %collective-permute-done.1.refs_1_, bf16[1,32,512]{2,1,0:T(8,128)(2,1)S(1)} %collective-permute-done.2.refs_2_, ...), custom_call_target="tpu_custom_call" | custom-call | tf_op jit(solution)/shard_map/main/pallas_call | solution.py:409
  14.6 0.1 collective-permute-start.3
  14.7 1.5 %collective-permute-done.3.got_ref = bf16[1088,128]{1,0:T(8,128)(2,1)S(1)} collective-permute-done((bf16[1088,128]{1,0:T(8,128)(2,1)S(1)}, bf16[1088,128]{1,0:T(8,128)(2,1)S(1)}, u32[]{:S(2)}, u32[]{:S(2)}) %collective-permute-start.3) | collective-permute-done | bytes 278560 | tf_op jit(solution)/shard_map/ppermute | solution.py:421
  16.2 0.1 core_sum.1
  16.3 1.3 %collective-permute-start.4 = (bf16[272,128]{1,0:T(8,128)(2,1)S(1)}, bf16[272,128]{1,0:T(8,128)(2,1)S(1)}, u32[]{:S(2)}, u32[]{:S(2)}) collective-permute-start(bf16[272,128]{1,0:T(8,128)(2,1)S(1)} %get-tuple-element.30), channel_id=1, source_target_pairs={{0,20},{1,21},{2,22},{3,23},{4,6},{5,7},{6,4},{7,5},{8,10},{9,11},... | collective-permute-start | bytes 208904 | tf_op jit(solution)/shard_map/ppermute | solution.py:436
  17.6 1.4 %collective-permute-start.5 = (bf16[272,128]{1,0:T(8,128)(2,1)S(1)}, bf16[272,128]{1,0:T(8,128)(2,1)S(1)}, u32[]{:S(2)}, u32[]{:S(2)}) collective-permute-start(bf16[272,128]{1,0:T(8,128)(2,1)S(1)} %get-tuple-element.31), channel_id=1, source_target_pairs={{0,24},{1,25},{2,26},{3,27},{4,7},{5,6},{6,5},{7,4},{8,11},{9,10},... | collective-permute-start | bytes 208904 | tf_op jit(solution)/shard_map/ppermute | solution.py:436
  19.1 0.2 collective-permute-start.6
  19.3 0.8 %collective-permute-done.4.rest_0_ = bf16[272,128]{1,0:T(8,128)(2,1)S(1)} collective-permute-done((bf16[272,128]{1,0:T(8,128)(2,1)S(1)}, bf16[272,128]{1,0:T(8,128)(2,1)S(1)}, u32[]{:S(2)}, u32[]{:S(2)}) %collective-permute-start.4) | collective-permute-done | bytes 69664 | tf_op jit(solution)/shard_map/ppermute | solution.py:436
  20.1 2.7 %collective-permute-done.5.rest_1_ = bf16[272,128]{1,0:T(8,128)(2,1)S(1)} collective-permute-done((bf16[272,128]{1,0:T(8,128)(2,1)S(1)}, bf16[272,128]{1,0:T(8,128)(2,1)S(1)}, u32[]{:S(2)}, u32[]{:S(2)}) %collective-permute-start.5) | collective-permute-done | bytes 69664 | tf_op jit(solution)/shard_map/ppermute | solution.py:436
  22.9 0.0 collective-permute-done.6.rest_2_
  22.9 1.3 %collective-permute-start.9 = (bf16[272,128]{1,0:T(8,128)(2,1)S(1)}, bf16[272,128]{1,0:T(8,128)(2,1)S(1)}, u32[]{:S(2)}, u32[]{:S(2)}) collective-permute-start(bf16[272,128]{1,0:T(8,128)(2,1)S(1)} %group_sum.1.refs_0_), channel_id=1, source_target_pairs={{0,2},{1,3},{2,0},{3,1},{4,16},{5,17},{6,18},{7,19},{8,28},{9,29},... | collective-permute-start | bytes 208904 | tf_op jit(solution)/shard_map/ppermute | solution.py:436
  24.2 1.3 %collective-permute-start.8 = (bf16[272,128]{1,0:T(8,128)(2,1)S(1)}, bf16[272,128]{1,0:T(8,128)(2,1)S(1)}, u32[]{:S(2)}, u32[]{:S(2)}) collective-permute-start(bf16[272,128]{1,0:T(8,128)(2,1)S(1)} %group_sum.1.refs_0_), channel_id=1, source_target_pairs={{0,3},{1,2},{2,1},{3,0},{4,28},{5,29},{6,30},{7,31},{8,16},{9,17},... | collective-permute-start | bytes 208904 | tf_op jit(solution)/shard_map/ppermute | solution.py:436
  25.5 0.9 %collective-permute-start.7 = (bf16[272,128]{1,0:T(8,128)(2,1)S(1)}, bf16[272,128]{1,0:T(8,128)(2,1)S(1)}, u32[]{:S(2)}, u32[]{:S(2)}) collective-permute-start(bf16[272,128]{1,0:T(8,128)(2,1)S(1)} %group_sum.1.refs_0_), channel_id=1, source_target_pairs={{0,1},{1,0},{2,3},{3,2},{4,8},{5,9},{6,10},{7,11},{8,4},{9,5},{10,... | collective-permute-start | bytes 208904 | tf_op jit(solution)/shard_map/ppermute | solution.py:436
  26.5 2.1 %collective-permute-done.9.refs_3_ = bf16[272,128]{1,0:T(8,128)(2,1)S(1)} collective-permute-done((bf16[272,128]{1,0:T(8,128)(2,1)S(1)}, bf16[272,128]{1,0:T(8,128)(2,1)S(1)}, u32[]{:S(2)}, u32[]{:S(2)}) %collective-permute-start.9) | collective-permute-done | bytes 69664 | tf_op jit(solution)/shard_map/ppermute | solution.py:436
  28.5 1.9 %collective-permute-done.8.refs_2_ = bf16[272,128]{1,0:T(8,128)(2,1)S(1)} collective-permute-done((bf16[272,128]{1,0:T(8,128)(2,1)S(1)}, bf16[272,128]{1,0:T(8,128)(2,1)S(1)}, u32[]{:S(2)}, u32[]{:S(2)}) %collective-permute-start.8) | collective-permute-done | bytes 69664 | tf_op jit(solution)/shard_map/ppermute | solution.py:436
  30.4 0.1 collective-permute-done.7.refs_1_
  30.6 0.1 collective-permute-start.12
  30.7 1.7 %collective-permute-start.11 = (bf16[272,128]{1,0:T(8,128)(2,1)S(1)}, bf16[272,128]{1,0:T(8,128)(2,1)S(1)}, u32[]{:S(2)}, u32[]{:S(2)}) collective-permute-start(bf16[272,128]{1,0:T(8,128)(2,1)S(1)} %space_sum.1.refs_0_), channel_id=1, source_target_pairs={{0,24},{1,25},{2,26},{3,27},{4,7},{5,6},{6,5},{7,4},{8,11},{9,10},... | collective-permute-start | bytes 208904 | tf_op jit(solution)/shard_map/ppermute | solution.py:436
  32.4 1.2 %collective-permute-start.10 = (bf16[272,128]{1,0:T(8,128)(2,1)S(1)}, bf16[272,128]{1,0:T(8,128)(2,1)S(1)}, u32[]{:S(2)}, u32[]{:S(2)}) collective-permute-start(bf16[272,128]{1,0:T(8,128)(2,1)S(1)} %space_sum.1.refs_0_), channel_id=1, source_target_pairs={{0,12},{1,13},{2,14},{3,15},{4,5},{5,4},{6,7},{7,6},{8,9},{9,8},{1... | collective-permute-start | bytes 208904 | tf_op jit(solution)/shard_map/ppermute | solution.py:436
  33.6 0.0 collective-permute-start.13
  33.6 0.8 %collective-permute-done.12.refs_3_ = bf16[272,128]{1,0:T(8,128)(2,1)S(1)} collective-permute-done((bf16[272,128]{1,0:T(8,128)(2,1)S(1)}, bf16[272,128]{1,0:T(8,128)(2,1)S(1)}, u32[]{:S(2)}, u32[]{:S(2)}) %collective-permute-start.12) | collective-permute-done | bytes 69664 | tf_op jit(solution)/shard_map/ppermute | solution.py:436
  34.4 1.1 %collective-permute-start.14 = (bf16[272,128]{1,0:T(8,128)(2,1)S(1)}, bf16[272,128]{1,0:T(8,128)(2,1)S(1)}, u32[]{:S(2)}, u32[]{:S(2)}) collective-permute-start(bf16[272,128]{1,0:T(8,128)(2,1)S(1)} %collective-permute-done.12.refs_3_), channel_id=1, source_target_pairs={{0,4},{4,0},{8,12},{12,8},{16,20},{20,16},{24,28},{28,24},{1,5},{5... | collective-permute-start | bytes 208904 | tf_op jit(solution)/shard_map/ppermute | solution.py:421
  35.5 0.4 %collective-permute-done.11.refs_2_ = bf16[272,128]{1,0:T(8,128)(2,1)S(1)} collective-permute-done((bf16[272,128]{1,0:T(8,128)(2,1)S(1)}, bf16[272,128]{1,0:T(8,128)(2,1)S(1)}, u32[]{:S(2)}, u32[]{:S(2)}) %collective-permute-start.11) | collective-permute-done | bytes 69664 | tf_op jit(solution)/shard_map/ppermute | solution.py:436
  36.0 0.7 %collective-permute-start.15 = (bf16[272,128]{1,0:T(8,128)(2,1)S(1)}, bf16[272,128]{1,0:T(8,128)(2,1)S(1)}, u32[]{:S(2)}, u32[]{:S(2)}) collective-permute-start(bf16[272,128]{1,0:T(8,128)(2,1)S(1)} %collective-permute-done.11.refs_2_), channel_id=1, source_target_pairs={{0,4},{4,0},{8,12},{12,8},{16,20},{20,16},{24,28},{28,24},{1,5},{5... | collective-permute-start | bytes 208904 | tf_op jit(solution)/shard_map/ppermute | solution.py:421
  36.7 0.0 collective-permute-done.10.refs_1_
  36.7 0.0 collective-permute-start.16
  36.7 0.0 collective-permute-done.13.refs_4_
  36.7 0.0 collective-permute-done.14.refs_5_
  36.7 1.0 %early.1.refs_8_ = f32[1728,128]{1,0:T(8,128)} custom-call(bf16[272,128]{1,0:T(8,128)(2,1)S(1)} %space_sum.1.refs_0_, bf16[272,128]{1,0:T(8,128)(2,1)S(1)} %collective-permute-done.10.refs_1_, bf16[272,128]{1,0:T(8,128)(2,1)S(1)} %collective-permute-done.11.refs_2_, bf16[272,128]{1,0:T(8,128)(2,1)S(1)} %collective-permute-done.12.refs_3_, ...), custom_call_target="tpu_custom_call" | custom-call | tf_op jit(solution)/shard_map/early/pallas_call | solution.py:491
  37.7 0.0 collective-permute-done.15.refs_6_
  37.7 0.2 collective-permute-done.16.refs_7_
  38.0 1.0 %unpack.1 = (f32[1728,128]{1,0:T(8,128)}, f32[27,32,64]{2,1,0:T(8,128)}, f32[1,64]{1,0:T(1,128)}, f32[1,128]{1,0:T(1,128)}) custom-call(bf16[272,128]{1,0:T(8,128)(2,1)S(1)} %space_sum.1.refs_0_, bf16[272,128]{1,0:T(8,128)(2,1)S(1)} %collective-permute-done.10.refs_1_, ...), custom_call_target="tpu_custom_call", output_to_operand_aliasing={{0}: (8, {})} | custom-call | tf_op jit(solution)/shard_map/unpack/pallas_call | solution.py:501
  (4 shorter events, 0.1 us)
Async XLA Ops:
  0.6 6.6 %copy-start.1 = (bf16[27,64,32]{1,2,0:T(8,128)(2,1)S(1)}, bf16[27,64,32]{1,2,0:T(8,128)(2,1)}, u32[]{:S(2)}) copy-start(bf16[27,64,32]{1,2,0:T(8,128)(2,1)} %param.8) | copy-start | bytes 331780
  1.5 7.8 %collective-permute-start.1 = (bf16[1,32,512]{2,1,0:T(8,128)(2,1)S(1)}, bf16[1,32,512]{2,1,0:T(8,128)(2,1)S(1)}, u32[]{:S(2)}, u32[]{:S(2)}) collective-permute-start(bf16[1,32,512]{2,1,0:T(8,128)(2,1)S(1)} %get-tuple-element.38), channel_id=1, source_target_pairs={{0,2},{1,3},{2,0},{3,1},{4,6},{5,7},{6,4},{7,5},{8,10},{9,11},{10,... | collective-permute-start | bytes 98312 | tf_op jit(solution)/shard_map/ppermute | solution.py:421
  5.6 5.7 %collective-permute-start = (bf16[1,32,512]{2,1,0:T(8,128)(2,1)S(1)}, bf16[1,32,512]{2,1,0:T(8,128)(2,1)S(1)}, u32[]{:S(2)}, u32[]{:S(2)}) collective-permute-start(bf16[1,32,512]{2,1,0:T(8,128)(2,1)S(1)} %get-tuple-element.39), channel_id=1, source_target_pairs={{0,3},{1,2},{2,1},{3,0},{4,7},{5,6},{6,5},{7,4},{8,11},{9,10},{10,... | collective-permute-start | bytes 98312 | tf_op jit(solution)/shard_map/ppermute | solution.py:421
  7.0 4.4 %collective-permute-start.2 = (bf16[1,32,512]{2,1,0:T(8,128)(2,1)S(1)}, bf16[1,32,512]{2,1,0:T(8,128)(2,1)S(1)}, u32[]{:S(2)}, u32[]{:S(2)}) collective-permute-start(bf16[1,32,512]{2,1,0:T(8,128)(2,1)S(1)} %get-tuple-element.40), channel_id=1, source_target_pairs={{0,1},{1,0},{2,3},{3,2},{4,5},{5,4},{6,7},{7,6},{8,9},{9,8},{10,11... | collective-permute-start | bytes 98312 | tf_op jit(solution)/shard_map/ppermute | solution.py:421
  7.2 0.7 %copy-start.3 = (f32[64]{0:T(128)S(1)}, f32[64]{0:T(128)}, u32[]{:S(2)}) copy-start(f32[64]{0:T(128)} %param.9) | copy-start | bytes 772
  7.2 0.7 %copy-start.4 = (f32[128]{0:T(128)S(1)}, f32[128]{0:T(128)}, u32[]{:S(2)}) copy-start(f32[128]{0:T(128)} %param.11) | copy-start | bytes 1540
  7.9 1.0 %copy-start = (bf16[27,128,64]{1,2,0:T(8,128)(2,1)S(1)}, bf16[27,128,64]{1,2,0:T(8,128)(2,1)}, u32[]{:S(2)}) copy-start(bf16[27,128,64]{1,2,0:T(8,128)(2,1)} %param.10) | copy-start | bytes 1327108
  8.9 2.5 %copy-start.2 = (bf16[1,128,256]{2,1,0:T(8,128)(2,1)S(1)}, bf16[1,128,256]{2,1,0:T(8,128)(2,1)}, u32[]{:S(2)}) copy-start(bf16[1,128,256]{2,1,0:T(8,128)(2,1)} %refs_4_.1) | copy-start | bytes 196612
  14.6 1.6 %collective-permute-start.3 = (bf16[1088,128]{1,0:T(8,128)(2,1)S(1)}, bf16[1088,128]{1,0:T(8,128)(2,1)S(1)}, u32[]{:S(2)}, u32[]{:S(2)}) collective-permute-start(bf16[1088,128]{1,0:T(8,128)(2,1)S(1)} %get-tuple-element.28), channel_id=1, source_target_pairs={{0,4},{4,0},{8,12},{12,8},{16,20},{20,16},{24,28},{28,24},{1,5},{5... | collective-permute-start | bytes 835592 | tf_op jit(solution)/shard_map/ppermute | solution.py:421
  16.3 3.8 %collective-permute-start.4 = (bf16[272,128]{1,0:T(8,128)(2,1)S(1)}, bf16[272,128]{1,0:T(8,128)(2,1)S(1)}, u32[]{:S(2)}, u32[]{:S(2)}) collective-permute-start(bf16[272,128]{1,0:T(8,128)(2,1)S(1)} %get-tuple-element.30), channel_id=1, source_target_pairs={{0,20},{1,21},{2,22},{3,23},{4,6},{5,7},{6,4},{7,5},{8,10},{9,11},... | collective-permute-start | bytes 208904 | tf_op jit(solution)/shard_map/ppermute | solution.py:436
  17.6 5.2 %collective-permute-start.5 = (bf16[272,128]{1,0:T(8,128)(2,1)S(1)}, bf16[272,128]{1,0:T(8,128)(2,1)S(1)}, u32[]{:S(2)}, u32[]{:S(2)}) collective-permute-start(bf16[272,128]{1,0:T(8,128)(2,1)S(1)} %get-tuple-element.31), channel_id=1, source_target_pairs={{0,24},{1,25},{2,26},{3,27},{4,7},{5,6},{6,5},{7,4},{8,11},{9,10},... | collective-permute-start | bytes 208904 | tf_op jit(solution)/shard_map/ppermute | solution.py:436
  19.1 3.8 %collective-permute-start.6 = (bf16[272,128]{1,0:T(8,128)(2,1)S(1)}, bf16[272,128]{1,0:T(8,128)(2,1)S(1)}, u32[]{:S(2)}, u32[]{:S(2)}) collective-permute-start(bf16[272,128]{1,0:T(8,128)(2,1)S(1)} %get-tuple-element.32), channel_id=1, source_target_pairs={{0,12},{1,13},{2,14},{3,15},{4,5},{5,4},{6,7},{7,6},{8,9},{9,8},{1... | collective-permute-start | bytes 208904 | tf_op jit(solution)/shard_map/ppermute | solution.py:436
  22.9 5.6 %collective-permute-start.9 = (bf16[272,128]{1,0:T(8,128)(2,1)S(1)}, bf16[272,128]{1,0:T(8,128)(2,1)S(1)}, u32[]{:S(2)}, u32[]{:S(2)}) collective-permute-start(bf16[272,128]{1,0:T(8,128)(2,1)S(1)} %group_sum.1.refs_0_), channel_id=1, source_target_pairs={{0,2},{1,3},{2,0},{3,1},{4,16},{5,17},{6,18},{7,19},{8,28},{9,29},... | collective-permute-start | bytes 208904 | tf_op jit(solution)/shard_map/ppermute | solution.py:436
  24.2 6.2 %collective-permute-start.8 = (bf16[272,128]{1,0:T(8,128)(2,1)S(1)}, bf16[272,128]{1,0:T(8,128)(2,1)S(1)}, u32[]{:S(2)}, u32[]{:S(2)}) collective-permute-start(bf16[272,128]{1,0:T(8,128)(2,1)S(1)} %group_sum.1.refs_0_), channel_id=1, source_target_pairs={{0,3},{1,2},{2,1},{3,0},{4,28},{5,29},{6,30},{7,31},{8,16},{9,17},... | collective-permute-start | bytes 208904 | tf_op jit(solution)/shard_map/ppermute | solution.py:436
  25.5 5.1 %collective-permute-start.7 = (bf16[272,128]{1,0:T(8,128)(2,1)S(1)}, bf16[272,128]{1,0:T(8,128)(2,1)S(1)}, u32[]{:S(2)}, u32[]{:S(2)}) collective-permute-start(bf16[272,128]{1,0:T(8,128)(2,1)S(1)} %group_sum.1.refs_0_), channel_id=1, source_target_pairs={{0,1},{1,0},{2,3},{3,2},{4,8},{5,9},{6,10},{7,11},{8,4},{9,5},{10,... | collective-permute-start | bytes 208904 | tf_op jit(solution)/shard_map/ppermute | solution.py:436
  30.6 3.8 %collective-permute-start.12 = (bf16[272,128]{1,0:T(8,128)(2,1)S(1)}, bf16[272,128]{1,0:T(8,128)(2,1)S(1)}, u32[]{:S(2)}, u32[]{:S(2)}) collective-permute-start(bf16[272,128]{1,0:T(8,128)(2,1)S(1)} %space_sum.1.refs_0_), channel_id=1, source_target_pairs={{0,20},{1,21},{2,22},{3,23},{4,6},{5,7},{6,4},{7,5},{8,10},{9,11},... | collective-permute-start | bytes 208904 | tf_op jit(solution)/shard_map/ppermute | solution.py:436
  30.7 5.3 %collective-permute-start.11 = (bf16[272,128]{1,0:T(8,128)(2,1)S(1)}, bf16[272,128]{1,0:T(8,128)(2,1)S(1)}, u32[]{:S(2)}, u32[]{:S(2)}) collective-permute-start(bf16[272,128]{1,0:T(8,128)(2,1)S(1)} %space_sum.1.refs_0_), channel_id=1, source_target_pairs={{0,24},{1,25},{2,26},{3,27},{4,7},{5,6},{6,5},{7,4},{8,11},{9,10},... | collective-permute-start | bytes 208904 | tf_op jit(solution)/shard_map/ppermute | solution.py:436
  32.4 4.3 %collective-permute-start.10 = (bf16[272,128]{1,0:T(8,128)(2,1)S(1)}, bf16[272,128]{1,0:T(8,128)(2,1)S(1)}, u32[]{:S(2)}, u32[]{:S(2)}) collective-permute-start(bf16[272,128]{1,0:T(8,128)(2,1)S(1)} %space_sum.1.refs_0_), channel_id=1, source_target_pairs={{0,12},{1,13},{2,14},{3,15},{4,5},{5,4},{6,7},{7,6},{8,9},{9,8},{1... | collective-permute-start | bytes 208904 | tf_op jit(solution)/shard_map/ppermute | solution.py:436
  33.6 3.1 %collective-permute-start.13 = (bf16[272,128]{1,0:T(8,128)(2,1)S(1)}, bf16[272,128]{1,0:T(8,128)(2,1)S(1)}, u32[]{:S(2)}, u32[]{:S(2)}) collective-permute-start(bf16[272,128]{1,0:T(8,128)(2,1)S(1)} %space_sum.1.refs_0_), channel_id=1, source_target_pairs={{0,4},{4,0},{8,12},{12,8},{16,20},{20,16},{24,28},{28,24},{1,5},{5... | collective-permute-start | bytes 208904 | tf_op jit(solution)/shard_map/ppermute | solution.py:421
  34.4 2.3 %collective-permute-start.14 = (bf16[272,128]{1,0:T(8,128)(2,1)S(1)}, bf16[272,128]{1,0:T(8,128)(2,1)S(1)}, u32[]{:S(2)}, u32[]{:S(2)}) collective-permute-start(bf16[272,128]{1,0:T(8,128)(2,1)S(1)} %collective-permute-done.12.refs_3_), channel_id=1, source_target_pairs={{0,4},{4,0},{8,12},{12,8},{16,20},{20,16},{24,28},{28,24},{1,5},{5... | collective-permute-start | bytes 208904 | tf_op jit(solution)/shard_map/ppermute | solution.py:421
  36.0 1.7 %collective-permute-start.15 = (bf16[272,128]{1,0:T(8,128)(2,1)S(1)}, bf16[272,128]{1,0:T(8,128)(2,1)S(1)}, u32[]{:S(2)}, u32[]{:S(2)}) collective-permute-start(bf16[272,128]{1,0:T(8,128)(2,1)S(1)} %collective-permute-done.11.refs_2_), channel_id=1, source_target_pairs={{0,4},{4,0},{8,12},{12,8},{16,20},{20,16},{24,28},{28,24},{1,5},{5... | collective-permute-start | bytes 208904 | tf_op jit(solution)/shard_map/ppermute | solution.py:421
  36.7 1.3 %collective-permute-start.16 = (bf16[272,128]{1,0:T(8,128)(2,1)S(1)}, bf16[272,128]{1,0:T(8,128)(2,1)S(1)}, u32[]{:S(2)}, u32[]{:S(2)}) collective-permute-start(bf16[272,128]{1,0:T(8,128)(2,1)S(1)} %collective-permute-done.10.refs_1_), channel_id=1, source_target_pairs={{0,4},{4,0},{8,12},{12,8},{16,20},{20,16},{24,28},{28,24},{1,5},{5... | collective-permute-start | bytes 208904 | tf_op jit(solution)/shard_map/ppermute | solution.py:421

commit v6 on v5

--- a/solution.py
+++ b/solution.py
@@ -113,8 +113,8 @@
         refs[: plan.space],
         *refs[plan.space : plan.space + 6],
     )
-    feat_ref, keep_ref, send_ref = refs[plan.space + 6 : plan.space + 9]
-    x_ref, s_one, t_one, slope_ref, lk_ref, d_one, s_two, t_two, d_two, sd_two, u_two, pay_ref = refs[plan.space + 9 :]
+    feat_ref, keep_ref, ahead_ref, send_ref = refs[plan.space + 6 : plan.space + 10]
+    x_ref, s_one, t_one, slope_ref, lk_ref, d_one, s_two, t_two, d_two, sd_two, u_two, pay_ref = refs[plan.space + 10 :]
     inner, mid, out = plan.inner, plan.mid, plan.out
     blocks, halves = plan.blocks, plan.halves
     place, own_core = lax.axis_index("space"), own_half(plan)
@@ -258,7 +258,14 @@
 
     share = plan.total // plan.cores
     keep_ref[...] = pay_ref[pl.ds(pl.multiple_of(own_core * share, ROWS), share), :]
-    send_ref[...] = pay_ref[pl.ds(pl.multiple_of((1 - own_core) * share, ROWS), share), :].astype(BF16)
+    there = place_in(plan, 1 - own_core)
+    for i, k in enumerate(plan.steps):
+        start = (1 - own_core) * share + (there ^ k) * plan.chunk
+        value = pay_ref[pl.ds(pl.multiple_of(start, ROWS), plan.chunk), :].astype(BF16)
+        if k:
+            ahead_ref[i * plan.chunk : (i + 1) * plan.chunk, :] = value
+        else:
+            send_ref[...] = value
 
 
 def split_again(values, plan, last):
@@ -269,20 +276,17 @@
     return jnp.where(last, parted, values[rows - ROWS :])
 
 
-def core_sum_kernel(plan, keep_ref, got_ref, own_ref, *rest):
-    sends, sum_ref = rest[:-1], rest[-1]
+def core_sum_kernel(plan, steps, keep_ref, got_ref, *outs):
     half = own_half(plan)
     place = place_in(plan, half)
-    rows = keep_ref.shape[0]
-    sum_ref[...] = keep_ref[...] + got_ref[...].astype(F32)
-    sum_ref[rows - ROWS :, :] = split_again(sum_ref[rows - ROWS :, :], plan, half == plan.cores - 1)
-
-    def chunk(k):
-        return sum_ref[pl.ds(pl.multiple_of((place ^ k) * plan.chunk, ROWS), plan.chunk), :]
-
-    own_ref[...] = chunk(0)
-    for k, send in enumerate(sends, start=1):
-        send[...] = chunk(k).astype(BF16)
+    rows = plan.chunk
+    for i, (k, out_ref) in enumerate(zip(steps, outs)):
+        there = place ^ k
+        mine = keep_ref[pl.ds(pl.multiple_of(there * rows, ROWS), rows), :]
+        total = mine + got_ref[i * rows : (i + 1) * rows, :].astype(F32)
+        last = (half == plan.cores - 1) & (there == plan.groups - 1)
+        out_ref[: rows - ROWS, :] = total[: rows - ROWS].astype(out_ref.dtype)
+        out_ref[rows - ROWS :, :] = split_again(total[rows - ROWS :], plan, last).astype(out_ref.dtype)
 
 
 def last_chunk(plan):
@@ -395,6 +399,7 @@
         self.halves = self.blocks // 8
         self.cores = 2
         self.groups = self.sample // self.cores
+        self.steps = [*range(1, self.groups), 0]
         self.crossed = self.groups == self.space
         cells = self.blocks * LANES * volumes.shape[0] * self.sample
         self.scale_one = 1.0 / math.sqrt(cells)
@@ -462,11 +467,11 @@
         ((3 * mid, small), F32),
         ((plan.total, LANES), F32),
     )
-    features, keep, send = call(
+    features, keep, ahead, send = call(
         main_kernel,
         plan,
         "main",
-        (((plan.owned, out, small), BF16), ((share, LANES), F32), ((share, LANES), BF16)),
+        (((plan.owned, out, small), BF16), ((share, LANES), F32), ((share - plan.chunk, LANES), BF16), ((plan.chunk, LANES), BF16)),
         *reversed(parts),
         grad_out,
         *weights,
@@ -474,8 +479,20 @@
         limit=48 * 1024 * 1024,
     )
     chunk = (plan.chunk, LANES)
-    got = swap(send, "sample", 1)
-    own, *sends = call(core_sum_kernel, plan, "core_sum", ((chunk, F32),) + ((chunk, BF16),) * (plan.groups - 1), keep, got, scratch=(((share, LANES), F32),))
+    got_ahead, got = swap(ahead, "sample", 1), swap(send, "sample", 1)
+    steps = plan.steps
+    summed = {}
+    for part, value in ((steps[:-1], got_ahead), (steps[-1:], got)):
+        sums = call(
+            lambda plan, *refs, part=part: core_sum_kernel(plan, part, *refs),
+            plan,
+            "core_sum",
+            [(chunk, BF16 if k else F32) for k in part],
+            keep,
+            value,
+        )
+        summed.update(zip(part, sums))
+    own, sends = summed[0], [summed[k] for k in range(1, plan.groups)]
     gots = [trade(plan, s, k, True) for k, s in enumerate(sends, start=1)]
     (partial,) = call(group_sum_kernel, plan, "group_sum", ((chunk, BF16),), own, *gots[1:], gots[0])
     gots = [trade(plan, partial, gray(k), False) for k in range(1, plan.space)]

time: 39.2 us -> 39 us (level)
  waiting for transfers between devices: 12.7 us -> 12.1 us
  starting transfers between devices: 17.2 us -> 17.7 us
    ppermute x8 -> x9, waiting for transfers between devices: 3.81 us -> 3.21 us  [swap(): lax.ppermute(value, axis, [(i, i ^ k) for i in range(lax.axis_size(axis))])]
    ppermute x8 -> x9, starting transfers between devices: 7.63 us -> 8.13 us  [swap(): lax.ppermute(value, axis, [(i, i ^ k) for i in range(lax.axis_size(axis))])]
    pallas_call x4 -> x5, Pallas kernels: 3.41 us -> 3.42 us  [call(): pl.pallas_call(functools.partial(kernel, plan), out_shape=[jax.ShapeDtype...]
  transfers between devices with their start and end apart: 17 -> 18, of which waited for: 10 -> 10; matrix products, arithmetic and copies ran while one was open for 0% -> 0% of each run, Pallas kernels for 4% -> 4%
where the time goes in v6:
time: 39 us; the launch traced here: 38.8 us
  starting transfers between devices  17.7 us (45%)
  waiting for transfers between devices  12.1 us (31%)
  Pallas kernels  5.82 us (15%)
  local copies, waits for them, and re-layouts  2.57 us (7%)
  between operations  0.74 us (2%)
    ppermute x9, starting transfers between devices, trade(): return lax.ppermute(value, ('sample', 'space'), pairs)  9.53 us
    ppermute x9, waiting for transfers between devices, trade(): return lax.ppermute(value, ('sample', 'space'), pairs)  8.84 us
    ppermute x9, starting transfers between devices, swap(): lax.ppermute(value, axis, [(i, i ^ k) for i in range(lax.axis_size(axis))])  8.13 us
    pallas_call x5, Pallas kernels, call(): pl.pallas_call(functools.partial(kernel, plan), out_shape=[jax.ShapeDtype...  3.42 us
    ppermute x9, waiting for transfers between devices, swap(): lax.ppermute(value, axis, [(i, i ^ k) for i in range(lax.axis_size(axis))])  3.21 us
    unnamed x10, local copies, waits for them, and re-layouts  1.69 us
    pallas_call x1, Pallas kernels, on_device(): pl.pallas_call(functools.partial(unpack_kernel, plan, names, late), out_s...  1.01 us
    pallas_call x1, Pallas kernels, on_device(): pl.pallas_call(functools.partial(early_kernel, plan, names[:soon]), out_s...  0.96 us
  transfers between devices with their start and end apart: 18, of which 10 were waited for; matrix products, arithmetic and copies ran while one was open for 0% of the time, Pallas kernels for 4%

profile of v6, /device:TPU:0, one launch (start us, length us, event | category | flops | bytes accessed | tf_op | source)
XLA Modules:
  0.0 38.8 jit_solution(13044319905758435730)
XLA Ops:
  0.6 0.0 copy-start.1
  0.7 0.9 %constant_dynamic-slice_fusion = (bf16[1,32,512]{2,1,0:T(8,128)(2,1)S(1)}, bf16[1,32,512]{2,1,0:T(8,128)(2,1)S(1)}, bf16[1,32,512]{2,1,0:T(8,128)(2,1)S(1)}, bf16[1,32,512]{2,1,0:T(8,128)(2,1)S(1)}) fusion(bf16[4,32,512]{2,1,0:T(8,128)(2,1)} %param.6, s32[]{:T(128)S(6)} %select_n.15, s32[]{:T(128)S(6)} %select_n.13, s32[]{:T(128)S(6)} %select_n.12, s32[]{:T(128)S(6)} %select_n.14), kind=kLoop, calls=%fused_computation | loop fusion | bytes 262160 | tf_op jit(solution)/shard_map/dynamic_slice | solution.py:450
  1.5 4.1 %collective-permute-start.1 = (bf16[1,32,512]{2,1,0:T(8,128)(2,1)S(1)}, bf16[1,32,512]{2,1,0:T(8,128)(2,1)S(1)}, u32[]{:S(2)}, u32[]{:S(2)}) collective-permute-start(bf16[1,32,512]{2,1,0:T(8,128)(2,1)S(1)} %get-tuple-element.38), channel_id=1, source_target_pairs={{0,2},{1,3},{2,0},{3,1},{4,6},{5,7},{6,4},{7,5},{8,10},{9,11},{10,... | collective-permute-start | bytes 98312 | tf_op jit(solution)/shard_map/ppermute | solution.py:426
  5.6 1.3 %collective-permute-start = (bf16[1,32,512]{2,1,0:T(8,128)(2,1)S(1)}, bf16[1,32,512]{2,1,0:T(8,128)(2,1)S(1)}, u32[]{:S(2)}, u32[]{:S(2)}) collective-permute-start(bf16[1,32,512]{2,1,0:T(8,128)(2,1)S(1)} %get-tuple-element.39), channel_id=1, source_target_pairs={{0,3},{1,2},{2,1},{3,0},{4,7},{5,6},{6,5},{7,4},{8,11},{9,10},{10,... | collective-permute-start | bytes 98312 | tf_op jit(solution)/shard_map/ppermute | solution.py:426
  7.0 0.2 collective-permute-start.2
  7.2 0.0 copy-done.1
  7.2 0.6 %copy-done.3 = f32[64]{0:T(128)S(1)} copy-done((f32[64]{0:T(128)S(1)}, f32[64]{0:T(128)}, u32[]{:S(2)}) %copy-start.3) | copy-done | bytes 280
  7.9 0.0 copy-done.4
  7.9 1.0 %copy-done = bf16[27,128,64]{1,2,0:T(8,128)(2,1)S(1)} copy-done((bf16[27,128,64]{1,2,0:T(8,128)(2,1)S(1)}, bf16[27,128,64]{1,2,0:T(8,128)(2,1)}, u32[]{:S(2)}) %copy-start) | copy-done | bytes 442392
  8.9 0.4 %weights.1 = (bf16[192,288]{1,0:T(8,128)(2,1)S(1)}, bf16[384,576]{1,0:T(8,128)(2,1)S(1)}, bf16[192,1152]{1,0:T(8,128)(2,1)S(1)}, f32[64,128]{1,0:T(8,128)S(1)}, f32[128,128]{1,0:T(8,128)S(1)}) custom-call(bf16[27,32,64]{2,1,0:T(8,128)(2,1)S(1)} %bitcast.11, bf16[27,64,128]{2,1,0:T(8,128)(2,1)S(1)} %bitcast.10, f32[1,64]{1,0:T(1,128)S(1)} %bitcast.12, ...), custom_call_target="tpu_custom_call" | custom-call | tf_op jit(solution)/shard_map/weights/pallas_call | solution.py:101
  9.3 0.0 collective-permute-done.1.refs_1_
  9.4 2.0 %collective-permute-done.refs_0_ = bf16[1,32,512]{2,1,0:T(8,128)(2,1)S(1)} collective-permute-done((bf16[1,32,512]{2,1,0:T(8,128)(2,1)S(1)}, bf16[1,32,512]{2,1,0:T(8,128)(2,1)S(1)}, u32[]{:S(2)}, u32[]{:S(2)}) %collective-permute-start) | collective-permute-done | bytes 32800 | tf_op jit(solution)/shard_map/ppermute | solution.py:426
  11.4 0.0 collective-permute-done.2.refs_2_
  11.4 0.0 copy-done.2
  11.4 3.2 %main.1 = (bf16[1,128,256]{2,1,0:T(8,128)(2,1)}, f32[1088,128]{1,0:T(8,128)S(1)}, bf16[816,128]{1,0:T(8,128)(2,1)S(1)}, bf16[272,128]{1,0:T(8,128)(2,1)S(1)}) custom-call(bf16[1,32,512]{2,1,0:T(8,128)(2,1)S(1)} %collective-permute-done.refs_0_, bf16[1,32,512]{2,1,0:T(8,128)(2,1)S(1)} %collective-permute-done.1.refs_1_, ...), custom_call_target="tpu_custom_call" | custom-call | tf_op jit(solution)/shard_map/main/pallas_call | solution.py:414
  14.6 0.1 collective-permute-start.4
  14.7 0.5 %collective-permute-start.3 = (bf16[272,128]{1,0:T(8,128)(2,1)S(1)}, bf16[272,128]{1,0:T(8,128)(2,1)S(1)}, u32[]{:S(2)}, u32[]{:S(2)}) collective-permute-start(bf16[272,128]{1,0:T(8,128)(2,1)S(1)} %get-tuple-element.28), channel_id=1, source_target_pairs={{0,4},{4,0},{8,12},{12,8},{16,20},{20,16},{24,28},{28,24},{1,5},{5... | collective-permute-start | bytes 208904 | tf_op jit(solution)/shard_map/ppermute | solution.py:426
  15.2 0.9 %collective-permute-done.4.refs_1_ = bf16[816,128]{1,0:T(8,128)(2,1)S(1)} collective-permute-done((bf16[816,128]{1,0:T(8,128)(2,1)S(1)}, bf16[816,128]{1,0:T(8,128)(2,1)S(1)}, u32[]{:S(2)}, u32[]{:S(2)}) %collective-permute-start.4) | collective-permute-done | bytes 208928 | tf_op jit(solution)/shard_map/ppermute | solution.py:426
  16.1 0.1 core_sum.3
  16.2 1.3 %collective-permute-start.5 = (bf16[272,128]{1,0:T(8,128)(2,1)S(1)}, bf16[272,128]{1,0:T(8,128)(2,1)S(1)}, u32[]{:S(2)}, u32[]{:S(2)}) collective-permute-start(bf16[272,128]{1,0:T(8,128)(2,1)S(1)} %get-tuple-element.30), channel_id=1, source_target_pairs={{0,20},{1,21},{2,22},{3,23},{4,6},{5,7},{6,4},{7,5},{8,10},{9,11},... | collective-permute-start | bytes 208904 | tf_op jit(solution)/shard_map/ppermute | solution.py:441
  17.5 1.4 %collective-permute-start.6 = (bf16[272,128]{1,0:T(8,128)(2,1)S(1)}, bf16[272,128]{1,0:T(8,128)(2,1)S(1)}, u32[]{:S(2)}, u32[]{:S(2)}) collective-permute-start(bf16[272,128]{1,0:T(8,128)(2,1)S(1)} %get-tuple-element.31), channel_id=1, source_target_pairs={{0,24},{1,25},{2,26},{3,27},{4,7},{5,6},{6,5},{7,4},{8,11},{9,10},... | collective-permute-start | bytes 208904 | tf_op jit(solution)/shard_map/ppermute | solution.py:441
  19.0 0.2 collective-permute-start.7
  19.2 0.0 collective-permute-done.3.refs_1_
  19.2 0.8 %collective-permute-done.5.rest_0_ = bf16[272,128]{1,0:T(8,128)(2,1)S(1)} collective-permute-done((bf16[272,128]{1,0:T(8,128)(2,1)S(1)}, bf16[272,128]{1,0:T(8,128)(2,1)S(1)}, u32[]{:S(2)}, u32[]{:S(2)}) %collective-permute-start.5) | collective-permute-done | bytes 69664 | tf_op jit(solution)/shard_map/ppermute | solution.py:441
  20.0 2.7 %collective-permute-done.6.rest_1_ = bf16[272,128]{1,0:T(8,128)(2,1)S(1)} collective-permute-done((bf16[272,128]{1,0:T(8,128)(2,1)S(1)}, bf16[272,128]{1,0:T(8,128)(2,1)S(1)}, u32[]{:S(2)}, u32[]{:S(2)}) %collective-permute-start.6) | collective-permute-done | bytes 69664 | tf_op jit(solution)/shard_map/ppermute | solution.py:441
  22.7 0.0 collective-permute-done.7.rest_2_
  22.8 1.3 %collective-permute-start.10 = (bf16[272,128]{1,0:T(8,128)(2,1)S(1)}, bf16[272,128]{1,0:T(8,128)(2,1)S(1)}, u32[]{:S(2)}, u32[]{:S(2)}) collective-permute-start(bf16[272,128]{1,0:T(8,128)(2,1)S(1)} %group_sum.1.refs_0_), channel_id=1, source_target_pairs={{0,2},{1,3},{2,0},{3,1},{4,16},{5,17},{6,18},{7,19},{8,28},{9,29},... | collective-permute-start | bytes 208904 | tf_op jit(solution)/shard_map/ppermute | solution.py:441
  24.1 1.3 %collective-permute-start.9 = (bf16[272,128]{1,0:T(8,128)(2,1)S(1)}, bf16[272,128]{1,0:T(8,128)(2,1)S(1)}, u32[]{:S(2)}, u32[]{:S(2)}) collective-permute-start(bf16[272,128]{1,0:T(8,128)(2,1)S(1)} %group_sum.1.refs_0_), channel_id=1, source_target_pairs={{0,3},{1,2},{2,1},{3,0},{4,28},{5,29},{6,30},{7,31},{8,16},{9,17},... | collective-permute-start | bytes 208904 | tf_op jit(solution)/shard_map/ppermute | solution.py:441
  25.4 0.9 %collective-permute-start.8 = (bf16[272,128]{1,0:T(8,128)(2,1)S(1)}, bf16[272,128]{1,0:T(8,128)(2,1)S(1)}, u32[]{:S(2)}, u32[]{:S(2)}) collective-permute-start(bf16[272,128]{1,0:T(8,128)(2,1)S(1)} %group_sum.1.refs_0_), channel_id=1, source_target_pairs={{0,1},{1,0},{2,3},{3,2},{4,8},{5,9},{6,10},{7,11},{8,4},{9,5},{10,... | collective-permute-start | bytes 208904 | tf_op jit(solution)/shard_map/ppermute | solution.py:441
  26.3 2.1 %collective-permute-done.10.refs_3_ = bf16[272,128]{1,0:T(8,128)(2,1)S(1)} collective-permute-done((bf16[272,128]{1,0:T(8,128)(2,1)S(1)}, bf16[272,128]{1,0:T(8,128)(2,1)S(1)}, u32[]{:S(2)}, u32[]{:S(2)}) %collective-permute-start.10) | collective-permute-done | bytes 69664 | tf_op jit(solution)/shard_map/ppermute | solution.py:441
  28.4 1.9 %collective-permute-done.9.refs_2_ = bf16[272,128]{1,0:T(8,128)(2,1)S(1)} collective-permute-done((bf16[272,128]{1,0:T(8,128)(2,1)S(1)}, bf16[272,128]{1,0:T(8,128)(2,1)S(1)}, u32[]{:S(2)}, u32[]{:S(2)}) %collective-permute-start.9) | collective-permute-done | bytes 69664 | tf_op jit(solution)/shard_map/ppermute | solution.py:441
  30.3 0.1 collective-permute-done.8.refs_1_
  30.5 0.1 collective-permute-start.13
  30.6 1.7 %collective-permute-start.12 = (bf16[272,128]{1,0:T(8,128)(2,1)S(1)}, bf16[272,128]{1,0:T(8,128)(2,1)S(1)}, u32[]{:S(2)}, u32[]{:S(2)}) collective-permute-start(bf16[272,128]{1,0:T(8,128)(2,1)S(1)} %space_sum.1.refs_0_), channel_id=1, source_target_pairs={{0,24},{1,25},{2,26},{3,27},{4,7},{5,6},{6,5},{7,4},{8,11},{9,10},... | collective-permute-start | bytes 208904 | tf_op jit(solution)/shard_map/ppermute | solution.py:441
  32.3 1.2 %collective-permute-start.11 = (bf16[272,128]{1,0:T(8,128)(2,1)S(1)}, bf16[272,128]{1,0:T(8,128)(2,1)S(1)}, u32[]{:S(2)}, u32[]{:S(2)}) collective-permute-start(bf16[272,128]{1,0:T(8,128)(2,1)S(1)} %space_sum.1.refs_0_), channel_id=1, source_target_pairs={{0,12},{1,13},{2,14},{3,15},{4,5},{5,4},{6,7},{7,6},{8,9},{9,8},{1... | collective-permute-start | bytes 208904 | tf_op jit(solution)/shard_map/ppermute | solution.py:441
  33.5 0.0 collective-permute-start.14
  33.5 0.8 %collective-permute-done.13.refs_3_ = bf16[272,128]{1,0:T(8,128)(2,1)S(1)} collective-permute-done((bf16[272,128]{1,0:T(8,128)(2,1)S(1)}, bf16[272,128]{1,0:T(8,128)(2,1)S(1)}, u32[]{:S(2)}, u32[]{:S(2)}) %collective-permute-start.13) | collective-permute-done | bytes 69664 | tf_op jit(solution)/shard_map/ppermute | solution.py:441
  34.3 1.1 %collective-permute-start.15 = (bf16[272,128]{1,0:T(8,128)(2,1)S(1)}, bf16[272,128]{1,0:T(8,128)(2,1)S(1)}, u32[]{:S(2)}, u32[]{:S(2)}) collective-permute-start(bf16[272,128]{1,0:T(8,128)(2,1)S(1)} %collective-permute-done.13.refs_3_), channel_id=1, source_target_pairs={{0,4},{4,0},{8,12},{12,8},{16,20},{20,16},{24,28},{28,24},{1,5},{5... | collective-permute-start | bytes 208904 | tf_op jit(solution)/shard_map/ppermute | solution.py:426
  35.4 0.4 %collective-permute-done.12.refs_2_ = bf16[272,128]{1,0:T(8,128)(2,1)S(1)} collective-permute-done((bf16[272,128]{1,0:T(8,128)(2,1)S(1)}, bf16[272,128]{1,0:T(8,128)(2,1)S(1)}, u32[]{:S(2)}, u32[]{:S(2)}) %collective-permute-start.12) | collective-permute-done | bytes 69664 | tf_op jit(solution)/shard_map/ppermute | solution.py:441
  35.8 0.7 %collective-permute-start.16 = (bf16[272,128]{1,0:T(8,128)(2,1)S(1)}, bf16[272,128]{1,0:T(8,128)(2,1)S(1)}, u32[]{:S(2)}, u32[]{:S(2)}) collective-permute-start(bf16[272,128]{1,0:T(8,128)(2,1)S(1)} %collective-permute-done.12.refs_2_), channel_id=1, source_target_pairs={{0,4},{4,0},{8,12},{12,8},{16,20},{20,16},{24,28},{28,24},{1,5},{5... | collective-permute-start | bytes 208904 | tf_op jit(solution)/shard_map/ppermute | solution.py:426
  36.6 0.0 collective-permute-done.11.refs_1_
  36.6 0.0 collective-permute-start.17
  36.6 0.0 collective-permute-done.14.refs_4_
  36.6 0.0 collective-permute-done.15.refs_5_
  36.6 1.0 %early.1.refs_8_ = f32[1728,128]{1,0:T(8,128)} custom-call(bf16[272,128]{1,0:T(8,128)(2,1)S(1)} %space_sum.1.refs_0_, bf16[272,128]{1,0:T(8,128)(2,1)S(1)} %collective-permute-done.11.refs_1_, bf16[272,128]{1,0:T(8,128)(2,1)S(1)} %collective-permute-done.12.refs_2_, bf16[272,128]{1,0:T(8,128)(2,1)S(1)} %collective-permute-done.13.refs_3_, ...), custom_call_target="tpu_custom_call" | custom-call | tf_op jit(solution)/shard_map/early/pallas_call | solution.py:508
  37.6 0.0 collective-permute-done.16.refs_6_
  37.6 0.2 collective-permute-done.17.refs_7_
  37.8 1.0 %unpack.1 = (f32[1728,128]{1,0:T(8,128)}, f32[27,32,64]{2,1,0:T(8,128)}, f32[1,64]{1,0:T(1,128)}, f32[1,128]{1,0:T(1,128)}) custom-call(bf16[272,128]{1,0:T(8,128)(2,1)S(1)} %space_sum.1.refs_0_, bf16[272,128]{1,0:T(8,128)(2,1)S(1)} %collective-permute-done.11.refs_1_, ...), custom_call_target="tpu_custom_call", output_to_operand_aliasing={{0}: (8, {})} | custom-call | tf_op jit(solution)/shard_map/unpack/pallas_call | solution.py:518
  (7 shorter events, 0.1 us)
Async XLA Ops:
  0.6 6.6 %copy-start.1 = (bf16[27,64,32]{1,2,0:T(8,128)(2,1)S(1)}, bf16[27,64,32]{1,2,0:T(8,128)(2,1)}, u32[]{:S(2)}) copy-start(bf16[27,64,32]{1,2,0:T(8,128)(2,1)} %param.8) | copy-start | bytes 331780
  1.5 7.8 %collective-permute-start.1 = (bf16[1,32,512]{2,1,0:T(8,128)(2,1)S(1)}, bf16[1,32,512]{2,1,0:T(8,128)(2,1)S(1)}, u32[]{:S(2)}, u32[]{:S(2)}) collective-permute-start(bf16[1,32,512]{2,1,0:T(8,128)(2,1)S(1)} %get-tuple-element.38), channel_id=1, source_target_pairs={{0,2},{1,3},{2,0},{3,1},{4,6},{5,7},{6,4},{7,5},{8,10},{9,11},{10,... | collective-permute-start | bytes 98312 | tf_op jit(solution)/shard_map/ppermute | solution.py:426
  5.6 5.7 %collective-permute-start = (bf16[1,32,512]{2,1,0:T(8,128)(2,1)S(1)}, bf16[1,32,512]{2,1,0:T(8,128)(2,1)S(1)}, u32[]{:S(2)}, u32[]{:S(2)}) collective-permute-start(bf16[1,32,512]{2,1,0:T(8,128)(2,1)S(1)} %get-tuple-element.39), channel_id=1, source_target_pairs={{0,3},{1,2},{2,1},{3,0},{4,7},{5,6},{6,5},{7,4},{8,11},{9,10},{10,... | collective-permute-start | bytes 98312 | tf_op jit(solution)/shard_map/ppermute | solution.py:426
  7.0 4.4 %collective-permute-start.2 = (bf16[1,32,512]{2,1,0:T(8,128)(2,1)S(1)}, bf16[1,32,512]{2,1,0:T(8,128)(2,1)S(1)}, u32[]{:S(2)}, u32[]{:S(2)}) collective-permute-start(bf16[1,32,512]{2,1,0:T(8,128)(2,1)S(1)} %get-tuple-element.40), channel_id=1, source_target_pairs={{0,1},{1,0},{2,3},{3,2},{4,5},{5,4},{6,7},{7,6},{8,9},{9,8},{10,11... | collective-permute-start | bytes 98312 | tf_op jit(solution)/shard_map/ppermute | solution.py:426
  7.2 0.7 %copy-start.3 = (f32[64]{0:T(128)S(1)}, f32[64]{0:T(128)}, u32[]{:S(2)}) copy-start(f32[64]{0:T(128)} %param.9) | copy-start | bytes 772
  7.2 0.7 %copy-start.4 = (f32[128]{0:T(128)S(1)}, f32[128]{0:T(128)}, u32[]{:S(2)}) copy-start(f32[128]{0:T(128)} %param.11) | copy-start | bytes 1540
  7.9 1.0 %copy-start = (bf16[27,128,64]{1,2,0:T(8,128)(2,1)S(1)}, bf16[27,128,64]{1,2,0:T(8,128)(2,1)}, u32[]{:S(2)}) copy-start(bf16[27,128,64]{1,2,0:T(8,128)(2,1)} %param.10) | copy-start | bytes 1327108
  8.9 2.5 %copy-start.2 = (bf16[1,128,256]{2,1,0:T(8,128)(2,1)S(1)}, bf16[1,128,256]{2,1,0:T(8,128)(2,1)}, u32[]{:S(2)}) copy-start(bf16[1,128,256]{2,1,0:T(8,128)(2,1)} %refs_4_.1) | copy-start | bytes 196612
  14.6 1.5 %collective-permute-start.4 = (bf16[816,128]{1,0:T(8,128)(2,1)S(1)}, bf16[816,128]{1,0:T(8,128)(2,1)S(1)}, u32[]{:S(2)}, u32[]{:S(2)}) collective-permute-start(bf16[816,128]{1,0:T(8,128)(2,1)S(1)} %get-tuple-element.29), channel_id=1, source_target_pairs={{0,4},{4,0},{8,12},{12,8},{16,20},{20,16},{24,28},{28,24},{1,5},{5... | collective-permute-start | bytes 626696 | tf_op jit(solution)/shard_map/ppermute | solution.py:426
  14.7 4.5 %collective-permute-start.3 = (bf16[272,128]{1,0:T(8,128)(2,1)S(1)}, bf16[272,128]{1,0:T(8,128)(2,1)S(1)}, u32[]{:S(2)}, u32[]{:S(2)}) collective-permute-start(bf16[272,128]{1,0:T(8,128)(2,1)S(1)} %get-tuple-element.28), channel_id=1, source_target_pairs={{0,4},{4,0},{8,12},{12,8},{16,20},{20,16},{24,28},{28,24},{1,5},{5... | collective-permute-start | bytes 208904 | tf_op jit(solution)/shard_map/ppermute | solution.py:426
  16.2 3.8 %collective-permute-start.5 = (bf16[272,128]{1,0:T(8,128)(2,1)S(1)}, bf16[272,128]{1,0:T(8,128)(2,1)S(1)}, u32[]{:S(2)}, u32[]{:S(2)}) collective-permute-start(bf16[272,128]{1,0:T(8,128)(2,1)S(1)} %get-tuple-element.30), channel_id=1, source_target_pairs={{0,20},{1,21},{2,22},{3,23},{4,6},{5,7},{6,4},{7,5},{8,10},{9,11},... | collective-permute-start | bytes 208904 | tf_op jit(solution)/shard_map/ppermute | solution.py:441
  17.5 5.2 %collective-permute-start.6 = (bf16[272,128]{1,0:T(8,128)(2,1)S(1)}, bf16[272,128]{1,0:T(8,128)(2,1)S(1)}, u32[]{:S(2)}, u32[]{:S(2)}) collective-permute-start(bf16[272,128]{1,0:T(8,128)(2,1)S(1)} %get-tuple-element.31), channel_id=1, source_target_pairs={{0,24},{1,25},{2,26},{3,27},{4,7},{5,6},{6,5},{7,4},{8,11},{9,10},... | collective-permute-start | bytes 208904 | tf_op jit(solution)/shard_map/ppermute | solution.py:441
  19.0 3.8 %collective-permute-start.7 = (bf16[272,128]{1,0:T(8,128)(2,1)S(1)}, bf16[272,128]{1,0:T(8,128)(2,1)S(1)}, u32[]{:S(2)}, u32[]{:S(2)}) collective-permute-start(bf16[272,128]{1,0:T(8,128)(2,1)S(1)} %get-tuple-element.32), channel_id=1, source_target_pairs={{0,12},{1,13},{2,14},{3,15},{4,5},{5,4},{6,7},{7,6},{8,9},{9,8},{1... | collective-permute-start | bytes 208904 | tf_op jit(solution)/shard_map/ppermute | solution.py:441
  22.8 5.6 %collective-permute-start.10 = (bf16[272,128]{1,0:T(8,128)(2,1)S(1)}, bf16[272,128]{1,0:T(8,128)(2,1)S(1)}, u32[]{:S(2)}, u32[]{:S(2)}) collective-permute-start(bf16[272,128]{1,0:T(8,128)(2,1)S(1)} %group_sum.1.refs_0_), channel_id=1, source_target_pairs={{0,2},{1,3},{2,0},{3,1},{4,16},{5,17},{6,18},{7,19},{8,28},{9,29},... | collective-permute-start | bytes 208904 | tf_op jit(solution)/shard_map/ppermute | solution.py:441
  24.1 6.2 %collective-permute-start.9 = (bf16[272,128]{1,0:T(8,128)(2,1)S(1)}, bf16[272,128]{1,0:T(8,128)(2,1)S(1)}, u32[]{:S(2)}, u32[]{:S(2)}) collective-permute-start(bf16[272,128]{1,0:T(8,128)(2,1)S(1)} %group_sum.1.refs_0_), channel_id=1, source_target_pairs={{0,3},{1,2},{2,1},{3,0},{4,28},{5,29},{6,30},{7,31},{8,16},{9,17},... | collective-permute-start | bytes 208904 | tf_op jit(solution)/shard_map/ppermute | solution.py:441
  25.4 5.1 %collective-permute-start.8 = (bf16[272,128]{1,0:T(8,128)(2,1)S(1)}, bf16[272,128]{1,0:T(8,128)(2,1)S(1)}, u32[]{:S(2)}, u32[]{:S(2)}) collective-permute-start(bf16[272,128]{1,0:T(8,128)(2,1)S(1)} %group_sum.1.refs_0_), channel_id=1, source_target_pairs={{0,1},{1,0},{2,3},{3,2},{4,8},{5,9},{6,10},{7,11},{8,4},{9,5},{10,... | collective-permute-start | bytes 208904 | tf_op jit(solution)/shard_map/ppermute | solution.py:441
  30.5 3.8 %collective-permute-start.13 = (bf16[272,128]{1,0:T(8,128)(2,1)S(1)}, bf16[272,128]{1,0:T(8,128)(2,1)S(1)}, u32[]{:S(2)}, u32[]{:S(2)}) collective-permute-start(bf16[272,128]{1,0:T(8,128)(2,1)S(1)} %space_sum.1.refs_0_), channel_id=1, source_target_pairs={{0,20},{1,21},{2,22},{3,23},{4,6},{5,7},{6,4},{7,5},{8,10},{9,11},... | collective-permute-start | bytes 208904 | tf_op jit(solution)/shard_map/ppermute | solution.py:441
  30.6 5.3 %collective-permute-start.12 = (bf16[272,128]{1,0:T(8,128)(2,1)S(1)}, bf16[272,128]{1,0:T(8,128)(2,1)S(1)}, u32[]{:S(2)}, u32[]{:S(2)}) collective-permute-start(bf16[272,128]{1,0:T(8,128)(2,1)S(1)} %space_sum.1.refs_0_), channel_id=1, source_target_pairs={{0,24},{1,25},{2,26},{3,27},{4,7},{5,6},{6,5},{7,4},{8,11},{9,10},... | collective-permute-start | bytes 208904 | tf_op jit(solution)/shard_map/ppermute | solution.py:441
  32.3 4.3 %collective-permute-start.11 = (bf16[272,128]{1,0:T(8,128)(2,1)S(1)}, bf16[272,128]{1,0:T(8,128)(2,1)S(1)}, u32[]{:S(2)}, u32[]{:S(2)}) collective-permute-start(bf16[272,128]{1,0:T(8,128)(2,1)S(1)} %space_sum.1.refs_0_), channel_id=1, source_target_pairs={{0,12},{1,13},{2,14},{3,15},{4,5},{5,4},{6,7},{7,6},{8,9},{9,8},{1... | collective-permute-start | bytes 208904 | tf_op jit(solution)/shard_map/ppermute | solution.py:441
  33.5 3.1 %collective-permute-start.14 = (bf16[272,128]{1,0:T(8,128)(2,1)S(1)}, bf16[272,128]{1,0:T(8,128)(2,1)S(1)}, u32[]{:S(2)}, u32[]{:S(2)}) collective-permute-start(bf16[272,128]{1,0:T(8,128)(2,1)S(1)} %space_sum.1.refs_0_), channel_id=1, source_target_pairs={{0,4},{4,0},{8,12},{12,8},{16,20},{20,16},{24,28},{28,24},{1,5},{5... | collective-permute-start | bytes 208904 | tf_op jit(solution)/shard_map/ppermute | solution.py:426
  34.3 2.3 %collective-permute-start.15 = (bf16[272,128]{1,0:T(8,128)(2,1)S(1)}, bf16[272,128]{1,0:T(8,128)(2,1)S(1)}, u32[]{:S(2)}, u32[]{:S(2)}) collective-permute-start(bf16[272,128]{1,0:T(8,128)(2,1)S(1)} %collective-permute-done.13.refs_3_), channel_id=1, source_target_pairs={{0,4},{4,0},{8,12},{12,8},{16,20},{20,16},{24,28},{28,24},{1,5},{5... | collective-permute-start | bytes 208904 | tf_op jit(solution)/shard_map/ppermute | solution.py:426
  35.8 1.7 %collective-permute-start.16 = (bf16[272,128]{1,0:T(8,128)(2,1)S(1)}, bf16[272,128]{1,0:T(8,128)(2,1)S(1)}, u32[]{:S(2)}, u32[]{:S(2)}) collective-permute-start(bf16[272,128]{1,0:T(8,128)(2,1)S(1)} %collective-permute-done.12.refs_2_), channel_id=1, source_target_pairs={{0,4},{4,0},{8,12},{12,8},{16,20},{20,16},{24,28},{28,24},{1,5},{5... | collective-permute-start | bytes 208904 | tf_op jit(solution)/shard_map/ppermute | solution.py:426
  36.6 1.3 %collective-permute-start.17 = (bf16[272,128]{1,0:T(8,128)(2,1)S(1)}, bf16[272,128]{1,0:T(8,128)(2,1)S(1)}, u32[]{:S(2)}, u32[]{:S(2)}) collective-permute-start(bf16[272,128]{1,0:T(8,128)(2,1)S(1)} %collective-permute-done.11.refs_1_), channel_id=1, source_target_pairs={{0,4},{4,0},{8,12},{12,8},{16,20},{20,16},{24,28},{28,24},{1,5},{5... | collective-permute-start | bytes 208904 | tf_op jit(solution)/shard_map/ppermute | solution.py:426
